TPU v7x, 32 devices: a whole 2x2x4 slice. The times are simulated.
32 devices in a mesh: cand: 2 (over y), gx: 4 (over z), gy: 2 (over x), gz: 2 (over core).
Axes of the slice: x: 2, y: 2, z: 4, core: 2. Of those that a mesh axis runs over, the one named last changes fastest.
Arguments:
- tokens: bfloat16 [64, 64, 16, 128], P(('cand', 'gx'), 'gy', 'gz'), parts along dimension 0, may hold values from -6 to 6
- region: int32 [64, 64, 16], P(('cand', 'gx'), 'gy', 'gz'), parts along dimension 0, may hold values from 0 to 2
- rel_index: int32 [256, 256], replicated, may hold values from 0 to 1574
- bias_table: float32 [1575, 4], replicated, may hold values from -3 to 303
- gain_attn: float32 [128], replicated, may hold values from 0.25 to 1.75
- w_qkv: bfloat16 [128, 384], replicated, may hold values from -0.5 to 0.5
- w_proj: bfloat16 [128, 128], replicated, may hold values from -0.5 to 0.5
- gain_mlp: float32 [128], replicated, may hold values from 0.25 to 1.75
- w_up: bfloat16 [128, 512], replicated, may hold values from -0.5 to 0.5
- w_down: bfloat16 [512, 128], replicated, may hold values from -0.25 to 0.25
Outputs:
- result: bfloat16 [64, 64, 16, 128], P(('cand', 'gx'), 'gy', 'gz'), parts along dimension 0
There are 2 independent parts, one for each index of `cand`. A program takes and returns all parts, laid end to end along the dimension named above; an argument that names none is the same for every part. Nothing has to cross between parts.
All inputs are finite; a program needn't handle non-finite values.
Results may differ from a plain program's by a relative error of at most 0.0065.
Values may be sent and summed in bfloat16 or wider, within the bound.
No kernel may reach another device: no remote copies, remote signals or barrier semaphores. Data moves between devices by JAX's collectives and lax.ppermute only.
A program may use at most 128 MiB of HBM per device.

v0:
```python
import math

import jax
import jax.numpy as jnp
from jax import lax
from jax.sharding import PartitionSpec as P

HEADS = 4
WX = 8
WY = 8
WZ = 4
SX = 4
SY = 4
SZ = 2


def shifted_2(value, axis, steps):
    count = lax.axis_size(axis)
    pairs = [(source, (source + steps) % count) for source in range(count)]
    return lax.ppermute(value, axis, pairs)


def layer_norm(values, norm_gain):
    center = values - jnp.mean(values, axis=-1, keepdims=True)
    spread = jnp.mean(center * center, axis=-1, keepdims=True)
    return center * lax.rsqrt(spread + 1e-05) * norm_gain


def to_windows(volume):
    size_x, size_y, size_z, width = volume.shape
    parted = volume.reshape(size_x // WX, WX, size_y // WY, WY, size_z // WZ, WZ, width)
    return parted.transpose(0, 2, 4, 1, 3, 5, 6).reshape(-1, WX * WY * WZ, width)


def from_windows(windows, size_x, size_y, size_z):
    width = windows.shape[-1]
    parted = windows.reshape(size_x // WX, size_y // WY, size_z // WZ, WX, WY, WZ, width)
    return parted.transpose(0, 3, 1, 4, 2, 5, 6).reshape(size_x, size_y, size_z, width)


def roll_along_x(volume, sign):
    piece = volume[:SX] if sign < 0 else volume[-SX:]
    arrived = shifted_2(piece, "gx", sign)
    if sign < 0:
        return jnp.concatenate([volume[SX:], arrived], axis=0)
    return jnp.concatenate([arrived, volume[:-SX]], axis=0)


def roll_along_y(volume, sign):
    piece = volume[:, :SY] if sign < 0 else volume[:, -SY:]
    arrived = shifted_2(piece, "gy", sign)
    if sign < 0:
        return jnp.concatenate([volume[:, SY:], arrived], axis=1)
    return jnp.concatenate([arrived, volume[:, :-SY]], axis=1)


def roll_along_z(volume, sign):
    piece = volume[:, :, :SZ] if sign < 0 else volume[:, :, -SZ:]
    arrived = shifted_2(piece, "gz", sign)
    if sign < 0:
        return jnp.concatenate([volume[:, :, SZ:], arrived], axis=2)
    return jnp.concatenate([arrived, volume[:, :, :-SZ]], axis=2)


def undo_roll(volume):
    return roll_along_z(roll_along_y(roll_along_x(volume, 1), 1), 1)


def attend(windows, labels, gain_attn, w_qkv, w_proj, bias_all):
    batch, length, width = windows.shape
    head_size = width // HEADS
    normed = layer_norm(windows.astype(jnp.float32), gain_attn).astype(jnp.bfloat16)
    qkv = jnp.dot(normed.reshape(batch * length, width), w_qkv, preferred_element_type=jnp.float32)
    qkv = qkv.astype(jnp.bfloat16).reshape(batch, length, 3, HEADS, head_size)
    query = qkv[:, :, 0]
    keys = qkv[:, :, 1]
    values = qkv[:, :, 2]
    scores = jnp.einsum("bihe,bjhe->bhij", query, keys, preferred_element_type=jnp.float32)
    scores = scores * head_size ** (-0.5) + bias_all[None]
    same = labels[:, :, None] == labels[:, None, :]
    scores = jnp.where(same[:, None], scores, -1000000000.0)
    peak_score = jnp.max(scores, axis=-1, keepdims=True)
    weights = jnp.exp(scores - peak_score)
    probs = (weights / jnp.sum(weights, axis=-1, keepdims=True)).astype(jnp.bfloat16)
    attended = jnp.einsum("bhij,bjhe->bihe", probs, values, preferred_element_type=jnp.float32)
    attended = attended.astype(jnp.bfloat16).reshape(batch * length, width)
    projected = jnp.dot(attended, w_proj, preferred_element_type=jnp.float32)
    flat = windows.reshape(batch * length, width).astype(jnp.float32)
    return (flat + projected).astype(jnp.bfloat16)


def feed_forward(middle, gain_mlp, w_up, w_down):
    normed = layer_norm(middle.astype(jnp.float32), gain_mlp).astype(jnp.bfloat16)
    hidden = jax.nn.gelu(
        jnp.dot(normed, w_up, preferred_element_type=jnp.float32), approximate=False
    )
    hidden = hidden.astype(jnp.bfloat16)
    return (
        middle.astype(jnp.float32) + jnp.dot(hidden, w_down, preferred_element_type=jnp.float32)
    ).astype(jnp.bfloat16)


def per_device(
    tokens, region, rel_index, bias_table, gain_attn, w_qkv, w_proj, gain_mlp, w_up, w_down
):
    size_x, size_y, size_z, width = tokens.shape
    shifted = roll_along_z(roll_along_y(roll_along_x(tokens, -1), -1), -1)
    windows = to_windows(shifted)
    labels = to_windows(region[..., None])[..., 0]
    bias_all = jnp.transpose(jnp.take(bias_table, rel_index, axis=0), (2, 0, 1))
    number = windows.shape[0]
    length = windows.shape[1]
    bundle = math.gcd(number, 8)
    grouped = windows.reshape(number // bundle, bundle, length, width)
    grouped_labels = labels.reshape(number // bundle, bundle, length)

    def one_bundle(pieces):
        return attend(pieces[0], pieces[1], gain_attn, w_qkv, w_proj, bias_all)

    middle = lax.map(one_bundle, (grouped, grouped_labels)).reshape(number * length, width)
    middle_field = from_windows(middle.reshape(number, length, width), size_x, size_y, size_z)
    middle_field = undo_roll(middle_field)
    after = feed_forward(middle_field.reshape(-1, width), gain_mlp, w_up, w_down)
    return after.reshape(size_x, size_y, size_z, width)


def solution(mesh):
    placed = (
        P(("cand", "gx"), "gy", "gz", None),
        P(("cand", "gx"), "gy", "gz"),
        P(),
        P(),
        P(),
        P(),
        P(),
        P(),
        P(),
        P(),
    )
    return jax.shard_map(
        per_device,
        mesh=mesh,
        in_specs=placed,
        out_specs=P(("cand", "gx"), "gy", "gz", None),
        check_vma=False,
    )
```

profile of v0, /device:TPU:0, one launch (start us, length us, event | category | flops | bytes accessed | tf_op | source)
XLA Modules:
  0.0 304.7 jit_solution(15365770654343845621)
XLA Ops:
  0.0 1.1 fusion.74
  1.1 5.1 %collective-permute-start = (bf16[4,32,8,128]{3,2,1,0:T(8,128)(2,1)S(1)}, bf16[4,32,8,128]{3,2,1,0:T(8,128)(2,1)S(1)}, u32[]{:S(2)}, u32[]{:S(2)}) collective-permute-start(bf16[4,32,8,128]{3,2,1,0:T(8,128)(2,1)S(1)} %get-tuple-element.34), channel_id=1, source_target_pairs={{0,12},{4,0},{8,4},{12,8},{1,13},{5,1},{9,5},{13,9},{2,14},{6,2},{... | collective-permute-start | bytes 786440 | tf_op jit(solution)/shard_map/ppermute | solution.py:20
  6.2 1.0 fusion.38
  7.2 1.0 compare_and_fusion
  8.2 1.0 copy.40
  9.3 0.1 copy.53
  9.5 217.1 %gather_fusion = f32[65536,4]{1,0:T(8,128)} fusion(f32[1575,4]{1,0:T(8,128)S(1)} %copy.40, s32[65536]{0:T(1024)S(1)} %broadcast_clamp_fusion), kind=kCustom, calls=%fused_computation | custom fusion | bytes 2359296 | tf_op jit(solution)/shard_map/jit(_take)/gather | solution.py:110
  226.5 19.0 %copy.41 = f32[256,256,4]{0,1,2:T(8,128)S(1)} copy(f32[256,256,4]{2,1,0:T(8,128)} %bitcast.87) | data formatting | bytes 2097152 | tf_op jit(solution)/shard_map/jit(_take)/gather | solution.py:110
  245.6 0.2 copy.39
  245.7 0.1 reshape_broadcast_in_dim.3
  245.9 0.4 copy.36
  246.3 0.2 eq.26
  246.5 1.1 select_bitcast_fusion
  247.6 1.6 collective-permute-start.1
  249.2 2.7 collective-permute-done.1
  252.1 0.5 broadcast_compare_fusion
  252.5 0.1 slice_maximum_fusion
  252.7 0.7 collective-permute-done.2
  253.4 0.2 maximum_convert_fusion
  253.6 0.3 copy.33
  253.9 0.6 bitcast_reduce_fusion
  254.6 1.3 fusion.28
  255.9 0.2 div.31
  256.1 0.2 rsqrt.24
  256.3 1.1 convolution_convert_fusion
  257.4 1.7 copy.34
  259.1 2.0 copy.52
  261.1 1.1 fusion.72
  262.2 7.8 %fusion.75 = (f32[8,4,256]{2,1,0:T(4,128)S(1)}, f32[8,4,256,256]{2,3,1,0:T(8,128)}) fusion(f32[4,256,256]{1,2,0:T(8,128)S(1)} %copy-done.1, pred[8,256,256]{1,2,0:T(8,128)(4,1)S(1)} %broadcast_compare_fusion, bf16[8,256,1,4,32]{1,0,4,3,2:T(8,128)(2,1)} %get-tuple-element.20, bf16[8,256,1,4,32]{1,0,4,3,2:T(8,128)(2,1)} %get-tuple-element.21), kind=kOutput, calls=%fused_computation.116 | convolution fusion | flops 144703744 | bytes 11042816 | tf_op jit(solution)/shard_map/while/body/eval_jaxpr/sub | solution.py:83
  270.0 4.1 %fusion.23 = bf16[8,256,4,32]{1,3,2,0:T(8,128)(2,1)S(1)} fusion(f32[8,4,256,256]{2,3,1,0:T(8,128)} %get-tuple-element.37, f32[8,4,256]{2,1,0:T(4,128)S(1)} %get-tuple-element.36, bf16[8,256,1,4,32]{1,0,4,3,2:T(8,128)(2,1)S(1)} %get-tuple-element.19), kind=kOutput, calls=%fused_computation.37 | convolution fusion | flops 138674176 | bytes 9469952 | tf_op jit(solution)/shard_map/while/body/eval_jaxpr/bhij,bjhe->bihe/dot_general | solution.py:85
  274.1 0.3 copy.43
  274.4 0.1 copy.54
  274.5 0.3 fusion.17
  274.9 0.1 copy.80
  275.0 0.2 collective-permute-start.3
  275.3 10.1 %collective-permute-done.3 = bf16[4,32,8,128]{3,1,2,0:T(8,128)(2,1)S(1)} collective-permute-done((bf16[4,32,8,128]{3,1,2,0:T(8,128)(2,1)S(1)}, bf16[4,32,8,128]{3,1,2,0:T(8,128)(2,1)S(1)}, u32[]{:S(2)}, u32[]{:S(2)}) %collective-permute-start.3) | collective-permute-done | bytes 262176 | tf_op jit(solution)/shard_map/ppermute | solution.py:20
  285.5 1.6 collective-permute-start.4
  287.0 2.8 collective-permute-done.4
  289.9 1.3 collective-permute-done.5
  291.3 0.2 fusion.32
  291.4 0.6 copy.45
  292.0 0.3 fusion.71
  292.4 0.1 copy.46
  292.5 0.7 multiply_reduce_fusion
  293.3 0.1 rsqrt.26
  293.4 0.1 div.36
  293.5 0.6 fusion.26
  294.2 10.5 %fusion.18 = bf16[2048,128]{1,0:T(8,128)(2,1)} fusion(f32[2048,128]{1,0:T(8,128)S(1)} %bitcast.100, bf16[512,128]{1,0:T(8,128)(2,1)S(1)} %copy-done, bf16[2048,128]{1,0:T(8,128)(2,1)S(1)} %fusion.26, bf16[128,512]{1,0:T(8,128)(2,1)S(1)} %copy-done.7), kind=kOutput, calls=%fused_computation.34 | convolution fusion | flops 605552640 | bytes 2359296 | tf_op jit(solution)/shard_map/dot_general | solution.py:99
  (31 shorter events, 0.6 us)
Async XLA Ops:
  0.0 294.1 %copy-start = (bf16[512,128]{1,0:T(8,128)(2,1)S(1)}, bf16[512,128]{1,0:T(8,128)(2,1)}, u32[]{:S(2)}) copy-start(bf16[512,128]{1,0:T(8,128)(2,1)} %param.19) | copy-start | bytes 393220
  1.1 246.5 %collective-permute-start = (bf16[4,32,8,128]{3,2,1,0:T(8,128)(2,1)S(1)}, bf16[4,32,8,128]{3,2,1,0:T(8,128)(2,1)S(1)}, u32[]{:S(2)}, u32[]{:S(2)}) collective-permute-start(bf16[4,32,8,128]{3,2,1,0:T(8,128)(2,1)S(1)} %get-tuple-element.34), channel_id=1, source_target_pairs={{0,12},{4,0},{8,4},{12,8},{1,13},{5,1},{9,5},{13,9},{2,14},{6,2},{... | collective-permute-start | bytes 786440 | tf_op jit(solution)/shard_map/ppermute | solution.py:20
  226.5 19.2 %copy-start.4 = (s32[8,32,8]{1,2,0:T(8,128)S(1)}, s32[8,32,8]{1,2,0:T(8,128)}, u32[]{:S(2)}) copy-start(s32[8,32,8]{1,2,0:T(8,128)} %param.11) | copy-start | bytes 24580
  247.6 4.3 %collective-permute-start.1 = (bf16[8,4,8,128]{3,2,1,0:T(8,128)(2,1)S(1)}, bf16[8,4,8,128]{3,2,1,0:T(8,128)(2,1)S(1)}, u32[]{:S(2)}, u32[]{:S(2)}) collective-permute-start(bf16[8,4,8,128]{3,2,1,0:T(8,128)(2,1)S(1)} %pad_maximum_fusion.5), channel_id=1, source_target_pairs={{0,2},{2,0},{1,3},{3,1},{4,6},{6,4},{5,7},{7,5},{8,10},{10,8},{9,1... | collective-permute-start | bytes 196616 | tf_op jit(solution)/shard_map/ppermute | solution.py:20
  252.0 1.4 collective-permute-start.2
  252.7 3.6 %copy-start.2 = (bf16[128,384]{1,0:T(8,128)(2,1)S(1)}, bf16[128,384]{1,0:T(8,128)(2,1)}, u32[]{:S(2)}) copy-start(bf16[128,384]{1,0:T(8,128)(2,1)} %param.15) | copy-start | bytes 294916
  252.7 3.6 %copy-start.5 = (f32[128]{0:T(128)S(1)}, f32[128]{0:T(128)}, u32[]{:S(2)}) copy-start(f32[128]{0:T(128)} %param.14) | copy-start | bytes 1540
  259.1 3.1 %copy-start.1 = (f32[4,256,256]{1,2,0:T(8,128)S(1)}, f32[4,256,256]{1,2,0:T(8,128)}, u32[]{:S(2)}) copy-start(f32[4,256,256]{1,2,0:T(8,128)} %select_bitcast_fusion) | copy-start | bytes 3145732
  270.0 4.5 %copy-start.3 = (bf16[128,128]{1,0:T(8,128)(2,1)S(1)}, bf16[128,128]{1,0:T(8,128)(2,1)}, u32[]{:S(2)}) copy-start(bf16[128,128]{1,0:T(8,128)(2,1)} %param.16) | copy-start | bytes 98308
  275.0 18.6 %copy-start.6 = (f32[128]{0:T(128)S(1)}, f32[128]{0:T(128)}, u32[]{:S(2)}) copy-start(f32[128]{0:T(128)} %param.17) | copy-start | bytes 1540
  275.0 10.4 %collective-permute-start.3 = (bf16[4,32,8,128]{3,1,2,0:T(8,128)(2,1)S(1)}, bf16[4,32,8,128]{3,1,2,0:T(8,128)(2,1)S(1)}, u32[]{:S(2)}, u32[]{:S(2)}) collective-permute-start(bf16[4,32,8,128]{3,1,2,0:T(8,128)(2,1)S(1)} %bitcast.107), channel_id=1, source_target_pairs={{0,4},{4,8},{8,12},{12,0},{1,5},{5,9},{9,13},{13,1},{2,6},{6,10},{... | collective-permute-start | bytes 786440 | tf_op jit(solution)/shard_map/ppermute | solution.py:20
  285.5 8.7 %copy-start.7 = (bf16[128,512]{1,0:T(8,128)(2,1)S(1)}, bf16[128,512]{1,0:T(8,128)(2,1)}, u32[]{:S(2)}) copy-start(bf16[128,512]{1,0:T(8,128)(2,1)} %param.18) | copy-start | bytes 393220
  285.5 4.3 %collective-permute-start.4 = (bf16[8,4,8,128]{3,1,2,0:T(4,128)(2,1)S(1)}, bf16[8,4,8,128]{3,1,2,0:T(4,128)(2,1)S(1)}, u32[]{:S(2)}, u32[]{:S(2)}) collective-permute-start(bf16[8,4,8,128]{3,1,2,0:T(4,128)(2,1)S(1)} %pad_maximum_fusion.4), channel_id=1, source_target_pairs={{0,2},{2,0},{1,3},{3,1},{4,6},{6,4},{5,7},{7,5},{8,10},{10,8},{9,1... | collective-permute-start | bytes 196616 | tf_op jit(solution)/shard_map/ppermute | solution.py:20
  289.9 1.4 collective-permute-start.5
where the time goes:
time: 305 us
  local copies, waits for them, and re-layouts  246 us (81%)
  matrix products  23.8 us (8%)
  waiting for transfers between devices  17.7 us (6%)
  starting transfers between devices  8.59 us (3%)
  other arithmetic  8 us (3%)
    gather x2, local copies, waits for them, and re-layouts, per_device(): bias_all = jnp.transpose(jnp.take(bias_table, rel_index, axis=0), (2, 0, 1))  236 us
    ppermute x6, waiting for transfers between devices, shifted_2(): return lax.ppermute(value, axis, pairs)  17.7 us
    dot_general x1, matrix products, feed_forward(): jnp.dot(hidden, w_down, preferred_element_type=jnp.float32)  10.5 us
    ppermute x6, starting transfers between devices, shifted_2(): return lax.ppermute(value, axis, pairs)  8.59 us
    sub x1, matrix products, attend(): weights = jnp.exp(scores - peak_score)  7.78 us
  transfers between devices with their start and end apart: 6, of which 5 were waited for; matrix products, arithmetic and copies ran while one was open for 79% of the time, Pallas kernels for 0%

commit v1 on v0

v1 whole, which is shorter than its diff:
```python
import functools

import jax
import jax.numpy as jnp
from jax import lax
from jax.experimental import pallas as pl
from jax.experimental.pallas import tpu as pltpu
from jax.sharding import PartitionSpec as P

HEADS = 4
WX = 8
WY = 8
WZ = 4
SX = 4
SY = 4
SZ = 2
WTOK = WX * WY * WZ
LANES = 128
F32 = jnp.float32
BF16 = jnp.bfloat16
LOG2E = 1.4426950408889634


def shifted_2(value, axis, steps):
    count = lax.axis_size(axis)
    pairs = [(source, (source + steps) % count) for source in range(count)]
    return lax.ppermute(value, axis, pairs)


def to_windows(volume):
    size_x, size_y, size_z, width = volume.shape
    parted = volume.reshape(size_x // WX, WX, size_y // WY, WY, size_z // WZ, WZ, width)
    return parted.transpose(0, 2, 4, 1, 3, 5, 6).reshape(-1, WX * WY * WZ, width)


def from_windows(windows, size_x, size_y, size_z):
    width = windows.shape[-1]
    parted = windows.reshape(size_x // WX, size_y // WY, size_z // WZ, WX, WY, WZ, width)
    return parted.transpose(0, 3, 1, 4, 2, 5, 6).reshape(size_x, size_y, size_z, width)


def roll_along(volume, axis, name, steps, sign):
    size = volume.shape[axis]
    if sign < 0:
        piece = lax.slice_in_dim(volume, 0, steps, axis=axis)
        rest = lax.slice_in_dim(volume, steps, size, axis=axis)
        return jnp.concatenate([rest, shifted_2(piece, name, -1)], axis=axis)
    piece = lax.slice_in_dim(volume, size - steps, size, axis=axis)
    rest = lax.slice_in_dim(volume, 0, size - steps, axis=axis)
    return jnp.concatenate([shifted_2(piece, name, 1), rest], axis=axis)


def bias_kernel(index_ref, table_ref, bias_ref):
    chunks = table_ref.shape[1]
    index = index_ref[...].astype(F32).T.astype(jnp.int32)
    for column in range(0, WTOK, LANES):
        for row in range(0, WTOK, 8):
            part = index[row : row + 8, column : column + LANES]
            low = part & (LANES - 1)
            high = part >> 7
            found = [jnp.zeros((8, LANES), F32) for _ in range(HEADS)]
            for chunk in range(chunks):
                here = high == chunk
                for head in range(HEADS):
                    line = jnp.broadcast_to(table_ref[head, chunk : chunk + 1, :], (8, LANES))
                    got = jnp.take_along_axis(line, low, axis=1, mode="promise_in_bounds")
                    found[head] = jnp.where(here, got, found[head])
            for head in range(HEADS):
                bias_ref[head, row : row + 8, column : column + LANES] = found[head] * LOG2E


def gather_bias(rel_index, bias_table):
    rows = bias_table.shape[0]
    chunks = -(-rows // LANES)
    table = jnp.pad(bias_table.T, ((0, 0), (0, chunks * LANES - rows))).reshape(HEADS, chunks, LANES)
    return pl.pallas_call(
        bias_kernel,
        out_shape=jax.ShapeDtypeStruct((HEADS, WTOK, WTOK), F32),
        compiler_params=pltpu.CompilerParams(vmem_limit_bytes=32 << 20),
        name="gather_bias",
    )(rel_index, table)


def dot_nn(left, right):
    return lax.dot_general(left, right, (((1,), (0,)), ((), ())), preferred_element_type=F32)


def dot_nt(left, right):
    return lax.dot_general(left, right, (((1,), (1,)), ((), ())), preferred_element_type=F32)


def eye(size):
    rows = lax.broadcasted_iota(jnp.int32, (size, size), 0)
    columns = lax.broadcasted_iota(jnp.int32, (size, size), 1)
    return (rows == columns).astype(BF16)


def gelu(value):
    return 0.5 * value * (1.0 + lax.erf(value * (0.5**0.5)))


def block_kernel(
    x_ref, label_ref, bias_ref, gain_attn_ref, w_qkv_ref, w_v_t_ref, w_q_t_ref, w_proj_t_ref,
    gain_mlp_ref, w_up_t_ref, w_down_t_ref, out_ref,
):
    count = x_ref.shape[0]
    width = x_ref.shape[2]
    size = width // HEADS
    scale = size**-0.5 * LOG2E
    eye_width = eye(width)
    eye_window = eye(WTOK)
    for at in range(count):
        x16 = x_ref[at]
        x = x16.astype(F32)
        center = x - jnp.mean(x, axis=1, keepdims=True)
        spread = jnp.mean(center * center, axis=1, keepdims=True)
        normed = (center * lax.rsqrt(spread + 1e-05) * gain_attn_ref[...]).astype(BF16)
        x_t = dot_nt(eye_width, x16)
        q_t = dot_nt(w_q_t_ref[...], normed).astype(BF16)
        v_t = dot_nt(w_v_t_ref[...], normed).astype(BF16)
        k = dot_nn(normed, w_qkv_ref[:, width : 2 * width]).astype(BF16)
        row = label_ref[at]
        column = dot_nt(eye_window, jnp.broadcast_to(row.astype(BF16), (WTOK, WTOK)))
        same = column == row
        parts = []
        for head in range(HEADS):
            span = slice(head * size, (head + 1) * size)
            scores = dot_nn(k[:, span], q_t[span]) * scale + bias_ref[head]
            scores = jnp.where(same, scores, -1e9 * LOG2E)
            weights = jnp.exp2(scores - jnp.max(scores, axis=0, keepdims=True))
            total = jnp.sum(weights, axis=0, keepdims=True)
            part = dot_nn(v_t[span], weights.astype(BF16))
            parts.append((part * (1.0 / total)).astype(BF16))
        attended = jnp.concatenate(parts, axis=0)
        middle = (x_t + dot_nn(w_proj_t_ref[...], attended)).astype(BF16).astype(F32)
        center = middle - jnp.mean(middle, axis=0, keepdims=True)
        spread = jnp.mean(center * center, axis=0, keepdims=True)
        normed = (center * lax.rsqrt(spread + 1e-05) * gain_mlp_ref[...]).astype(BF16)
        hidden = gelu(dot_nn(w_up_t_ref[...], normed)).astype(BF16)
        after = (middle + dot_nn(w_down_t_ref[...], hidden)).astype(BF16)
        out_ref[at] = dot_nt(eye_window, after).astype(BF16)


def window_block(windows, labels, bias, gain_attn, w_qkv, w_proj, gain_mlp, w_up, w_down):
    number, length, width = windows.shape
    step = 2
    whole = lambda a: pl.BlockSpec(a.shape, lambda i: (0,) * a.ndim)
    fixed = (
        bias,
        gain_attn[None],
        w_qkv,
        w_qkv[:, 2 * width :].T,
        w_qkv[:, :width].T,
        w_proj.T,
        gain_mlp[:, None],
        w_up.T,
        w_down.T,
    )
    return pl.pallas_call(
        block_kernel,
        grid=(number // step,),
        in_specs=[
            pl.BlockSpec((step, length, width), lambda i: (i, 0, 0)),
            pl.BlockSpec((step, 1, length), lambda i: (i, 0, 0)),
        ]
        + [whole(a) for a in fixed],
        out_specs=pl.BlockSpec((step, length, width), lambda i: (i, 0, 0)),
        out_shape=jax.ShapeDtypeStruct((number, length, width), BF16),
        compiler_params=pltpu.CompilerParams(vmem_limit_bytes=48 << 20),
        name="window_block",
    )(windows, labels, *fixed)


def per_device(
    tokens, region, rel_index, bias_table, gain_attn, w_qkv, w_proj, gain_mlp, w_up, w_down
):
    size_x, size_y, size_z, width = tokens.shape
    shifted = roll_along(tokens, 0, "gx", SX, -1)
    shifted = roll_along(shifted, 1, "gy", SY, -1)
    shifted = roll_along(shifted, 2, "gz", SZ, -1)
    bias = gather_bias(rel_index, bias_table)
    windows = to_windows(shifted)
    labels = to_windows(region[..., None])[..., 0].astype(F32)[:, None, :]
    after = window_block(
        windows, labels, bias, gain_attn, w_qkv, w_proj, gain_mlp, w_up, w_down
    )
    field = from_windows(after, size_x, size_y, size_z)
    field = roll_along(field, 2, "gz", SZ, 1)
    field = roll_along(field, 1, "gy", SY, 1)
    return roll_along(field, 0, "gx", SX, 1)


def solution(mesh):
    field = P(("cand", "gx"), "gy", "gz", None)
    placed = (field, P(("cand", "gx"), "gy", "gz")) + (P(),) * 8
    return jax.shard_map(
        per_device, mesh=mesh, in_specs=placed, out_specs=field, check_vma=False
    )
```

time: 305 us -> 62.1 us (0.20)
  local copies, waits for them, and re-layouts: 246 us -> 8.04 us
  matrix products: 23.8 us -> 0 us
  Pallas kernels: 0 us -> 21.2 us
  other arithmetic: 8 us -> 1.67 us
  waiting for transfers between devices: 17.7 us -> 21.7 us
    gather x2 -> x0, local copies, waits for them, and re-layouts: 236 us -> none  [per_device(): bias_all = jnp.transpose(jnp.take(bias_table, rel_index, axis=0), (2, 0, 1))]
    pallas_call x0 -> x2, Pallas kernels: none -> 21.2 us  [the longest x1 17.3 us: window_block(): pl.pallas_call(block_kernel, grid=(number // step,), in_specs=[pl.BlockSp...]
    dot_general x4 -> x0, matrix products: 16 us -> none  [the longest x1 10.5 us: feed_forward(): jnp.dot(hidden, w_down, preferred_element_type=jnp.float32)]
    sub x1 -> x0, matrix products: 7.78 us -> none  [attend(): weights = jnp.exp(scores - peak_score)]
    ppermute x6, waiting for transfers between devices: 17.7 us -> 21.7 us  [shifted_2(): return lax.ppermute(value, axis, pairs)]
  transfers between devices with their start and end apart: 6 -> 6, of which waited for: 5 -> 5; matrix products, arithmetic and copies ran while one was open for 79% -> 3% of each run, Pallas kernels for 0% -> 6%
where the time goes in v1:
time: 62.1 us; the launch traced here: 61.7 us
  waiting for transfers between devices  21.7 us (35%)
  Pallas kernels  21.2 us (34%)
  starting transfers between devices  8.87 us (14%)
  local copies, waits for them, and re-layouts  8.04 us (13%)
  other arithmetic  1.67 us (3%)
    ppermute x6, waiting for transfers between devices, shifted_2(): return lax.ppermute(value, axis, pairs)  21.7 us
    pallas_call x1, Pallas kernels, window_block(): pl.pallas_call(block_kernel, grid=(number // step,), in_specs=[pl.BlockSp...  17.3 us
    ppermute x6, starting transfers between devices, shifted_2(): return lax.ppermute(value, axis, pairs)  8.87 us
    unnamed x23, local copies, waits for them, and re-layouts  5.44 us
    pallas_call x1, Pallas kernels, gather_bias(): pl.pallas_call(bias_kernel, out_shape=jax.ShapeDtypeStruct((HEADS, WTOK,...  3.85 us
  transfers between devices with their start and end apart: 6, of which 5 were waited for; matrix products, arithmetic and copies ran while one was open for 3% of the time, Pallas kernels for 6%

profile of v1, /device:TPU:0, one launch (start us, length us, event | category | flops | bytes accessed | tf_op | source)
XLA Modules:
  0.0 61.7 jit_solution(7013730311216031371)
XLA Ops:
  0.0 1.1 %fusion.3 = (bf16[4,32,8,128]{3,2,1,0:T(8,128)(2,1)S(1)}, bf16[4,32,8,128]{3,2,1,0:T(8,128)(2,1)S(1)}) fusion(bf16[8,32,8,128]{3,2,1,0:T(8,128)(2,1)} %param.10), kind=kLoop, calls=%fused_computation.12 | loop fusion | bytes 1048576 | tf_op jit(solution)/shard_map/slice | solution.py:46
  1.1 5.1 %collective-permute-start = (bf16[4,32,8,128]{3,2,1,0:T(8,128)(2,1)S(1)}, bf16[4,32,8,128]{3,2,1,0:T(8,128)(2,1)S(1)}, u32[]{:S(2)}, u32[]{:S(2)}) collective-permute-start(bf16[4,32,8,128]{3,2,1,0:T(8,128)(2,1)S(1)} %get-tuple-element.8), channel_id=1, source_target_pairs={{0,12},{4,0},{8,4},{12,8},{1,13},{5,1},{9,5},{13,9},{2,14},{6,2},{... | collective-permute-start | bytes 786440 | tf_op jit(solution)/shard_map/ppermute | solution.py:27
  6.2 5.6 %collective-permute-done = bf16[4,32,8,128]{3,2,1,0:T(8,128)(2,1)S(1)} collective-permute-done((bf16[4,32,8,128]{3,2,1,0:T(8,128)(2,1)S(1)}, bf16[4,32,8,128]{3,2,1,0:T(8,128)(2,1)S(1)}, u32[]{:S(2)}, u32[]{:S(2)}) %collective-permute-start) | collective-permute-done | bytes 262176 | tf_op jit(solution)/shard_map/ppermute | solution.py:27
  11.7 1.6 %collective-permute-start.1 = (bf16[8,4,8,128]{3,2,1,0:T(8,128)(2,1)S(1)}, bf16[8,4,8,128]{3,2,1,0:T(8,128)(2,1)S(1)}, u32[]{:S(2)}, u32[]{:S(2)}) collective-permute-start(bf16[8,4,8,128]{3,2,1,0:T(8,128)(2,1)S(1)} %pad_maximum_fusion.5), channel_id=1, source_target_pairs={{0,2},{2,0},{1,3},{3,1},{4,6},{6,4},{5,7},{7,5},{8,10},{10,8},{9,1... | collective-permute-start | bytes 196616 | tf_op jit(solution)/shard_map/ppermute | solution.py:27
  13.3 0.0 copy-start
  13.4 2.7 %collective-permute-done.1 = bf16[8,4,8,128]{3,2,1,0:T(8,128)(2,1)S(1)} collective-permute-done((bf16[8,4,8,128]{3,2,1,0:T(8,128)(2,1)S(1)}, bf16[8,4,8,128]{3,2,1,0:T(8,128)(2,1)S(1)}, u32[]{:S(2)}, u32[]{:S(2)}) %collective-permute-start.1) | collective-permute-done | bytes 65568 | tf_op jit(solution)/shard_map/ppermute | solution.py:27
  16.1 0.1 pad_maximum_fusion.3
  16.1 0.0 copy-start.7
  16.2 0.1 collective-permute-start.2
  16.2 0.0 copy-done
  16.3 0.6 %copy-done.7 = f32[1575,4]{0,1:T(4,128)S(1)} copy-done((f32[1575,4]{0,1:T(4,128)S(1)}, f32[1575,4]{0,1:T(4,128)}, u32[]{:S(2)}) %copy-start.7) | copy-done | bytes 25224
  16.9 0.0 copy-start.5
  16.9 0.7 %copy-done.5 = s32[8,32,8]{1,2,0:T(8,128)S(1)} copy-done((s32[8,32,8]{1,2,0:T(8,128)S(1)}, s32[8,32,8]{1,2,0:T(8,128)}, u32[]{:S(2)}) %copy-start.5) | copy-done | bytes 8216
  17.7 0.0 copy-start.6
  17.7 0.8 %copy-done.6 = bf16[128,128]{1,0:T(8,128)(2,1)S(1)} copy-done((bf16[128,128]{1,0:T(8,128)(2,1)S(1)}, bf16[128,128]{1,0:T(8,128)(2,1)}, u32[]{:S(2)}) %copy-start.6) | copy-done | bytes 32792
  18.4 0.1 copy.24
  18.5 0.0 copy-start.8
  18.5 0.7 %copy-done.8 = f32[128]{0:T(128)S(1)} copy-done((f32[128]{0:T(128)S(1)}, f32[128]{0:T(128)}, u32[]{:S(2)}) %copy-start.8) | copy-done | bytes 536
  19.2 0.1 copy.28.gain_mlp_ref
  19.3 0.1 copy.31
  19.4 0.1 copy.30
  19.6 0.1 convert_element_type.22
  19.7 0.4 copy.21
  20.1 0.0 copy-start.3
  20.1 0.2 convert_element_type.25.label_ref
  20.3 0.7 %copy-done.3 = bf16[128,512]{1,0:T(8,128)(2,1)S(1)} copy-done((bf16[128,512]{1,0:T(8,128)(2,1)S(1)}, bf16[128,512]{1,0:T(8,128)(2,1)}, u32[]{:S(2)}) %copy-start.3) | copy-done | bytes 131096
  21.0 0.1 copy.25
  21.2 0.0 copy-done.4
  21.2 0.1 copy.26
  21.3 0.7 %copy-done.1 = s32[256,256]{1,0:T(8,128)S(1)} copy-done((s32[256,256]{1,0:T(8,128)S(1)}, s32[256,256]{1,0:T(8,128)}, u32[]{:S(2)}) %copy-start.1) | copy-done | bytes 262168
  22.0 3.9 %gather_bias.1.bias_ref = f32[4,256,256]{2,1,0:T(8,128)S(1)} custom-call(s32[256,256]{1,0:T(8,128)S(1)} %copy-done.1, f32[4,13,128]{2,1,0:T(8,128)S(1)} %reshape.29.table_ref), custom_call_target="tpu_custom_call" | custom-call | tf_op jit(solution)/shard_map/gather_bias/pallas_call | solution.py:76
  25.9 0.1 slice_maximum_fusion
  26.0 0.0 collective-permute-done.2
  26.0 0.3 pad_maximum_fusion.1
  26.3 0.2 copy.20
  26.5 0.0 copy-start.2
  26.5 0.6 %copy-done.2 = f32[128]{0:T(128)S(1)} copy-done((f32[128]{0:T(128)S(1)}, f32[128]{0:T(128)}, u32[]{:S(2)}) %copy-start.2) | copy-done | bytes 536
  27.2 17.3 %window_block.1 = bf16[8,256,128]{2,1,0:T(8,128)(2,1)S(1)} custom-call(bf16[8,256,128]{2,1,0:T(8,128)(2,1)S(1)} %bitcast.24, f32[8,1,256]{2,1,0:T(1,128)S(1)} %convert_element_type.25.label_ref, f32[4,256,256]{2,1,0:T(8,128)S(1)} %gather_bias.1.bias_ref, f32[1,128]{1,0:T(1,128)S(1)} %bitcast.31, bf16[128,384]{1,0:T(8,128)(2,1)S(1)} %copy-done, ...), custom_call_target="tpu_custom_call" | custom-call | tf_op jit(solution)/shard_map/window_block/pallas_call | solution.py:159
  44.5 0.3 copy.29
  44.8 0.1 slice.60
  45.0 0.1 collective-permute-start.3
  45.0 1.3 %collective-permute-done.3 = bf16[8,32,2,128]{3,2,1,0:T(2,128)(2,1)S(1)} collective-permute-done((bf16[8,32,2,128]{3,2,1,0:T(2,128)(2,1)S(1)}, bf16[8,32,2,128]{3,2,1,0:T(2,128)(2,1)S(1)}, u32[]{:S(2)}, u32[]{:S(2)}) %collective-permute-start.3) | collective-permute-done | bytes 131104 | tf_op jit(solution)/shard_map/ppermute | solution.py:27
  46.4 1.6 %collective-permute-start.4 = (bf16[8,4,8,128]{3,2,1,0:T(8,128)(2,1)S(1)}, bf16[8,4,8,128]{3,2,1,0:T(8,128)(2,1)S(1)}, u32[]{:S(2)}, u32[]{:S(2)}) collective-permute-start(bf16[8,4,8,128]{3,2,1,0:T(8,128)(2,1)S(1)} %pad_maximum_fusion.4), channel_id=1, source_target_pairs={{0,2},{2,0},{1,3},{3,1},{4,6},{6,4},{5,7},{7,5},{8,10},{10,8},{9,1... | collective-permute-start | bytes 196616 | tf_op jit(solution)/shard_map/ppermute | solution.py:27
  48.0 2.8 %collective-permute-done.4 = bf16[8,4,8,128]{3,2,1,0:T(8,128)(2,1)S(1)} collective-permute-done((bf16[8,4,8,128]{3,2,1,0:T(8,128)(2,1)S(1)}, bf16[8,4,8,128]{3,2,1,0:T(8,128)(2,1)S(1)}, u32[]{:S(2)}, u32[]{:S(2)}) %collective-permute-start.4) | collective-permute-done | bytes 65568 | tf_op jit(solution)/shard_map/ppermute | solution.py:27
  50.7 0.2 fusion
  51.0 0.5 collective-permute-start.5
  51.5 9.3 %collective-permute-done.5 = bf16[4,32,8,128]{3,2,1,0:T(8,128)(2,1)S(1)} collective-permute-done((bf16[4,32,8,128]{3,2,1,0:T(8,128)(2,1)S(1)}, bf16[4,32,8,128]{3,2,1,0:T(8,128)(2,1)S(1)}, u32[]{:S(2)}, u32[]{:S(2)}) %collective-permute-start.5) | collective-permute-done | bytes 262176 | tf_op jit(solution)/shard_map/ppermute | solution.py:27
  60.8 0.8 %pad_maximum_fusion.2 = bf16[8,32,8,128]{3,2,1,0:T(8,128)(2,1)} fusion(bf16[4,32,8,128]{3,2,1,0:T(8,128)(2,1)S(1)} %get-tuple-element.6, bf16[4,32,8,128]{3,2,1,0:T(8,128)(2,1)S(1)} %collective-permute-done.5), kind=kLoop, calls=%fused_computation.6 | loop fusion | flops 262144 | bytes 1048576 | tf_op jit(solution)/shard_map/concatenate | solution.py:50
  (10 shorter events, 0.2 us)
Async XLA Ops:
  1.1 10.7 %collective-permute-start = (bf16[4,32,8,128]{3,2,1,0:T(8,128)(2,1)S(1)}, bf16[4,32,8,128]{3,2,1,0:T(8,128)(2,1)S(1)}, u32[]{:S(2)}, u32[]{:S(2)}) collective-permute-start(bf16[4,32,8,128]{3,2,1,0:T(8,128)(2,1)S(1)} %get-tuple-element.8), channel_id=1, source_target_pairs={{0,12},{4,0},{8,4},{12,8},{1,13},{5,1},{9,5},{13,9},{2,14},{6,2},{... | collective-permute-start | bytes 786440 | tf_op jit(solution)/shard_map/ppermute | solution.py:27
  11.7 4.3 %collective-permute-start.1 = (bf16[8,4,8,128]{3,2,1,0:T(8,128)(2,1)S(1)}, bf16[8,4,8,128]{3,2,1,0:T(8,128)(2,1)S(1)}, u32[]{:S(2)}, u32[]{:S(2)}) collective-permute-start(bf16[8,4,8,128]{3,2,1,0:T(8,128)(2,1)S(1)} %pad_maximum_fusion.5), channel_id=1, source_target_pairs={{0,2},{2,0},{1,3},{3,1},{4,6},{6,4},{5,7},{7,5},{8,10},{10,8},{9,1... | collective-permute-start | bytes 196616 | tf_op jit(solution)/shard_map/ppermute | solution.py:27
  13.3 2.9 %copy-start = (bf16[128,384]{1,0:T(8,128)(2,1)S(1)}, bf16[128,384]{1,0:T(8,128)(2,1)}, u32[]{:S(2)}) copy-start(bf16[128,384]{1,0:T(8,128)(2,1)} %w_qkv_ref.1) | copy-start | bytes 294916
  16.1 0.7 %copy-start.7 = (f32[1575,4]{0,1:T(4,128)S(1)}, f32[1575,4]{0,1:T(4,128)}, u32[]{:S(2)}) copy-start(f32[1575,4]{0,1:T(4,128)} %param.13) | copy-start | bytes 75604
  16.2 9.8 %collective-permute-start.2 = (bf16[8,32,2,128]{3,2,1,0:T(2,128)(2,1)S(1)}, bf16[8,32,2,128]{3,2,1,0:T(2,128)(2,1)S(1)}, u32[]{:S(2)}, u32[]{:S(2)}) collective-permute-start(bf16[8,32,2,128]{3,2,1,0:T(2,128)(2,1)S(1)} %pad_maximum_fusion.3), channel_id=1, source_target_pairs={{0,1},{1,0},{2,3},{3,2},{4,5},{5,4},{6,7},{7,6},{8,9},{9,8},{10,11... | collective-permute-start | bytes 393224 | tf_op jit(solution)/shard_map/ppermute | solution.py:27
  16.9 0.8 %copy-start.5 = (s32[8,32,8]{1,2,0:T(8,128)S(1)}, s32[8,32,8]{1,2,0:T(8,128)}, u32[]{:S(2)}) copy-start(s32[8,32,8]{1,2,0:T(8,128)} %param.11) | copy-start | bytes 24580
  17.7 0.8 %copy-start.6 = (bf16[128,128]{1,0:T(8,128)(2,1)S(1)}, bf16[128,128]{1,0:T(8,128)(2,1)}, u32[]{:S(2)}) copy-start(bf16[128,128]{1,0:T(8,128)(2,1)} %param.16) | copy-start | bytes 98308
  18.5 0.7 %copy-start.8 = (f32[128]{0:T(128)S(1)}, f32[128]{0:T(128)}, u32[]{:S(2)}) copy-start(f32[128]{0:T(128)} %param.17) | copy-start | bytes 1540
  20.1 0.9 %copy-start.3 = (bf16[128,512]{1,0:T(8,128)(2,1)S(1)}, bf16[128,512]{1,0:T(8,128)(2,1)}, u32[]{:S(2)}) copy-start(bf16[128,512]{1,0:T(8,128)(2,1)} %param.18) | copy-start | bytes 393220
  20.1 1.0 %copy-start.4 = (bf16[512,128]{1,0:T(8,128)(2,1)S(1)}, bf16[512,128]{1,0:T(8,128)(2,1)}, u32[]{:S(2)}) copy-start(bf16[512,128]{1,0:T(8,128)(2,1)} %param.19) | copy-start | bytes 393220
  21.0 1.0 %copy-start.1 = (s32[256,256]{1,0:T(8,128)S(1)}, s32[256,256]{1,0:T(8,128)}, u32[]{:S(2)}) copy-start(s32[256,256]{1,0:T(8,128)} %index_ref.1) | copy-start | bytes 786436
  26.5 0.7 %copy-start.2 = (f32[128]{0:T(128)S(1)}, f32[128]{0:T(128)}, u32[]{:S(2)}) copy-start(f32[128]{0:T(128)} %param.14) | copy-start | bytes 1540
  45.0 1.4 %collective-permute-start.3 = (bf16[8,32,2,128]{3,2,1,0:T(2,128)(2,1)S(1)}, bf16[8,32,2,128]{3,2,1,0:T(2,128)(2,1)S(1)}, u32[]{:S(2)}, u32[]{:S(2)}) collective-permute-start(bf16[8,32,2,128]{3,2,1,0:T(2,128)(2,1)S(1)} %slice.60), channel_id=1, source_target_pairs={{0,1},{1,0},{2,3},{3,2},{4,5},{5,4},{6,7},{7,6},{8,9},{9,8},{10,11... | collective-permute-start | bytes 393224 | tf_op jit(solution)/shard_map/ppermute | solution.py:27
  46.4 4.3 %collective-permute-start.4 = (bf16[8,4,8,128]{3,2,1,0:T(8,128)(2,1)S(1)}, bf16[8,4,8,128]{3,2,1,0:T(8,128)(2,1)S(1)}, u32[]{:S(2)}, u32[]{:S(2)}) collective-permute-start(bf16[8,4,8,128]{3,2,1,0:T(8,128)(2,1)S(1)} %pad_maximum_fusion.4), channel_id=1, source_target_pairs={{0,2},{2,0},{1,3},{3,1},{4,6},{6,4},{5,7},{7,5},{8,10},{10,8},{9,1... | collective-permute-start | bytes 196616 | tf_op jit(solution)/shard_map/ppermute | solution.py:27
  51.0 9.8 %collective-permute-start.5 = (bf16[4,32,8,128]{3,2,1,0:T(8,128)(2,1)S(1)}, bf16[4,32,8,128]{3,2,1,0:T(8,128)(2,1)S(1)}, u32[]{:S(2)}, u32[]{:S(2)}) collective-permute-start(bf16[4,32,8,128]{3,2,1,0:T(8,128)(2,1)S(1)} %get-tuple-element.5), channel_id=1, source_target_pairs={{0,4},{4,8},{8,12},{12,0},{1,5},{5,9},{9,13},{13,1},{2,6},{6,10},{... | collective-permute-start | bytes 786440 | tf_op jit(solution)/shard_map/ppermute | solution.py:27

commit v2 on v1

v2 whole, which is shorter than its diff:
```python
import math

import jax
import jax.numpy as jnp
from jax import lax
from jax.experimental import pallas as pl
from jax.experimental.pallas import tpu as pltpu
from jax.sharding import PartitionSpec as P

HEADS = 4
WX = 8
WY = 8
WZ = 4
SX = 4
SY = 4
SZ = 2
WTOK = WX * WY * WZ
LANES = 128
F32 = jnp.float32
BF16 = jnp.bfloat16
LOG2E = 1.4426950408889634


def prepare_kernel(
    index_ref, table_ref, w_qkv_ref, w_proj_ref, w_up_ref, w_down_ref,
    bias_ref, w_qv_t_ref, w_k_ref, w_proj_t_ref, w_up_t_ref, w_down_t_ref,
):
    width = w_proj_ref.shape[0]
    w_qv_t_ref[:width] = w_qkv_ref[:, :width].T
    w_qv_t_ref[width:] = w_qkv_ref[:, 2 * width :].T
    w_k_ref[...] = w_qkv_ref[:, width : 2 * width]
    w_proj_t_ref[...] = w_proj_ref[...].T
    w_up_t_ref[...] = w_up_ref[...].T
    w_down_t_ref[...] = w_down_ref[...].T
    chunks = table_ref.shape[1]
    index = index_ref[...].astype(F32).T.astype(jnp.int32)
    for column in range(0, WTOK, LANES):
        for row in range(0, WTOK, 8):
            part = index[row : row + 8, column : column + LANES]
            low = part & (LANES - 1)
            high = part >> 7
            found = [jnp.zeros((8, LANES), F32) for _ in range(HEADS)]
            for chunk in range(chunks):
                here = high == chunk
                for head in range(HEADS):
                    line = jnp.broadcast_to(table_ref[head, chunk : chunk + 1, :], (8, LANES))
                    got = jnp.take_along_axis(line, low, axis=1, mode="promise_in_bounds")
                    found[head] = jnp.where(here, got, found[head])
            for head in range(HEADS):
                bias_ref[head, row : row + 8, column : column + LANES] = found[head] * LOG2E


def prepare(rel_index, bias_table, w_qkv, w_proj, w_up, w_down):
    rows = bias_table.shape[0]
    width, hidden = w_up.shape
    chunks = -(-rows // LANES)
    table = jnp.pad(bias_table.T, ((0, 0), (0, chunks * LANES - rows))).reshape(HEADS, chunks, LANES)
    shapes = [(2 * width, width), (width, width), (width, width), (hidden, width), (width, hidden)]
    return pl.pallas_call(
        prepare_kernel,
        out_shape=[jax.ShapeDtypeStruct((HEADS, WTOK, WTOK), F32)]
        + [jax.ShapeDtypeStruct(shape, BF16) for shape in shapes],
        cost_estimate=cost(4),
        compiler_params=pltpu.CompilerParams(vmem_limit_bytes=32 << 20),
        name="bias_and_weights",
    )(rel_index, table, w_qkv, w_proj, w_up, w_down)


def dot_nn(left, right):
    return lax.dot_general(left, right, (((1,), (0,)), ((), ())), preferred_element_type=F32)


def dot_nt(left, right):
    return lax.dot_general(left, right, (((1,), (1,)), ((), ())), preferred_element_type=F32)


def eye(size):
    rows = lax.broadcasted_iota(jnp.int32, (size, size), 0)
    columns = lax.broadcasted_iota(jnp.int32, (size, size), 1)
    return (rows == columns).astype(BF16)


def gelu(value):
    return 0.5 * value * (1.0 + lax.erf(value * (0.5**0.5)))


HALF = SX * WY * WZ
EDGE = HALF // 2


def moved(value, axis, steps):
    names = (axis,) if isinstance(axis, str) else tuple(axis)
    moves = (steps,) if isinstance(axis, str) else tuple(steps)
    counts = [lax.axis_size(name) for name in names]
    pairs = []
    for source in range(math.prod(counts)):
        left, target, stride = source, 0, 1
        for count, move in zip(reversed(counts), reversed(moves)):
            target += (left % count + move) % count * stride
            left //= count
            stride *= count
        pairs.append((source, target))
    return lax.ppermute(value, names, pairs)


def turned(value, steps):
    return pltpu.roll(value, steps % 8, axis=1)


def sublane(shape):
    return lax.broadcasted_iota(jnp.int32, shape, 1)


def pair_core(tall):
    number = tall.shape[0]
    split = tall.reshape(number // 2, 2, 8, LANES)
    first, second = split[:, 0], split[:, 1]
    return jnp.where(sublane(first.shape) < 4, turned(first, -2), turned(second, 2))


def quad_low(tall):
    number = tall.shape[0]
    split = tall.reshape(number // 4, 4, 8, LANES)
    at = sublane((number // 4, 8, LANES))
    low = jnp.where(at < 2, split[:, 0], turned(split[:, 1], 2))
    high = jnp.where(at < 6, turned(split[:, 2], 4), turned(split[:, 3], 6))
    return jnp.where(at < 4, low, high)


def pair_edge(tall, quads):
    number = tall.shape[0]
    split = tall.reshape(number // 4, 4, 8, LANES)
    at = sublane(quads.shape)
    even = jnp.where(
        at < 4,
        jnp.where(at < 2, turned(split[:, 0], 2), turned(quads, 2)),
        jnp.where(at < 6, turned(split[:, 1], -2), turned(quads, 4)),
    )
    odd = jnp.where(
        at < 4,
        jnp.where(at < 2, turned(split[:, 2], 2), turned(quads, -2)),
        jnp.where(at < 6, turned(split[:, 3], -2), quads),
    )
    return jnp.stack([even, odd], axis=1).reshape(number // 2, 8, LANES)


def unpair_edge(pairs):
    number = pairs.shape[0]
    split = pairs.reshape(number // 2, 2, 8, LANES)
    first, second = split[:, 0], split[:, 1]
    at = sublane(first.shape)
    near = jnp.where(
        at < 4,
        jnp.where(at < 2, first, turned(first, -2)),
        jnp.where(at < 6, turned(second, 4), turned(second, 2)),
    )
    far = jnp.where(
        at < 4,
        jnp.where(at < 2, turned(first, -2), turned(first, 4)),
        jnp.where(at < 6, turned(second, 2), second),
    )
    return near, far


def join_tall(low, core, near):
    number = low.shape[0]
    split = core.reshape(number, 2, 8, LANES)
    at = sublane(low.shape)
    parts = []
    for y in range(4):
        bottom = turned(low, -2 * y)
        top = turned(near, 6 - 2 * y)
        middle = turned(split[:, y // 2], 2 - 4 * (y % 2))
        parts.append(jnp.where(at < 2, bottom, jnp.where(at < 6, middle, top)))
    return jnp.stack(parts, axis=1).reshape(number * 4, 8, LANES)


def tall_of(ref, x_from, y_from, y_to, size_z=8):
    part = ref[x_from : x_from + SX, y_from * size_z : y_to * size_z, :]
    return part.astype(F32).reshape(-1, 8, LANES)


def rows_of(groups, *lead):
    return groups.reshape(*lead, -1, LANES).astype(BF16)


def as_groups(ref_value):
    return ref_value.astype(F32).reshape(-1, 8, LANES)


def first_kernel(tokens_ref, send_ref, own_ref, low_ref):
    blocks = own_ref.shape[0]
    for block in range(blocks):
        start = SY + block * WY
        for x_from, out_ref in ((SX, send_ref), (0, own_ref)):
            out_ref[block] = rows_of(pair_core(tall_of(tokens_ref, x_from, start, start + WY)))
    size_y = low_ref.shape[1] // SZ
    for x_from in (0, SX):
        low = quad_low(tall_of(tokens_ref, x_from, 0, size_y))
        low_ref[x_from : x_from + SX] = rows_of(low, SX)


def second_kernel(tokens_ref, low_ref, label_ref, send_ref, own_ref, border_ref, inner_ref):
    blocks = own_ref.shape[0]
    size_y = low_ref.shape[1] // SZ

    def edge(x_from, start, stop):
        return pair_edge(
            tall_of(tokens_ref, x_from, start, stop), tall_of(low_ref, x_from, start, stop, SZ)
        )

    for block in range(blocks):
        start = SY + block * WY
        send_ref[block * HALF : (block + 1) * HALF] = rows_of(edge(SX, start, start + WY))
        own_ref[block] = rows_of(edge(0, start, start + WY))
    send_ref[blocks * HALF :] = label_ref[...]
    for half, x_from in enumerate((SX, 0)):
        for start, out_ref in ((0, border_ref), (size_y - SY, inner_ref)):
            stop = start + SY
            out_ref[half, 0] = rows_of(pair_core(tall_of(tokens_ref, x_from, start, stop)))
            out_ref[half, 1] = rows_of(edge(x_from, start, stop))


def third_kernel(inner_ref, border_ref, send_ref, own_ref):
    rows = SY * WZ
    for half, out_ref in enumerate((send_ref, own_ref)):
        for window in range(out_ref.shape[0]):
            for plane in range(SX):
                span = slice(plane * rows, (plane + 1) * rows)
                at = 2 * plane * rows
                out_ref[window, at : at + rows] = inner_ref[half, window, span]
                out_ref[window, at + rows : at + 2 * rows] = border_ref[half, window, span]


def windows_after(x16s, rows, bias_ref, weights, ahead=4):
    gain_attn, gain_mlp, w_qv_t, w_k, w_proj_t, w_up_t, w_down_t = weights
    width = x16s[0].shape[1]
    size = width // HEADS
    scale = size**-0.5 * LOG2E
    eye_window = eye(WTOK)
    eye_width = eye(width)
    n = len(x16s)
    st = []
    for x16, row in zip(x16s, rows):
        x = x16.astype(F32)
        center = x - jnp.mean(x, axis=1, keepdims=True)
        spread = jnp.mean(center * center, axis=1, keepdims=True)
        normed = (center * lax.rsqrt(spread + 1e-05) * gain_attn[...]).astype(BF16)
        x_t = dot_nt(eye_width, x16)
        qv_t = dot_nt(w_qv_t[...], normed).astype(BF16)
        q_t, v_t = qv_t[:width], qv_t[width:]
        k = dot_nn(normed, w_k[...]).astype(BF16)
        column = dot_nt(eye_window, jnp.broadcast_to(row, (WTOK, WTOK)).astype(BF16))
        fade = jnp.where(column == row, 0.0, -1e9 * LOG2E)
        st.append((x_t, q_t, v_t, k, fade))

    tasks = [(w, h) for w in range(n) for h in range(HEADS)]

    def scores(task):
        w, h = task
        x_t, q_t, v_t, k, fade = st[w]
        span = slice(h * size, (h + 1) * size)
        pieces = [jnp.zeros((size, WTOK), BF16)] * HEADS
        pieces[h] = q_t[span]
        return dot_nn(k, jnp.concatenate(pieces, axis=0))

    def attend(task, raw):
        w, h = task
        x_t, q_t, v_t, k, fade = st[w]
        span = slice(h * size, (h + 1) * size)
        score = raw * scale + bias_ref[h] + fade
        weight = jnp.exp2(score - jnp.max(score, axis=0, keepdims=True))
        total = jnp.sum(weight, axis=0, keepdims=True)
        part = dot_nn(v_t[span], weight.astype(BF16))
        return (part * (1.0 / total)).astype(BF16)

    raws = {}
    outs = {}
    for i in range(min(ahead, len(tasks))):
        raws[i] = scores(tasks[i])
    for i, task in enumerate(tasks):
        if i + ahead < len(tasks):
            raws[i + ahead] = scores(tasks[i + ahead])
        outs[task] = attend(task, raws.pop(i))
    middles = []
    for w in range(n):
        attended = jnp.concatenate([outs[(w, h)] for h in range(HEADS)], axis=0)
        middles.append((st[w][0] + dot_nn(w_proj_t[...], attended)).astype(BF16).astype(F32))
    normeds = []
    for middle in middles:
        center = middle - jnp.mean(middle, axis=0, keepdims=True)
        spread = jnp.mean(center * center, axis=0, keepdims=True)
        normeds.append((center * lax.rsqrt(spread + 1e-05) * gain_mlp[...]).astype(BF16))
    hiddens = [dot_nn(w_up_t[...], normed) for normed in normeds]
    hiddens = [gelu(hidden).astype(BF16) for hidden in hiddens]
    afters = [(m + dot_nn(w_down_t[...], h)).astype(BF16) for m, h in zip(middles, hiddens)]
    return [dot_nt(eye_window, after) for after in afters]


def label_row(label_ref, base, window):
    at = base + 2 * window
    pair = label_ref[at : at + 2, :].astype(F32)
    return jnp.concatenate([pair[0:1], pair[1:2]], axis=1)


def inside_kernel(near0_ref, own0_ref, near1_ref, own1_ref, bias_ref, *rest):
    weights, (back_ref, kept_ref) = rest[:7], rest[7:]
    blocks = own0_ref.shape[0]
    x16s, rows = [], []
    for block in range(blocks):
        span = slice(block * HALF, (block + 1) * HALF)
        x16s.append(jnp.concatenate([near0_ref[block], own0_ref[block]], axis=0))
        x16s.append(jnp.concatenate([near1_ref[span], own1_ref[block]], axis=0))
        rows += [label_row(near1_ref, blocks * HALF, 2 * block + layer) for layer in range(2)]
    afters = windows_after(x16s, rows, bias_ref, weights)
    for at, after in enumerate(afters):
        after = after.astype(BF16)
        back_ref[at % 2, at // 2] = after[:HALF]
        kept_ref[at % 2, at // 2] = after[HALF:]


def across_kernel(label_ref, near_ref, own_ref, bias_ref, *rest):
    weights, outs = rest[:7], rest[7:]
    blocks = label_ref.shape[0] // HALF
    x16s = [jnp.concatenate([near_ref[at], own_ref[at]], axis=0) for at in range(2)]
    rows = [label_row(label_ref, blocks * HALF, 2 * blocks + at) for at in range(2)]
    afters = windows_after(x16s, rows, bias_ref, weights)
    for at, after in enumerate(afters):
        split = after.astype(BF16).reshape(2, SX, 2, SY * WZ, LANES)
        for half in range(2):
            for side in range(2):
                outs[2 * half + side][at] = split[half, :, side].reshape(EDGE, LANES)


def far_kernel(
    kept_ref, back_ref, inner_own_ref, inner_back_ref, border_own_ref, border_back_ref, out_ref
):
    blocks = kept_ref.shape[1]
    size_y = out_ref.shape[1] // SZ
    for x_from, whole_ref, inner_ref, border_ref in (
        (0, kept_ref, inner_own_ref, border_own_ref),
        (SX, back_ref, inner_back_ref, border_back_ref),
    ):
        pieces = [(SY + block * WY, WY, whole_ref[1, block]) for block in range(blocks)]
        pieces += [(size_y - SY, SY, inner_ref[1]), (0, SY, border_ref[1])]
        for start, count, piece in pieces:
            far = unpair_edge(as_groups(piece))[1]
            out_ref[x_from : x_from + SX, start * SZ : (start + count) * SZ] = rows_of(far, SX)


def last_kernel(
    low_ref, kept_ref, back_ref, inner_own_ref, inner_back_ref, border_own_ref, border_back_ref, out_ref
):
    blocks = kept_ref.shape[1]
    size_y = low_ref.shape[1] // SZ
    size_z = 8
    for x_from, whole_ref, inner_ref, border_ref in (
        (0, kept_ref, inner_own_ref, border_own_ref),
        (SX, back_ref, inner_back_ref, border_back_ref),
    ):
        pieces = [
            (SY + block * WY, WY, whole_ref[0, block], whole_ref[1, block]) for block in range(blocks)
        ]
        pieces += [(size_y - SY, SY, inner_ref[0], inner_ref[1]), (0, SY, border_ref[0], border_ref[1])]
        for start, count, core, edge in pieces:
            low = tall_of(low_ref, x_from, start, start + count, SZ)
            near = unpair_edge(as_groups(edge))[0]
            tall = join_tall(low, as_groups(core), near)
            out_ref[x_from : x_from + SX, start * size_z : (start + count) * size_z] = rows_of(tall, SX)


def cost(micros):
    return pl.CostEstimate(flops=int(micros * 1.1e9), bytes_accessed=int(micros * 3.3e6), transcendentals=0)


def kernel_call(kernel, name, micros, outs, *operands):
    return pl.pallas_call(
        kernel,
        out_shape=[jax.ShapeDtypeStruct(shape, BF16) for shape in outs],
        cost_estimate=cost(micros),
        compiler_params=pltpu.CompilerParams(vmem_limit_bytes=48 << 20),
        name=name,
    )(*operands)


def per_device(
    tokens, region, rel_index, bias_table, gain_attn, w_qkv, w_proj, gain_mlp, w_up, w_down
):
    size_x, size_y, size_z, width = tokens.shape
    blocks = size_y // WY - 1
    flat = tokens.reshape(size_x, size_y * size_z, width)
    halves = (blocks, HALF, width)
    edges = (2, EDGE, width)
    labels = region.reshape(size_x, size_y // WY, WY, size_z // WZ, WZ).transpose(1, 3, 0, 2, 4)
    labels = labels.reshape(-1, LANES).astype(BF16)

    send0, own0, low = kernel_call(
        first_kernel, "first_pieces", 0.2, [halves, halves, (size_x, size_y * SZ, width)], flat
    )
    near0 = moved(send0, "gx", 1)
    low = moved(low, "gz", -1)
    send1, own1, border, inner = kernel_call(
        second_kernel,
        "second_pieces",
        0.2,
        [(blocks * HALF + labels.shape[0], width), halves, (2,) + edges, (2,) + edges],
        flat,
        low,
        labels,
    )
    near1 = moved(send1, "gx", 1)
    border = moved(border, "gy", -1)
    bias, *turned_weights = prepare(rel_index, bias_table, w_qkv, w_proj, w_up, w_down)
    send2, own2 = kernel_call(
        third_kernel, "third_pieces", 0.2, [(2, HALF, width), (2, HALF, width)], inner, border
    )
    near2 = moved(send2, "gx", 1)
    fixed = (bias, gain_attn[None], gain_mlp[:, None], *turned_weights)
    back, kept = kernel_call(
        inside_kernel, "inside_windows", 5, [(2,) + halves, (2,) + halves], near0, own0, near1, own1, *fixed
    )
    back = moved(back, "gx", -1)
    inner_back, border_back, inner_own, border_own = kernel_call(
        across_kernel, "across_windows", 2.3, [edges] * 4, near1, near2, own2, *fixed
    )
    inner_back = moved(inner_back, "gx", -1)
    border_back = moved(border_back, ("gx", "gy"), (-1, 1))
    border_own = moved(border_own, "gy", 1)
    after = (kept, back, inner_own, inner_back, border_own, border_back)
    far = kernel_call(far_kernel, "far_pieces", 0.1, [(size_x, size_y * SZ, width)], *after)[0]
    far = moved(far, "gz", 1)
    out = kernel_call(last_kernel, "last_pieces", 1, [flat.shape], far, *after)[0]
    return out.reshape(tokens.shape)


def solution(mesh):
    field = P(("cand", "gx"), "gy", "gz", None)
    placed = (field, P(("cand", "gx"), "gy", "gz")) + (P(),) * 8
    return jax.shard_map(
        per_device, mesh=mesh, in_specs=placed, out_specs=field, check_vma=False
    )
```

time: 62.1 us -> 34.3 us (0.55)
  waiting for transfers between devices: 21.7 us -> 4.55 us
  Pallas kernels: 21.2 us -> 12.6 us
  local copies, waits for them, and re-layouts: 8.04 us -> 3.83 us
  starting transfers between devices: 8.87 us -> 12.9 us
  other arithmetic: 1.67 us -> 0.01 us
    ppermute x6 -> x10, waiting for transfers between devices: 21.7 us -> 4.55 us  [moved(): return lax.ppermute(value, names, pairs)]
    pallas_call x2 -> x8, Pallas kernels: 21.2 us -> 12.6 us  [the longest x7 8.65 us: kernel_call(): pl.pallas_call(kernel, out_shape=[jax.ShapeDtypeStruct(shape, BF16) for s...]
    ppermute x6 -> x10, starting transfers between devices: 8.87 us -> 12.9 us  [moved(): return lax.ppermute(value, names, pairs)]
    unnamed x23 -> x22, local copies, waits for them, and re-layouts: 5.44 us -> 2.94 us
    concatenate x7 -> x0, other arithmetic: 1.63 us -> none  [the longest x2 1.08 us: roll_along(): return jnp.concatenate([shifted_2(piece, name, 1), rest], axis=axis)]
    slice x4 -> x0, local copies, waits for them, and re-layouts: 1.25 us -> none  [the longest x1 1.06 us: roll_along(): rest = lax.slice_in_dim(volume, steps, size, axis=axis)]
  transfers between devices with their start and end apart: 6 -> 10, of which waited for: 5 -> 4; matrix products, arithmetic and copies ran while one was open for 3% -> 3% of each run, Pallas kernels for 6% -> 33%
where the time goes in v2:
time: 34.3 us; the launch traced here: 34.1 us
  starting transfers between devices  12.9 us (38%)
  Pallas kernels  12.6 us (37%)
  waiting for transfers between devices  4.55 us (13%)
  local copies, waits for them, and re-layouts  3.83 us (11%)
    ppermute x10, starting transfers between devices, moved(): return lax.ppermute(value, names, pairs)  12.9 us
    pallas_call x7, Pallas kernels, kernel_call(): pl.pallas_call(kernel, out_shape=[jax.ShapeDtypeStruct(shape, BF16) for s...  8.65 us
    ppermute x10, waiting for transfers between devices, moved(): return lax.ppermute(value, names, pairs)  4.55 us
    pallas_call x1, Pallas kernels, prepare(): pl.pallas_call(prepare_kernel, out_shape=[jax.ShapeDtypeStruct((HEADS, WT...  3.95 us
    unnamed x22, local copies, waits for them, and re-layouts  2.94 us
    convert_element_type x3, local copies, waits for them, and re-layouts, per_device(): labels = labels.reshape(-1, LANES).astype(BF16)  0.75 us
  transfers between devices with their start and end apart: 10, of which 4 were waited for; matrix products, arithmetic and copies ran while one was open for 3% of the time, Pallas kernels for 33%

profile of v2, /device:TPU:0, one launch (start us, length us, event | category | flops | bytes accessed | tf_op | source)
XLA Modules:
  0.0 34.1 jit_solution(18187737658072283963)
XLA Ops:
  0.0 1.0 %copy-done = bf16[8,32,8,128]{3,2,1,0:T(8,128)(2,1)S(1)} copy-done((bf16[8,32,8,128]{3,2,1,0:T(8,128)(2,1)S(1)}, bf16[8,32,8,128]{3,2,1,0:T(8,128)(2,1)}, u32[]{:S(2)}) %copy-start) | copy-done | bytes 524312
  1.0 0.2 first_pieces.1
  1.2 0.5 %collective-permute-start.1 = (bf16[8,64,128]{2,1,0:T(8,128)(2,1)S(1)}, bf16[8,64,128]{2,1,0:T(8,128)(2,1)S(1)}, u32[]{:S(2)}, u32[]{:S(2)}) collective-permute-start(bf16[8,64,128]{2,1,0:T(8,128)(2,1)S(1)} %get-tuple-element.28), channel_id=1, source_target_pairs={{0,1},{1,0},{2,3},{3,2},{4,5},{5,4},{6,7},{7,6},{8,9},{9,8},{10,11... | collective-permute-start | bytes 393224 | tf_op jit(solution)/shard_map/ppermute | solution.py:103
  1.7 2.6 %collective-permute-start = (bf16[3,128,128]{2,1,0:T(8,128)(2,1)S(1)}, bf16[3,128,128]{2,1,0:T(8,128)(2,1)S(1)}, u32[]{:S(2)}, u32[]{:S(2)}) collective-permute-start(bf16[3,128,128]{2,1,0:T(8,128)(2,1)S(1)} %get-tuple-element.26), channel_id=1, source_target_pairs={{0,4},{4,8},{8,12},{12,0},{1,5},{5,9},{9,13},{13,1},{2,6},{6,10},{... | collective-permute-start | bytes 294920 | tf_op jit(solution)/shard_map/ppermute | solution.py:103
  4.4 0.0 copy-done.8
  4.4 0.1 convert_element_type.12
  4.5 0.5 %copy.14 = bf16[8,4,8,2,4]{4,2,0,3,1:T(8,128)(2,1)S(1)} copy(bf16[8,4,8,2,4]{2,1,4,3,0:T(4,128)(2,1)S(1)} %convert_element_type.12) | data formatting | bytes 8192 | tf_op jit(solution)/shard_map/convert_element_type | solution.py:395
  4.9 0.2 convert_element_type.14.label_ref
  5.1 0.6 %copy-done.9 = f32[1575,4]{0,1:T(4,128)S(1)} copy-done((f32[1575,4]{0,1:T(4,128)S(1)}, f32[1575,4]{0,1:T(4,128)}, u32[]{:S(2)}) %copy-start.9) | copy-done | bytes 25224
  5.7 0.0 copy-start.2
  5.7 0.0 copy-start.3
  5.7 0.0 copy-start.4
  5.8 0.0 copy-start.5
  5.8 0.0 copy-start.6
  5.8 0.0 collective-permute-done.1.low_ref
  5.8 0.0 copy-done.1
  5.8 0.2 second_pieces.1
  6.0 1.6 %collective-permute-start.4 = (bf16[2,2,64,128]{3,2,1,0:T(8,128)(2,1)S(1)}, bf16[2,2,64,128]{3,2,1,0:T(8,128)(2,1)S(1)}, u32[]{:S(2)}, u32[]{:S(2)}) collective-permute-start(bf16[2,2,64,128]{3,2,1,0:T(8,128)(2,1)S(1)} %get-tuple-element.40), channel_id=1, source_target_pairs={{0,2},{2,0},{1,3},{3,1},{4,6},{6,4},{5,7},{7,5},{8,10},{10,8},{9,1... | collective-permute-start | bytes 196616 | tf_op jit(solution)/shard_map/ppermute | solution.py:103
  7.5 1.6 %collective-permute-start.2 = (bf16[400,128]{1,0:T(8,128)(2,1)S(1)}, bf16[400,128]{1,0:T(8,128)(2,1)S(1)}, u32[]{:S(2)}, u32[]{:S(2)}) collective-permute-start(bf16[400,128]{1,0:T(8,128)(2,1)S(1)} %get-tuple-element.29), channel_id=1, source_target_pairs={{0,4},{4,8},{8,12},{12,0},{1,5},{5,9},{9,13},{13,1},{2,6},{6,10},{... | collective-permute-start | bytes 307208 | tf_op jit(solution)/shard_map/ppermute | solution.py:103
  9.1 0.0 copy-done.2
  9.1 0.0 copy-done.3
  9.1 0.0 copy-done.4
  9.1 0.0 copy-done.5
  9.1 0.0 copy-done.6
  9.1 4.0 %bias_and_weights.1 = (f32[4,256,256]{2,1,0:T(8,128)S(1)}, bf16[256,128]{1,0:T(8,128)(2,1)S(1)}, bf16[128,128]{1,0:T(8,128)(2,1)S(1)}, bf16[128,128]{1,0:T(8,128...) custom-call(s32[256,256]{1,0:T(8,128)S(1)} %copy-done.2, f32[4,13,128]{2,1,0:T(8,128)S(1)} %reshape.14.table_ref, ...), custom_call_target="tpu_custom_call" | custom-call | flops 4400000000 | bytes 13200000 | tf_op jit(solution)/shard_map/bias_and_weights/pallas_call | solution.py:59
  13.1 0.0 copy-start.10
  13.1 0.6 %copy-done.10 = f32[128]{0:T(128)S(1)} copy-done((f32[128]{0:T(128)S(1)}, f32[128]{0:T(128)}, u32[]{:S(2)}) %copy-start.10) | copy-done | bytes 536
  13.8 0.1 copy.15.rest_1_
  13.9 0.0 collective-permute-done.4.border_ref
  13.9 1.6 %collective-permute-start.5 = (bf16[2,128,128]{2,1,0:T(8,128)(2,1)S(1)}, bf16[2,128,128]{2,1,0:T(8,128)(2,1)S(1)}, u32[]{:S(2)}, u32[]{:S(2)}) collective-permute-start(bf16[2,128,128]{2,1,0:T(8,128)(2,1)S(1)} %get-tuple-element.41), channel_id=1, source_target_pairs={{0,4},{4,8},{8,12},{12,0},{1,5},{5,9},{9,13},{13,1},{2,6},{6,10},{... | collective-permute-start | bytes 196616 | tf_op jit(solution)/shard_map/ppermute | solution.py:103
  15.5 0.0 collective-permute-done.near0_ref
  15.5 0.0 collective-permute-done.2.near1_ref.label_ref
  15.5 0.7 %copy-done.7 = f32[128]{0:T(128)S(1)} copy-done((f32[128]{0:T(128)S(1)}, f32[128]{0:T(128)}, u32[]{:S(2)}) %copy-start.7) | copy-done | bytes 536
  16.2 4.9 %inside_windows.1 = (bf16[2,3,128,128]{3,2,1,0:T(8,128)(2,1)S(1)}, bf16[2,3,128,128]{3,2,1,0:T(8,128)(2,1)S(1)}) custom-call(bf16[3,128,128]{2,1,0:T(8,128)(2,1)S(1)} %collective-permute-done.near0_ref, bf16[3,128,128]{2,1,0:T(8,128)(2,1)S(1)} %get-tuple-element.27.own0_ref, bf16[400,128]{1,0:T(8,128)(2,1)S(1)} %collective-permute-done.2.near1_ref.label_ref, ...), custom_call_target="tpu_custom_call" | custom-call | flops 5500000256 | bytes 16500000 | tf_op jit(solution)/shard_map/inside_windows/pallas_call | solution.py:377
  21.1 2.3 %collective-permute-start.3 = (bf16[2,3,128,128]{3,2,1,0:T(8,128)(2,1)S(1)}, bf16[2,3,128,128]{3,2,1,0:T(8,128)(2,1)S(1)}, u32[]{:S(2)}, u32[]{:S(2)}) collective-permute-start(bf16[2,3,128,128]{3,2,1,0:T(8,128)(2,1)S(1)} %get-tuple-element.38), channel_id=1, source_target_pairs={{0,12},{4,0},{8,4},{12,8},{1,13},{5,1},{9,5},{13,9},{2,14},{6,2},{... | collective-permute-start | bytes 589832 | tf_op jit(solution)/shard_map/ppermute | solution.py:103
  23.4 0.0 collective-permute-done.5.near_ref
  23.4 2.3 %across_windows.1 = (bf16[2,64,128]{2,1,0:T(8,128)(2,1)S(1)}, bf16[2,64,128]{2,1,0:T(8,128)(2,1)S(1)}, bf16[2,64,128]{2,1,0:T(8,128)(2,1)S(1)}, bf16[2,64,128]{2,1,0:T(8,128)(2,1)S(1)}) custom-call(bf16[400,128]{1,0:T(8,128)(2,1)S(1)} %collective-permute-done.2.near1_ref.label_ref, bf16[2,128,128]{2,1,0:T(8,128)(2,1)S(1)} %collective-permute-done.5.near_ref, ...), custom_call_target="tpu_custom_call" | custom-call | flops 2529999872 | bytes 7589999 | tf_op jit(solution)/shard_map/across_windows/pallas_call | solution.py:377
  25.7 0.5 %collective-permute-start.6 = (bf16[2,64,128]{2,1,0:T(8,128)(2,1)S(1)}, bf16[2,64,128]{2,1,0:T(8,128)(2,1)S(1)}, u32[]{:S(2)}, u32[]{:S(2)}) collective-permute-start(bf16[2,64,128]{2,1,0:T(8,128)(2,1)S(1)} %get-tuple-element.44), channel_id=1, source_target_pairs={{0,12},{4,0},{8,4},{12,8},{1,13},{5,1},{9,5},{13,9},{2,14},{6,2},{... | collective-permute-start | bytes 98312 | tf_op jit(solution)/shard_map/ppermute | solution.py:103
  26.2 0.5 %collective-permute-start.7 = (bf16[2,64,128]{2,1,0:T(8,128)(2,1)S(1)}, bf16[2,64,128]{2,1,0:T(8,128)(2,1)S(1)}, u32[]{:S(2)}, u32[]{:S(2)}) collective-permute-start(bf16[2,64,128]{2,1,0:T(8,128)(2,1)S(1)} %get-tuple-element.45), channel_id=1, source_target_pairs={{0,2},{2,0},{1,3},{3,1},{4,6},{6,4},{5,7},{7,5},{8,10},{10,8},{9,1... | collective-permute-start | bytes 98312 | tf_op jit(solution)/shard_map/ppermute | solution.py:103
  26.7 1.6 %collective-permute-start.8 = (bf16[2,64,128]{2,1,0:T(8,128)(2,1)S(1)}, bf16[2,64,128]{2,1,0:T(8,128)(2,1)S(1)}, u32[]{:S(2)}, u32[]{:S(2)}) collective-permute-start(bf16[2,64,128]{2,1,0:T(8,128)(2,1)S(1)} %get-tuple-element.46), channel_id=1, source_target_pairs={{0,14},{2,12},{4,2},{6,0},{8,6},{10,4},{12,10},{14,8},{1,15},{3,13... | collective-permute-start | bytes 98312 | tf_op jit(solution)/shard_map/ppermute | solution.py:103
  28.3 1.3 %collective-permute-done.6.inner_back_ref = bf16[2,64,128]{2,1,0:T(8,128)(2,1)S(1)} collective-permute-done((bf16[2,64,128]{2,1,0:T(8,128)(2,1)S(1)}, bf16[2,64,128]{2,1,0:T(8,128)(2,1)S(1)}, u32[]{:S(2)}, u32[]{:S(2)}) %collective-permute-start.6) | collective-permute-done | bytes 32800 | tf_op jit(solution)/shard_map/ppermute | solution.py:103
  29.6 0.4 %collective-permute-done.7.border_own_ref = bf16[2,64,128]{2,1,0:T(8,128)(2,1)S(1)} collective-permute-done((bf16[2,64,128]{2,1,0:T(8,128)(2,1)S(1)}, bf16[2,64,128]{2,1,0:T(8,128)(2,1)S(1)}, u32[]{:S(2)}, u32[]{:S(2)}) %collective-permute-start.7) | collective-permute-done | bytes 32800 | tf_op jit(solution)/shard_map/ppermute | solution.py:103
  30.1 1.4 %collective-permute-done.8.border_back_ref = bf16[2,64,128]{2,1,0:T(8,128)(2,1)S(1)} collective-permute-done((bf16[2,64,128]{2,1,0:T(8,128)(2,1)S(1)}, bf16[2,64,128]{2,1,0:T(8,128)(2,1)S(1)}, u32[]{:S(2)}, u32[]{:S(2)}) %collective-permute-start.8) | collective-permute-done | bytes 32800 | tf_op jit(solution)/shard_map/ppermute | solution.py:103
  31.5 0.0 collective-permute-done.3.back_ref
  31.5 0.1 far_pieces.1
  31.6 0.1 collective-permute-start.9
  31.7 1.3 %collective-permute-done.9.low_ref = bf16[8,64,128]{2,1,0:T(8,128)(2,1)S(1)} collective-permute-done((bf16[8,64,128]{2,1,0:T(8,128)(2,1)S(1)}, bf16[8,64,128]{2,1,0:T(8,128)(2,1)S(1)}, u32[]{:S(2)}, u32[]{:S(2)}) %collective-permute-start.9) | collective-permute-done | bytes 131104 | tf_op jit(solution)/shard_map/ppermute | solution.py:103
  33.0 1.1 %last_pieces.1 = bf16[8,256,128]{2,1,0:T(8,128)(2,1)} custom-call(bf16[8,64,128]{2,1,0:T(8,128)(2,1)S(1)} %collective-permute-done.9.low_ref, bf16[2,3,128,128]{3,2,1,0:T(8,128)(2,1)S(1)} %get-tuple-element.37.kept_ref, bf16[2,3,128,128]{3,2,1,0:T(8,128)(2,1)S(1)} %collective-permute-done.3.back_ref, ...), custom_call_target="tpu_custom_call" | custom-call | flops 1100000000 | bytes 3300000 | tf_op jit(solution)/shard_map/last_pieces/pallas_call | solution.py:377
  (9 shorter events, 0.1 us)
Async XLA Ops:
  0.0 1.0 %copy-start = (bf16[8,32,8,128]{3,2,1,0:T(8,128)(2,1)S(1)}, bf16[8,32,8,128]{3,2,1,0:T(8,128)(2,1)}, u32[]{:S(2)}) copy-start(bf16[8,32,8,128]{3,2,1,0:T(8,128)(2,1)} %param.10) | copy-start | bytes 1572868
  1.0 3.3 %copy-start.8 = (s32[8,32,8]{1,2,0:T(8,128)S(1)}, s32[8,32,8]{1,2,0:T(8,128)}, u32[]{:S(2)}) copy-start(s32[8,32,8]{1,2,0:T(8,128)} %param.11) | copy-start | bytes 24580
  1.0 4.7 %copy-start.1 = (bf16[8,32,8,128]{3,2,1,0:T(8,128)(2,1)S(1)}, bf16[8,32,8,128]{3,2,1,0:T(8,128)(2,1)}, u32[]{:S(2)}) copy-start(bf16[8,32,8,128]{3,2,1,0:T(8,128)(2,1)} %param.10) | copy-start | bytes 1572868
  1.2 4.6 %collective-permute-start.1 = (bf16[8,64,128]{2,1,0:T(8,128)(2,1)S(1)}, bf16[8,64,128]{2,1,0:T(8,128)(2,1)S(1)}, u32[]{:S(2)}, u32[]{:S(2)}) collective-permute-start(bf16[8,64,128]{2,1,0:T(8,128)(2,1)S(1)} %get-tuple-element.28), channel_id=1, source_target_pairs={{0,1},{1,0},{2,3},{3,2},{4,5},{5,4},{6,7},{7,6},{8,9},{9,8},{10,11... | collective-permute-start | bytes 393224 | tf_op jit(solution)/shard_map/ppermute | solution.py:103
  1.7 13.8 %collective-permute-start = (bf16[3,128,128]{2,1,0:T(8,128)(2,1)S(1)}, bf16[3,128,128]{2,1,0:T(8,128)(2,1)S(1)}, u32[]{:S(2)}, u32[]{:S(2)}) collective-permute-start(bf16[3,128,128]{2,1,0:T(8,128)(2,1)S(1)} %get-tuple-element.26), channel_id=1, source_target_pairs={{0,4},{4,8},{8,12},{12,0},{1,5},{5,9},{9,13},{13,1},{2,6},{6,10},{... | collective-permute-start | bytes 294920 | tf_op jit(solution)/shard_map/ppermute | solution.py:103
  4.9 0.7 %copy-start.9 = (f32[1575,4]{0,1:T(4,128)S(1)}, f32[1575,4]{0,1:T(4,128)}, u32[]{:S(2)}) copy-start(f32[1575,4]{0,1:T(4,128)} %param.13) | copy-start | bytes 75604
  5.7 3.4 %copy-start.2 = (s32[256,256]{1,0:T(8,128)S(1)}, s32[256,256]{1,0:T(8,128)}, u32[]{:S(2)}) copy-start(s32[256,256]{1,0:T(8,128)} %index_ref.1) | copy-start | bytes 786436
  5.7 3.4 %copy-start.3 = (bf16[128,512]{1,0:T(8,128)(2,1)S(1)}, bf16[128,512]{1,0:T(8,128)(2,1)}, u32[]{:S(2)}) copy-start(bf16[128,512]{1,0:T(8,128)(2,1)} %w_up_ref.1) | copy-start | bytes 393220
  5.7 3.4 %copy-start.4 = (bf16[512,128]{1,0:T(8,128)(2,1)S(1)}, bf16[512,128]{1,0:T(8,128)(2,1)}, u32[]{:S(2)}) copy-start(bf16[512,128]{1,0:T(8,128)(2,1)} %w_down_ref.1) | copy-start | bytes 393220
  5.8 3.4 %copy-start.5 = (bf16[128,384]{1,0:T(8,128)(2,1)S(1)}, bf16[128,384]{1,0:T(8,128)(2,1)}, u32[]{:S(2)}) copy-start(bf16[128,384]{1,0:T(8,128)(2,1)} %w_qkv_ref.1) | copy-start | bytes 294916
  5.8 3.4 %copy-start.6 = (bf16[128,128]{1,0:T(8,128)(2,1)S(1)}, bf16[128,128]{1,0:T(8,128)(2,1)}, u32[]{:S(2)}) copy-start(bf16[128,128]{1,0:T(8,128)(2,1)} %w_proj_ref.1) | copy-start | bytes 98308
  6.0 7.9 %collective-permute-start.4 = (bf16[2,2,64,128]{3,2,1,0:T(8,128)(2,1)S(1)}, bf16[2,2,64,128]{3,2,1,0:T(8,128)(2,1)S(1)}, u32[]{:S(2)}, u32[]{:S(2)}) collective-permute-start(bf16[2,2,64,128]{3,2,1,0:T(8,128)(2,1)S(1)} %get-tuple-element.40), channel_id=1, source_target_pairs={{0,2},{2,0},{1,3},{3,1},{4,6},{6,4},{5,7},{7,5},{8,10},{10,8},{9,1... | collective-permute-start | bytes 196616 | tf_op jit(solution)/shard_map/ppermute | solution.py:103
  7.5 8.0 %collective-permute-start.2 = (bf16[400,128]{1,0:T(8,128)(2,1)S(1)}, bf16[400,128]{1,0:T(8,128)(2,1)S(1)}, u32[]{:S(2)}, u32[]{:S(2)}) collective-permute-start(bf16[400,128]{1,0:T(8,128)(2,1)S(1)} %get-tuple-element.29), channel_id=1, source_target_pairs={{0,4},{4,8},{8,12},{12,0},{1,5},{5,9},{9,13},{13,1},{2,6},{6,10},{... | collective-permute-start | bytes 307208 | tf_op jit(solution)/shard_map/ppermute | solution.py:103
  13.1 0.7 %copy-start.10 = (f32[128]{0:T(128)S(1)}, f32[128]{0:T(128)}, u32[]{:S(2)}) copy-start(f32[128]{0:T(128)} %param.17) | copy-start | bytes 1540
  13.9 9.5 %collective-permute-start.5 = (bf16[2,128,128]{2,1,0:T(8,128)(2,1)S(1)}, bf16[2,128,128]{2,1,0:T(8,128)(2,1)S(1)}, u32[]{:S(2)}, u32[]{:S(2)}) collective-permute-start(bf16[2,128,128]{2,1,0:T(8,128)(2,1)S(1)} %get-tuple-element.41), channel_id=1, source_target_pairs={{0,4},{4,8},{8,12},{12,0},{1,5},{5,9},{9,13},{13,1},{2,6},{6,10},{... | collective-permute-start | bytes 196616 | tf_op jit(solution)/shard_map/ppermute | solution.py:103
  15.5 0.7 %copy-start.7 = (f32[128]{0:T(128)S(1)}, f32[128]{0:T(128)}, u32[]{:S(2)}) copy-start(f32[128]{0:T(128)} %param.14) | copy-start | bytes 1540
  21.1 10.5 %collective-permute-start.3 = (bf16[2,3,128,128]{3,2,1,0:T(8,128)(2,1)S(1)}, bf16[2,3,128,128]{3,2,1,0:T(8,128)(2,1)S(1)}, u32[]{:S(2)}, u32[]{:S(2)}) collective-permute-start(bf16[2,3,128,128]{3,2,1,0:T(8,128)(2,1)S(1)} %get-tuple-element.38), channel_id=1, source_target_pairs={{0,12},{4,0},{8,4},{12,8},{1,13},{5,1},{9,5},{13,9},{2,14},{6,2},{... | collective-permute-start | bytes 589832 | tf_op jit(solution)/shard_map/ppermute | solution.py:103
  25.7 4.0 %collective-permute-start.6 = (bf16[2,64,128]{2,1,0:T(8,128)(2,1)S(1)}, bf16[2,64,128]{2,1,0:T(8,128)(2,1)S(1)}, u32[]{:S(2)}, u32[]{:S(2)}) collective-permute-start(bf16[2,64,128]{2,1,0:T(8,128)(2,1)S(1)} %get-tuple-element.44), channel_id=1, source_target_pairs={{0,12},{4,0},{8,4},{12,8},{1,13},{5,1},{9,5},{13,9},{2,14},{6,2},{... | collective-permute-start | bytes 98312 | tf_op jit(solution)/shard_map/ppermute | solution.py:103
  26.2 3.9 %collective-permute-start.7 = (bf16[2,64,128]{2,1,0:T(8,128)(2,1)S(1)}, bf16[2,64,128]{2,1,0:T(8,128)(2,1)S(1)}, u32[]{:S(2)}, u32[]{:S(2)}) collective-permute-start(bf16[2,64,128]{2,1,0:T(8,128)(2,1)S(1)} %get-tuple-element.45), channel_id=1, source_target_pairs={{0,2},{2,0},{1,3},{3,1},{4,6},{6,4},{5,7},{7,5},{8,10},{10,8},{9,1... | collective-permute-start | bytes 98312 | tf_op jit(solution)/shard_map/ppermute | solution.py:103
  26.7 4.8 %collective-permute-start.8 = (bf16[2,64,128]{2,1,0:T(8,128)(2,1)S(1)}, bf16[2,64,128]{2,1,0:T(8,128)(2,1)S(1)}, u32[]{:S(2)}, u32[]{:S(2)}) collective-permute-start(bf16[2,64,128]{2,1,0:T(8,128)(2,1)S(1)} %get-tuple-element.46), channel_id=1, source_target_pairs={{0,14},{2,12},{4,2},{6,0},{8,6},{10,4},{12,10},{14,8},{1,15},{3,13... | collective-permute-start | bytes 98312 | tf_op jit(solution)/shard_map/ppermute | solution.py:103
  31.6 1.4 %collective-permute-start.9 = (bf16[8,64,128]{2,1,0:T(8,128)(2,1)S(1)}, bf16[8,64,128]{2,1,0:T(8,128)(2,1)S(1)}, u32[]{:S(2)}, u32[]{:S(2)}) collective-permute-start(bf16[8,64,128]{2,1,0:T(8,128)(2,1)S(1)} %far_pieces.1), channel_id=1, source_target_pairs={{0,1},{1,0},{2,3},{3,2},{4,5},{5,4},{6,7},{7,6},{8,9},{9,8},{10,11... | collective-permute-start | bytes 393224 | tf_op jit(solution)/shard_map/ppermute | solution.py:103

commit v3 on v2

v3 whole, which is shorter than its diff:
```python
import math

import jax
import jax.numpy as jnp
from jax import lax
from jax.experimental import pallas as pl
from jax.experimental.pallas import tpu as pltpu
from jax.sharding import PartitionSpec as P

HEADS = 4
WX = 8
WY = 8
WZ = 4
SX = 4
SY = 4
SZ = 2
WTOK = WX * WY * WZ
LANES = 128
F32 = jnp.float32
BF16 = jnp.bfloat16
LOG2E = 1.4426950408889634


def reordered(value):
    run = SY * WZ
    blocks = [
        value[(x * 2 + side) * run : (x * 2 + side + 1) * run] for side in range(2) for x in range(WX)
    ]
    return jnp.concatenate(blocks, axis=0)


def prepare_kernel(
    index_ref, given_ref, w_qkv_ref, w_proj_ref, w_up_ref, w_down_ref, gain_attn_ref, gain_ref,
    bias_ref, gain_attn_out_ref, w_qv_t_ref, w_k_ref, w_proj_t_ref, w_up_t_ref, w_down_t_ref, gain_t_ref, table_ref,
):
    width = w_proj_ref.shape[0]
    w_qv_t_ref[:width] = w_qkv_ref[:, :width].T
    w_qv_t_ref[width:] = w_qkv_ref[:, 2 * width :].T
    w_k_ref[...] = w_qkv_ref[:, width : 2 * width]
    w_proj_t_ref[...] = w_proj_ref[...].T
    w_up_t_ref[...] = w_up_ref[...].T
    w_down_t_ref[...] = w_down_ref[...].T
    gain_attn_out_ref[...] = gain_attn_ref[...]
    gain_t_ref[...] = jnp.broadcast_to(gain_ref[...], (LANES, width)).T
    rows = given_ref.shape[1]
    table_ref[:, :rows] = given_ref[...]
    chunks = table_ref.shape[1] // LANES
    index = reordered(reordered(index_ref[...].astype(F32)).T).astype(jnp.int32)
    for column in range(0, WTOK, LANES):
        for row in range(0, WTOK, 8):
            part = index[row : row + 8, column : column + LANES]
            low = part & (LANES - 1)
            high = part >> 7
            found = [jnp.zeros((8, LANES), F32) for _ in range(HEADS)]
            for chunk in range(chunks):
                here = high == chunk
                for head in range(HEADS):
                    span = slice(chunk * LANES, (chunk + 1) * LANES)
                    line = jnp.broadcast_to(table_ref[head : head + 1, span], (8, LANES))
                    got = jnp.take_along_axis(line, low, axis=1, mode="promise_in_bounds")
                    found[head] = jnp.where(here, got, found[head])
            for head in range(HEADS):
                bias_ref[head, row : row + 8, column : column + LANES] = found[head] * LOG2E


def prepare(rel_index, table, w_qkv, w_proj, w_up, w_down, gain_attn, gain_mlp):
    width, hidden = w_up.shape
    shapes = [(2 * width, width), (width, width), (width, width), (hidden, width), (width, hidden)]
    return pl.pallas_call(
        prepare_kernel,
        out_shape=[jax.ShapeDtypeStruct((HEADS, WTOK, WTOK), F32), jax.ShapeDtypeStruct((1, width), F32)]
        + [jax.ShapeDtypeStruct(shape, BF16) for shape in shapes]
        + [jax.ShapeDtypeStruct((width, LANES), F32)],
        scratch_shapes=[pltpu.VMEM((HEADS, -(-table.shape[1] // LANES) * LANES), F32)],
        cost_estimate=cost(1),
        compiler_params=pltpu.CompilerParams(vmem_limit_bytes=32 << 20),
        name="bias_and_weights",
    )(rel_index, table, w_qkv, w_proj, w_up, w_down, gain_attn, gain_mlp)


def cost(micros):
    return pl.CostEstimate(
        flops=int(micros * 1.1e9), bytes_accessed=int(micros * 3.3e6), transcendentals=0
    )


def dot_nn(left, right):
    return lax.dot_general(left, right, (((1,), (0,)), ((), ())), preferred_element_type=F32)


def dot_nt(left, right):
    return lax.dot_general(left, right, (((1,), (1,)), ((), ())), preferred_element_type=F32)


def eye(size):
    rows = lax.broadcasted_iota(jnp.int32, (size, size), 0)
    columns = lax.broadcasted_iota(jnp.int32, (size, size), 1)
    return (rows == columns).astype(BF16)


def gelu(value):
    return 0.5 * value * (1.0 + lax.erf(value * (0.5**0.5)))


HALF = SX * WY * WZ
QUARTER = HALF // 2


def moved(value, axis, steps):
    names = (axis,) if isinstance(axis, str) else tuple(axis)
    moves = (steps,) if isinstance(axis, str) else tuple(steps)
    counts = [lax.axis_size(name) for name in names]
    pairs = []
    for source in range(math.prod(counts)):
        left, target, stride = source, 0, 1
        for count, move in zip(reversed(counts), reversed(moves)):
            target += (left % count + move) % count * stride
            left //= count
            stride *= count
        pairs.append((source, target))
    return lax.ppermute(value, names, pairs)


def turned(value, steps):
    return pltpu.roll(value, steps % 8, axis=1)


def sublane(shape):
    return lax.broadcasted_iota(jnp.int32, shape, 1)


def pair_core(tall):
    number = tall.shape[0]
    split = tall.reshape(number // 2, 2, 8, LANES)
    first, second = split[:, 0], split[:, 1]
    return jnp.where(sublane(first.shape) < 4, turned(first, -2), turned(second, 2))


def quad_low(tall):
    number = tall.shape[0]
    split = tall.reshape(number // 4, 4, 8, LANES)
    at = sublane((number // 4, 8, LANES))
    low = jnp.where(at < 2, split[:, 0], turned(split[:, 1], 2))
    high = jnp.where(at < 6, turned(split[:, 2], 4), turned(split[:, 3], 6))
    return jnp.where(at < 4, low, high)


def pair_edge(tall, quads):
    number = tall.shape[0]
    split = tall.reshape(number // 4, 4, 8, LANES)
    at = sublane(quads.shape)
    even = jnp.where(
        at < 4,
        jnp.where(at < 2, turned(split[:, 0], 2), turned(quads, 2)),
        jnp.where(at < 6, turned(split[:, 1], -2), turned(quads, 4)),
    )
    odd = jnp.where(
        at < 4,
        jnp.where(at < 2, turned(split[:, 2], 2), turned(quads, -2)),
        jnp.where(at < 6, turned(split[:, 3], -2), quads),
    )
    return jnp.stack([even, odd], axis=1).reshape(number // 2, 8, LANES)


def unpair_edge(pairs):
    number = pairs.shape[0]
    split = pairs.reshape(number // 2, 2, 8, LANES)
    first, second = split[:, 0], split[:, 1]
    at = sublane(first.shape)
    near = jnp.where(
        at < 4,
        jnp.where(at < 2, first, turned(first, -2)),
        jnp.where(at < 6, turned(second, 4), turned(second, 2)),
    )
    far = jnp.where(
        at < 4,
        jnp.where(at < 2, turned(first, -2), turned(first, 4)),
        jnp.where(at < 6, turned(second, 2), second),
    )
    return near, far


def join_tall(low, core, near):
    number = low.shape[0]
    split = core.reshape(number, 2, 8, LANES)
    at = sublane(low.shape)
    parts = []
    for y in range(4):
        bottom = turned(low, -2 * y)
        top = turned(near, 6 - 2 * y)
        middle = turned(split[:, y // 2], 2 - 4 * (y % 2))
        parts.append(jnp.where(at < 2, bottom, jnp.where(at < 6, middle, top)))
    return jnp.stack(parts, axis=1).reshape(number * 4, 8, LANES)


def tall_of(ref, x_from, y_from, y_to, size_z=8):
    part = ref[x_from : x_from + SX, y_from * size_z : y_to * size_z, :]
    return part.astype(F32).reshape(-1, 8, LANES)


def rows_of(groups, *lead):
    return groups.reshape(*lead, -1, LANES).astype(BF16)


def as_groups(ref_value):
    return ref_value.astype(F32).reshape(-1, 8, LANES)


def low_kernel(tokens_ref, low_ref):
    size_y = low_ref.shape[1] // SZ
    for x_from in (0, SX):
        low = quad_low(tall_of(tokens_ref, x_from, 0, size_y))
        low_ref[x_from : x_from + SX] = rows_of(low, SX)


def shifted_kernel(tokens_ref, low_ref, region_ref, send_ref, own_ref, send_y_ref, own_y_ref):
    windows = own_ref.shape[0]
    size_y = low_ref.shape[1] // SZ

    def core(x_from, start):
        return rows_of(pair_core(tall_of(tokens_ref, x_from, start, start + SY)))

    def edge(x_from, start):
        return rows_of(
            pair_edge(
                tall_of(tokens_ref, x_from, start, start + SY),
                tall_of(low_ref, x_from, start, start + SY, SZ),
            )
        )

    for at in range(windows):
        piece = (core, edge)[at % 2]
        for side in range(2):
            start = SY + at // 2 * WY + side * SY
            row = at * HALF + side * QUARTER
            send_ref[row : row + QUARTER] = piece(SX, start)
            own_ref[at, side * QUARTER : (side + 1) * QUARTER] = piece(0, start)
    for strip, start in enumerate((0, size_y - SY)):
        for half, x_from in enumerate((SX, 0)):
            for layer, piece in enumerate((core, edge)):
                row = ((strip * 2 + half) * 2 + layer) * QUARTER
                rows = piece(x_from, start)
                send_y_ref[row : row + QUARTER] = rows
                own_y_ref[row : row + QUARTER] = rows
    labels = region_ref[...].astype(F32).reshape(-1, size_y)
    blank = jnp.zeros((labels.shape[0], LANES - size_y), F32)
    labels = jnp.concatenate([labels, blank], axis=1).astype(BF16)
    send_ref[windows * HALF :] = labels
    send_y_ref[8 * QUARTER :] = labels


def across_pieces_kernel(own_ref, got_ref, send_ref):
    strip = 2 * QUARTER
    send_ref[:strip] = own_ref[2 * strip : 3 * strip]
    send_ref[strip : 2 * strip] = got_ref[:strip]
    send_ref[2 * strip : 3 * strip] = got_ref[2 * strip : 3 * strip]
    send_ref[3 * strip : 4 * strip] = own_ref[:strip]
    send_ref[4 * strip :] = got_ref[4 * strip :]


def windows_after(x16s, labels, spans, bias_ref, weights, ahead=4):
    gain_attn, w_qv_t, w_k, w_proj_t, w_up_t, w_down_t, gain_mlp = weights
    width = x16s[0].shape[1]
    size = width // HEADS
    scale = size**-0.5 * LOG2E
    eye_window = eye(WTOK)
    eye_width = eye(width)
    gain_mlp = jnp.concatenate([gain_mlp[...]] * (WTOK // LANES), axis=1)
    states = []
    for x16, (column, row), span in zip(x16s, labels, spans):
        x = x16.astype(F32)
        center = x - jnp.mean(x, axis=1, keepdims=True)
        spread = jnp.mean(center * center, axis=1, keepdims=True)
        normed = (center * lax.rsqrt(spread + 1e-05) * gain_attn[...]).astype(BF16)
        x_t = dot_nt(eye_width, x16[span])
        if span == slice(0, WTOK):
            qv_t = dot_nt(w_qv_t[...], normed).astype(BF16)
            q_t, v_t = qv_t[:width], qv_t[width:]
        else:
            q_t = dot_nt(w_qv_t[:width], normed[span]).astype(BF16)
            v_t = dot_nt(w_qv_t[width:], normed).astype(BF16)
        k = dot_nn(normed, w_k[...]).astype(BF16)
        fade = jnp.where(column[:, span] == row[:, span], 0.0, -1e9 * LOG2E)
        states.append((x_t, q_t, v_t, k, fade, span))
    tasks = [(at, head) for at in range(len(states)) for head in range(HEADS)]

    def scores(task):
        at, head = task
        _, q_t, _, k, _, _ = states[at]
        pieces = [jnp.zeros((size, q_t.shape[1]), BF16)] * HEADS
        pieces[head] = q_t[head * size : (head + 1) * size]
        return dot_nn(k, jnp.concatenate(pieces, axis=0))

    def attend(task, raw):
        at, head = task
        _, _, v_t, _, fade, span = states[at]
        score = raw * scale + bias_ref[head, :, span] + fade
        weight = jnp.exp2(score - jnp.max(score, axis=0, keepdims=True))
        total = jnp.sum(weight, axis=0, keepdims=True)
        part = dot_nn(v_t[head * size : (head + 1) * size], weight.astype(BF16))
        return (part * (1.0 / total)).astype(BF16)

    raws, parts = {}, {}
    for at in range(min(ahead, len(tasks))):
        raws[at] = scores(tasks[at])
    for at, task in enumerate(tasks):
        if at + ahead < len(tasks):
            raws[at + ahead] = scores(tasks[at + ahead])
        parts[task] = attend(task, raws.pop(at))
    attended = [
        jnp.concatenate([parts[at, head] for head in range(HEADS)], axis=0)
        for at in range(len(states))
    ]
    residual = [state[0] for state in states]
    joined = WTOK // residual[0].shape[1]
    if joined > 1:
        group = lambda values: [
            jnp.concatenate(values[at : at + joined], axis=1) for at in range(0, len(values), joined)
        ]
        attended, residual = group(attended), group(residual)
    middles = [
        (x_t + dot_nn(w_proj_t[...], value)).astype(BF16).astype(F32)
        for x_t, value in zip(residual, attended)
    ]
    normeds = []
    for middle in middles:
        center = middle - jnp.mean(middle, axis=0, keepdims=True)
        spread = jnp.mean(center * center, axis=0, keepdims=True)
        normeds.append((center * lax.rsqrt(spread + 1e-05) * gain_mlp).astype(BF16))
    hiddens = [dot_nn(w_up_t[...], normed) for normed in normeds]
    hiddens = [gelu(hidden).astype(BF16) for hidden in hiddens]
    afters = [
        (middle + dot_nn(w_down_t[...], hidden)).astype(BF16)
        for middle, hidden in zip(middles, hiddens)
    ]
    return [dot_nt(eye_window, after).astype(BF16) for after in afters]


def window_labels(region, number):
    at = lax.broadcasted_iota(jnp.int32, (WTOK, region.shape[0]), 0)
    line = lax.broadcasted_iota(jnp.int32, (WTOK, region.shape[0]), 1)
    wanted = (at % HALF) // (SY * WZ) * 8 + (number % 2) * WZ + at % WZ
    lines = dot_nn((line == wanted).astype(BF16), region)
    at = lax.broadcasted_iota(jnp.int32, lines.shape, 0)
    y = lax.broadcasted_iota(jnp.int32, lines.shape, 1)
    wanted = number // 2 * WY + at // HALF * SY + at // WZ % SY
    lone = jnp.where(y == wanted, lines, 0.0).astype(BF16)
    ones = jnp.ones((WTOK, lines.shape[1]), BF16)
    return dot_nt(lone, ones), dot_nt(ones[:8], lone)[:1]


def quarters(rows, start):
    at = start * QUARTER
    return rows[at : at + QUARTER]


def inside_kernel(near_ref, own_ref, bias_ref, *rest):
    weights, (back_ref, kept_ref) = rest[:7], rest[7:]
    windows = own_ref.shape[0]
    region = near_ref[windows * HALF :]
    x16s = []
    for at in range(windows):
        near, own = near_ref[at * HALF : (at + 1) * HALF], own_ref[at]
        x16s.append(
            jnp.concatenate([near[:QUARTER], own[:QUARTER], near[QUARTER:], own[QUARTER:]], axis=0)
        )
    labels = [window_labels(region, at) for at in range(windows)]
    afters = windows_after(x16s, labels, [slice(0, WTOK)] * windows, bias_ref, weights)
    for at, after in enumerate(afters):
        for side in range(2):
            back_ref[at % 2, at // 2, side] = quarters(after, 2 * side)
            kept_ref[at % 2, at // 2, side] = quarters(after, 2 * side + 1)


def across_kernel(inside_ref, near_ref, own_ref, got_ref, bias_ref, *rest):
    weights, (back_ref, kept_ref) = rest[:7], rest[7:]
    size = near_ref.shape[0] - 8 * QUARTER
    windows = (inside_ref.shape[0] - size) // HALF
    x16s, labels, spans = [], [], []
    for place in range(2):
        region = (inside_ref[windows * HALF :], near_ref[8 * QUARTER :])[place]
        for layer in range(2):
            near = [quarters(near_ref, 4 * place + 2 * side + layer) for side in range(2)]
            if place == 0:
                own = [quarters(own_ref, 6 + layer), quarters(got_ref, 2 + layer)]
            else:
                own = [quarters(got_ref, 6 + layer), quarters(own_ref, 2 + layer)]
            x16s.append(jnp.concatenate([near[0], own[0], near[1], own[1]], axis=0))
            labels.append(window_labels(region, windows + layer))
            spans.append(slice(place * HALF, (place + 1) * HALF))
    afters = windows_after(x16s, labels, spans, bias_ref, weights)
    for place, after in enumerate(afters):
        for layer in range(2):
            back_ref[layer, place] = quarters(after, 2 * layer)
            kept_ref[layer, place] = quarters(after, 2 * layer + 1)


def strips(size_y, inside_ref, across_ref):
    blocks = inside_ref.shape[1]
    for block in range(blocks):
        for side in range(2):
            yield SY + block * WY + side * SY, [inside_ref[layer, block, side] for layer in range(2)]
    yield size_y - SY, [across_ref[layer, 0] for layer in range(2)]
    yield 0, [across_ref[layer, 1] for layer in range(2)]


def far_kernel(kept_ref, back_ref, kept_across_ref, back_across_ref, out_ref):
    size_y = out_ref.shape[1] // SZ
    for x_from, inside_ref, across_ref in (
        (0, kept_ref, kept_across_ref),
        (SX, back_ref, back_across_ref),
    ):
        for start, (_, edge) in strips(size_y, inside_ref, across_ref):
            far = unpair_edge(as_groups(edge))[1]
            out_ref[x_from : x_from + SX, start * SZ : (start + SY) * SZ] = rows_of(far, SX)


def last_kernel(low_ref, kept_ref, back_ref, kept_across_ref, back_across_ref, out_ref):
    size_y = low_ref.shape[1] // SZ
    size_z = 8
    for x_from, inside_ref, across_ref in (
        (0, kept_ref, kept_across_ref),
        (SX, back_ref, back_across_ref),
    ):
        for start, (core, edge) in strips(size_y, inside_ref, across_ref):
            low = tall_of(low_ref, x_from, start, start + SY, SZ)
            near = unpair_edge(as_groups(edge))[0]
            tall = join_tall(low, as_groups(core), near)
            out_ref[x_from : x_from + SX, start * size_z : (start + SY) * size_z] = rows_of(tall, SX)


def kernel_call(kernel, name, micros, outs, *operands):
    return pl.pallas_call(
        kernel,
        out_shape=[jax.ShapeDtypeStruct(shape, BF16) for shape in outs],
        cost_estimate=cost(micros),
        compiler_params=pltpu.CompilerParams(vmem_limit_bytes=48 << 20),
        name=name,
    )(*operands)


def per_device(
    tokens, region, rel_index, bias_table, gain_attn, w_qkv, w_proj, gain_mlp, w_up, w_down
):
    size_x, size_y, size_z, width = tokens.shape
    windows = 2 * (size_y // WY - 1)
    lines = size_x * size_z
    flat = tokens.reshape(size_x, size_y * size_z, width)
    low = kernel_call(low_kernel, "low_pieces", 0.2, [(size_x, size_y * SZ, width)], flat)[0]
    low = moved(low, "gz", -1)
    sent, own, strip, own_strip = kernel_call(
        shifted_kernel,
        "shifted_pieces",
        0.3,
        [
            (windows * HALF + lines, width),
            (windows, HALF, width),
            (8 * QUARTER + lines, width),
            (8 * QUARTER, width),
        ],
        flat,
        low,
        region.transpose(0, 2, 1),
    )
    near = moved(sent, "gx", 1)
    if lax.axis_size("gy") == 2:
        got = moved(strip, "gy", 1)
    else:
        got = jnp.concatenate(
            [moved(strip[: 4 * QUARTER], "gy", -1), moved(strip[4 * QUARTER :], "gy", 1)]
        )
    fixed = prepare(
        rel_index, bias_table.T, w_qkv, w_proj, w_up, w_down, gain_attn[None], gain_mlp[None]
    )
    sent_across = kernel_call(
        across_pieces_kernel, "across_pieces", 0.2, [(8 * QUARTER + lines, width)], own_strip, got
    )[0]
    near_across = moved(sent_across, "gx", 1)
    halves = (2, windows // 2, 2, QUARTER, width)
    back, kept = kernel_call(
        inside_kernel, "inside_windows", 15, [halves, halves], near, own, *fixed
    )
    back = moved(back, "gx", -1)
    halves = (2, 2, QUARTER, width)
    back_across, kept_across = kernel_call(
        across_kernel, "across_windows", 2.3, [halves, halves], near, near_across, own_strip, got, *fixed
    )
    back_across = moved(back_across, "gx", -1)
    after = (kept, back, kept_across, back_across)
    far = kernel_call(far_kernel, "far_pieces", 0.1, [(size_x, size_y * SZ, width)], *after)[0]
    far = moved(far, "gz", 1)
    out = kernel_call(last_kernel, "last_pieces", 1, [flat.shape], far, *after)[0]
    return out.reshape(tokens.shape)


def solution(mesh):
    field = P(("cand", "gx"), "gy", "gz", None)
    placed = (field, P(("cand", "gx"), "gy", "gz")) + (P(),) * 8
    return jax.shard_map(
        per_device, mesh=mesh, in_specs=placed, out_specs=field, check_vma=False
    )
```

time: 34.3 us -> 30.9 us (0.901)
  starting transfers between devices: 12.9 us -> 9.49 us
  local copies, waits for them, and re-layouts: 3.83 us -> 1.7 us
  waiting for transfers between devices: 4.55 us -> 6.15 us
  Pallas kernels: 12.6 us -> 13.3 us
    ppermute x10 -> x7, starting transfers between devices: 12.9 us -> 9.49 us  [moved(): return lax.ppermute(value, names, pairs)]
    ppermute x10 -> x7, waiting for transfers between devices: 4.55 us -> 6.15 us  [moved(): return lax.ppermute(value, names, pairs)]
    unnamed x22 -> x20, local copies, waits for them, and re-layouts: 2.94 us -> 1.7 us
    convert_element_type x3 -> x0, local copies, waits for them, and re-layouts: 0.75 us -> none  [per_device(): labels = labels.reshape(-1, LANES).astype(BF16)]
    pallas_call x7, Pallas kernels: 8.65 us -> 9.3 us  [kernel_call(): pl.pallas_call(kernel, out_shape=[jax.ShapeDtypeStruct(shape, BF16) for s...]
  transfers between devices with their start and end apart: 10 -> 7, of which waited for: 4 -> 3; matrix products, arithmetic and copies ran while one was open for 3% -> 0% of each run, Pallas kernels for 33% -> 38%
where the time goes in v3:
time: 30.9 us; the launch traced here: 30.7 us
  Pallas kernels  13.3 us (43%)
  starting transfers between devices  9.49 us (31%)
  waiting for transfers between devices  6.15 us (20%)
  local copies, waits for them, and re-layouts  1.7 us (6%)
    ppermute x7, starting transfers between devices, moved(): return lax.ppermute(value, names, pairs)  9.49 us
    pallas_call x7, Pallas kernels, kernel_call(): pl.pallas_call(kernel, out_shape=[jax.ShapeDtypeStruct(shape, BF16) for s...  9.3 us
    ppermute x7, waiting for transfers between devices, moved(): return lax.ppermute(value, names, pairs)  6.15 us
    pallas_call x1, Pallas kernels, prepare(): pl.pallas_call(prepare_kernel, out_shape=[jax.ShapeDtypeStruct((HEADS, WT...  3.97 us
    unnamed x20, local copies, waits for them, and re-layouts  1.7 us
  transfers between devices with their start and end apart: 7, of which 3 were waited for; matrix products, arithmetic and copies ran while one was open for 0% of the time, Pallas kernels for 38%

profile of v3, /device:TPU:0, one launch (start us, length us, event | category | flops | bytes accessed | tf_op | source)
XLA Modules:
  0.0 30.7 jit_solution(10591576879172300804)
XLA Ops:
  0.0 0.0 copy-start
  0.0 1.0 %copy-done = bf16[8,32,8,128]{3,2,1,0:T(8,128)(2,1)S(1)} copy-done((bf16[8,32,8,128]{3,2,1,0:T(8,128)(2,1)S(1)}, bf16[8,32,8,128]{3,2,1,0:T(8,128)(2,1)}, u32[]{:S(2)}) %copy-start) | copy-done | bytes 524312
  1.0 0.0 copy-start.5
  1.0 0.1 low_pieces.1
  1.1 0.5 %collective-permute-start = (bf16[8,64,128]{2,1,0:T(8,128)(2,1)S(1)}, bf16[8,64,128]{2,1,0:T(8,128)(2,1)S(1)}, u32[]{:S(2)}, u32[]{:S(2)}) collective-permute-start(bf16[8,64,128]{2,1,0:T(8,128)(2,1)S(1)} %low_pieces.1), channel_id=1, source_target_pairs={{0,1},{1,0},{2,3},{3,2},{4,5},{5,4},{6,7},{7,6},{8,9},{9,8},{10,11... | collective-permute-start | bytes 393224 | tf_op jit(solution)/shard_map/ppermute | solution.py:121
  1.7 1.0 %collective-permute-done.low_ref = bf16[8,64,128]{2,1,0:T(8,128)(2,1)S(1)} collective-permute-done((bf16[8,64,128]{2,1,0:T(8,128)(2,1)S(1)}, bf16[8,64,128]{2,1,0:T(8,128)(2,1)S(1)}, u32[]{:S(2)}, u32[]{:S(2)}) %collective-permute-start) | collective-permute-done | bytes 131104 | tf_op jit(solution)/shard_map/ppermute | solution.py:121
  2.6 0.0 copy-done.5
  2.6 0.0 copy-start.1
  2.7 0.0 copy-start.2
  2.7 0.0 copy-start.3
  2.7 0.0 copy-start.4
  2.7 0.0 copy-start.6
  2.7 0.0 copy-start.7
  2.7 0.2 shifted_pieces.1
  2.9 3.0 %collective-permute-start.1 = (bf16[832,128]{1,0:T(8,128)(2,1)S(1)}, bf16[832,128]{1,0:T(8,128)(2,1)S(1)}, u32[]{:S(2)}, u32[]{:S(2)}) collective-permute-start(bf16[832,128]{1,0:T(8,128)(2,1)S(1)} %get-tuple-element.21), channel_id=1, source_target_pairs={{0,4},{4,8},{8,12},{12,0},{1,5},{5,9},{9,13},{13,1},{2,6},{6,10},{... | collective-permute-start | bytes 638984 | tf_op jit(solution)/shard_map/ppermute | solution.py:121
  5.9 1.5 %collective-permute-start.3 = (bf16[576,128]{1,0:T(8,128)(2,1)S(1)}, bf16[576,128]{1,0:T(8,128)(2,1)S(1)}, u32[]{:S(2)}, u32[]{:S(2)}) collective-permute-start(bf16[576,128]{1,0:T(8,128)(2,1)S(1)} %get-tuple-element.34), channel_id=1, source_target_pairs={{0,2},{2,0},{1,3},{3,1},{4,6},{6,4},{5,7},{7,5},{8,10},{10,8},{9,1... | collective-permute-start | bytes 442376 | tf_op jit(solution)/shard_map/ppermute | solution.py:121
  7.4 0.0 copy-start.8
  7.4 0.0 copy-start.9
  7.4 0.0 copy-done.1
  7.4 0.0 copy-done.2
  7.4 0.0 copy-done.3
  7.5 0.0 copy-done.4
  7.5 0.0 copy-done.6
  7.5 0.0 copy-done.7
  7.5 0.6 %copy-done.8 = f32[128]{0:T(128)S(1)} copy-done((f32[128]{0:T(128)S(1)}, f32[128]{0:T(128)}, u32[]{:S(2)}) %copy-start.8) | copy-done | bytes 536
  8.1 0.0 copy-done.9
  8.1 4.0 %bias_and_weights.1 = (f32[4,256,256]{2,1,0:T(8,128)S(1)}, f32[1,128]{1,0:T(1,128)S(1)}, bf16[256,128]{1,0:T(8,128)(2,1)S(1)}, bf16[128,128]{1,0:T(8,128)(2,1)S(...) custom-call(s32[256,256]{1,0:T(8,128)S(1)} %copy-done.1, ...), custom_call_target="tpu_custom_call" | custom-call | flops 1100000000 | bytes 3300000 | tf_op jit(solution)/shard_map/bias_and_weights/pallas_call | solution.py:69
  12.1 0.0 collective-permute-done.3.got_ref
  12.1 1.6 %collective-permute-start.4 = (bf16[576,128]{1,0:T(8,128)(2,1)S(1)}, bf16[576,128]{1,0:T(8,128)(2,1)S(1)}, u32[]{:S(2)}, u32[]{:S(2)}) collective-permute-start(bf16[576,128]{1,0:T(8,128)(2,1)S(1)} %across_pieces.1), channel_id=1, source_target_pairs={{0,4},{4,8},{8,12},{12,0},{1,5},{5,9},{9,13},{13,1},{2,6},{6,10},{... | collective-permute-start | bytes 442376 | tf_op jit(solution)/shard_map/ppermute | solution.py:121
  13.7 0.0 collective-permute-done.1.near_ref.inside_ref
  13.7 4.9 %inside_windows.1 = (bf16[2,3,2,64,128]{4,3,2,1,0:T(8,128)(2,1)S(1)}, bf16[2,3,2,64,128]{4,3,2,1,0:T(8,128)(2,1)S(1)}) custom-call(bf16[832,128]{1,0:T(8,128)(2,1)S(1)} %collective-permute-done.1.near_ref.inside_ref, bf16[6,128,128]{2,1,0:T(8,128)(2,1)S(1)} %get-tuple-element.22.own_ref, f32[4,256,256]{2,1,0:T(8,128)S(1)} %get-tuple-element.23.bias_ref, ...), custom_call_target="tpu_custom_call" | custom-call | flops 16499999744 | bytes 49500000 | tf_op jit(solution)/shard_map/inside_windows/pallas_call | solution.py:433
  18.7 2.3 %collective-permute-start.2 = (bf16[2,3,2,64,128]{4,3,2,1,0:T(8,128)(2,1)S(1)}, bf16[2,3,2,64,128]{4,3,2,1,0:T(8,128)(2,1)S(1)}, u32[]{:S(2)}, u32[]{:S(2)}) collective-permute-start(bf16[2,3,2,64,128]{4,3,2,1,0:T(8,128)(2,1)S(1)} %get-tuple-element.32), channel_id=1, source_target_pairs={{0,12},{4,0},{8,4},{12,8},{1,13},{5,1},{9,5},{13,9},{2,14},{6,2},{... | collective-permute-start | bytes 589832 | tf_op jit(solution)/shard_map/ppermute | solution.py:121
  21.0 0.0 collective-permute-done.4.near_ref
  21.0 2.9 %across_windows.1 = (bf16[2,2,64,128]{3,2,1,0:T(8,128)(2,1)S(1)}, bf16[2,2,64,128]{3,2,1,0:T(8,128)(2,1)S(1)}) custom-call(bf16[832,128]{1,0:T(8,128)(2,1)S(1)} %collective-permute-done.1.near_ref.inside_ref, bf16[576,128]{1,0:T(8,128)(2,1)S(1)} %collective-permute-done.4.near_ref, bf16[512,128]{1,0:T(8,128)(2,1)S(1)} %get-tuple-element.33.own_ref, ...), custom_call_target="tpu_custom_call" | custom-call | flops 2529999872 | bytes 7589999 | tf_op jit(solution)/shard_map/across_windows/pallas_call | solution.py:433
  23.8 0.5 %collective-permute-start.5 = (bf16[2,2,64,128]{3,2,1,0:T(8,128)(2,1)S(1)}, bf16[2,2,64,128]{3,2,1,0:T(8,128)(2,1)S(1)}, u32[]{:S(2)}, u32[]{:S(2)}) collective-permute-start(bf16[2,2,64,128]{3,2,1,0:T(8,128)(2,1)S(1)} %get-tuple-element.36), channel_id=1, source_target_pairs={{0,12},{4,0},{8,4},{12,8},{1,13},{5,1},{9,5},{13,9},{2,14},{6,2},{... | collective-permute-start | bytes 196616 | tf_op jit(solution)/shard_map/ppermute | solution.py:121
  24.3 3.8 %collective-permute-done.5.back_across_ref = bf16[2,2,64,128]{3,2,1,0:T(8,128)(2,1)S(1)} collective-permute-done((bf16[2,2,64,128]{3,2,1,0:T(8,128)(2,1)S(1)}, bf16[2,2,64,128]{3,2,1,0:T(8,128)(2,1)S(1)}, u32[]{:S(2)}, u32[]{:S(2)}) %collective-permute-start.5) | collective-permute-done | bytes 65568 | tf_op jit(solution)/shard_map/ppermute | solution.py:121
  28.2 0.0 collective-permute-done.2.back_ref
  28.2 0.1 far_pieces.1
  28.3 0.1 collective-permute-start.6
  28.3 1.3 %collective-permute-done.6.low_ref = bf16[8,64,128]{2,1,0:T(8,128)(2,1)S(1)} collective-permute-done((bf16[8,64,128]{2,1,0:T(8,128)(2,1)S(1)}, bf16[8,64,128]{2,1,0:T(8,128)(2,1)S(1)}, u32[]{:S(2)}, u32[]{:S(2)}) %collective-permute-start.6) | collective-permute-done | bytes 131104 | tf_op jit(solution)/shard_map/ppermute | solution.py:121
  29.7 1.1 %last_pieces.1 = bf16[8,256,128]{2,1,0:T(8,128)(2,1)} custom-call(bf16[8,64,128]{2,1,0:T(8,128)(2,1)S(1)} %collective-permute-done.6.low_ref, bf16[2,3,2,64,128]{4,3,2,1,0:T(8,128)(2,1)S(1)} %get-tuple-element.31.kept_ref, bf16[2,3,2,64,128]{4,3,2,1,0:T(8,128)(2,1)S(1)} %collective-permute-done.2.back_ref, ...), custom_call_target="tpu_custom_call" | custom-call | flops 1100000000 | bytes 3300000 | tf_op jit(solution)/shard_map/last_pieces/pallas_call | solution.py:433
  (1 shorter events, 0.0 us)
Async XLA Ops:
  0.0 1.0 %copy-start = (bf16[8,32,8,128]{3,2,1,0:T(8,128)(2,1)S(1)}, bf16[8,32,8,128]{3,2,1,0:T(8,128)(2,1)}, u32[]{:S(2)}) copy-start(bf16[8,32,8,128]{3,2,1,0:T(8,128)(2,1)} %param.10) | copy-start | bytes 1572868
  1.0 1.6 %copy-start.5 = (s32[8,32,8]{1,2,0:T(8,128)S(1)}, s32[8,32,8]{1,2,0:T(8,128)}, u32[]{:S(2)}) copy-start(s32[8,32,8]{1,2,0:T(8,128)} %param.11) | copy-start | bytes 24580
  1.1 1.5 %collective-permute-start = (bf16[8,64,128]{2,1,0:T(8,128)(2,1)S(1)}, bf16[8,64,128]{2,1,0:T(8,128)(2,1)S(1)}, u32[]{:S(2)}, u32[]{:S(2)}) collective-permute-start(bf16[8,64,128]{2,1,0:T(8,128)(2,1)S(1)} %low_pieces.1), channel_id=1, source_target_pairs={{0,1},{1,0},{2,3},{3,2},{4,5},{5,4},{6,7},{7,6},{8,9},{9,8},{10,11... | collective-permute-start | bytes 393224 | tf_op jit(solution)/shard_map/ppermute | solution.py:121
  2.6 4.8 %copy-start.1 = (s32[256,256]{1,0:T(8,128)S(1)}, s32[256,256]{1,0:T(8,128)}, u32[]{:S(2)}) copy-start(s32[256,256]{1,0:T(8,128)} %index_ref.1) | copy-start | bytes 786436
  2.7 4.8 %copy-start.2 = (bf16[128,512]{1,0:T(8,128)(2,1)S(1)}, bf16[128,512]{1,0:T(8,128)(2,1)}, u32[]{:S(2)}) copy-start(bf16[128,512]{1,0:T(8,128)(2,1)} %w_up_ref.1) | copy-start | bytes 393220
  2.7 4.8 %copy-start.3 = (bf16[512,128]{1,0:T(8,128)(2,1)S(1)}, bf16[512,128]{1,0:T(8,128)(2,1)}, u32[]{:S(2)}) copy-start(bf16[512,128]{1,0:T(8,128)(2,1)} %w_down_ref.1) | copy-start | bytes 393220
  2.7 4.8 %copy-start.4 = (bf16[128,384]{1,0:T(8,128)(2,1)S(1)}, bf16[128,384]{1,0:T(8,128)(2,1)}, u32[]{:S(2)}) copy-start(bf16[128,384]{1,0:T(8,128)(2,1)} %w_qkv_ref.1) | copy-start | bytes 294916
  2.7 4.8 %copy-start.6 = (bf16[128,128]{1,0:T(8,128)(2,1)S(1)}, bf16[128,128]{1,0:T(8,128)(2,1)}, u32[]{:S(2)}) copy-start(bf16[128,128]{1,0:T(8,128)(2,1)} %w_proj_ref.1) | copy-start | bytes 98308
  2.7 4.8 %copy-start.7 = (f32[1575,4]{0,1:T(4,128)S(1)}, f32[1575,4]{0,1:T(4,128)}, u32[]{:S(2)}) copy-start(f32[1575,4]{0,1:T(4,128)} %param.13) | copy-start | bytes 75604
  2.9 10.8 %collective-permute-start.1 = (bf16[832,128]{1,0:T(8,128)(2,1)S(1)}, bf16[832,128]{1,0:T(8,128)(2,1)S(1)}, u32[]{:S(2)}, u32[]{:S(2)}) collective-permute-start(bf16[832,128]{1,0:T(8,128)(2,1)S(1)} %get-tuple-element.21), channel_id=1, source_target_pairs={{0,4},{4,8},{8,12},{12,0},{1,5},{5,9},{9,13},{13,1},{2,6},{6,10},{... | collective-permute-start | bytes 638984 | tf_op jit(solution)/shard_map/ppermute | solution.py:121
  5.9 6.1 %collective-permute-start.3 = (bf16[576,128]{1,0:T(8,128)(2,1)S(1)}, bf16[576,128]{1,0:T(8,128)(2,1)S(1)}, u32[]{:S(2)}, u32[]{:S(2)}) collective-permute-start(bf16[576,128]{1,0:T(8,128)(2,1)S(1)} %get-tuple-element.34), channel_id=1, source_target_pairs={{0,2},{2,0},{1,3},{3,1},{4,6},{6,4},{5,7},{7,5},{8,10},{10,8},{9,1... | collective-permute-start | bytes 442376 | tf_op jit(solution)/shard_map/ppermute | solution.py:121
  7.4 0.7 %copy-start.8 = (f32[128]{0:T(128)S(1)}, f32[128]{0:T(128)}, u32[]{:S(2)}) copy-start(f32[128]{0:T(128)} %param.14) | copy-start | bytes 1540
  7.4 0.7 %copy-start.9 = (f32[128]{0:T(128)S(1)}, f32[128]{0:T(128)}, u32[]{:S(2)}) copy-start(f32[128]{0:T(128)} %param.17) | copy-start | bytes 1540
  12.1 8.9 %collective-permute-start.4 = (bf16[576,128]{1,0:T(8,128)(2,1)S(1)}, bf16[576,128]{1,0:T(8,128)(2,1)S(1)}, u32[]{:S(2)}, u32[]{:S(2)}) collective-permute-start(bf16[576,128]{1,0:T(8,128)(2,1)S(1)} %across_pieces.1), channel_id=1, source_target_pairs={{0,4},{4,8},{8,12},{12,0},{1,5},{5,9},{9,13},{13,1},{2,6},{6,10},{... | collective-permute-start | bytes 442376 | tf_op jit(solution)/shard_map/ppermute | solution.py:121
  18.7 9.5 %collective-permute-start.2 = (bf16[2,3,2,64,128]{4,3,2,1,0:T(8,128)(2,1)S(1)}, bf16[2,3,2,64,128]{4,3,2,1,0:T(8,128)(2,1)S(1)}, u32[]{:S(2)}, u32[]{:S(2)}) collective-permute-start(bf16[2,3,2,64,128]{4,3,2,1,0:T(8,128)(2,1)S(1)} %get-tuple-element.32), channel_id=1, source_target_pairs={{0,12},{4,0},{8,4},{12,8},{1,13},{5,1},{9,5},{13,9},{2,14},{6,2},{... | collective-permute-start | bytes 589832 | tf_op jit(solution)/shard_map/ppermute | solution.py:121
  23.8 4.3 %collective-permute-start.5 = (bf16[2,2,64,128]{3,2,1,0:T(8,128)(2,1)S(1)}, bf16[2,2,64,128]{3,2,1,0:T(8,128)(2,1)S(1)}, u32[]{:S(2)}, u32[]{:S(2)}) collective-permute-start(bf16[2,2,64,128]{3,2,1,0:T(8,128)(2,1)S(1)} %get-tuple-element.36), channel_id=1, source_target_pairs={{0,12},{4,0},{8,4},{12,8},{1,13},{5,1},{9,5},{13,9},{2,14},{6,2},{... | collective-permute-start | bytes 196616 | tf_op jit(solution)/shard_map/ppermute | solution.py:121
  28.3 1.4 %collective-permute-start.6 = (bf16[8,64,128]{2,1,0:T(8,128)(2,1)S(1)}, bf16[8,64,128]{2,1,0:T(8,128)(2,1)S(1)}, u32[]{:S(2)}, u32[]{:S(2)}) collective-permute-start(bf16[8,64,128]{2,1,0:T(8,128)(2,1)S(1)} %far_pieces.1), channel_id=1, source_target_pairs={{0,1},{1,0},{2,3},{3,2},{4,5},{5,4},{6,7},{7,6},{8,9},{9,8},{10,11... | collective-permute-start | bytes 393224 | tf_op jit(solution)/shard_map/ppermute | solution.py:121

commit v4 on v3

--- a/solution.py
+++ b/solution.py
@@ -29,9 +29,9 @@
     return jnp.concatenate(blocks, axis=0)
 
 
-def prepare_kernel(
-    index_ref, given_ref, w_qkv_ref, w_proj_ref, w_up_ref, w_down_ref, gain_attn_ref, gain_ref,
-    bias_ref, gain_attn_out_ref, w_qv_t_ref, w_k_ref, w_proj_t_ref, w_up_t_ref, w_down_t_ref, gain_t_ref, table_ref,
+def weights_kernel(
+    _, w_qkv_ref, w_proj_ref, w_up_ref, w_down_ref, gain_attn_ref, gain_ref,
+    gain_attn_out_ref, w_qv_t_ref, w_k_ref, w_proj_t_ref, w_up_t_ref, w_down_t_ref, gain_t_ref,
 ):
     width = w_proj_ref.shape[0]
     w_qv_t_ref[:width] = w_qkv_ref[:, :width].T
@@ -42,6 +42,9 @@
     w_down_t_ref[...] = w_down_ref[...].T
     gain_attn_out_ref[...] = gain_attn_ref[...]
     gain_t_ref[...] = jnp.broadcast_to(gain_ref[...], (LANES, width)).T
+
+
+def bias_kernel(index_ref, given_ref, bias_ref, table_ref):
     rows = given_ref.shape[1]
     table_ref[:, :rows] = given_ref[...]
     chunks = table_ref.shape[1] // LANES
@@ -65,17 +68,26 @@
 
 def prepare(rel_index, table, w_qkv, w_proj, w_up, w_down, gain_attn, gain_mlp):
     width, hidden = w_up.shape
-    shapes = [(2 * width, width), (width, width), (width, width), (hidden, width), (width, hidden)]
-    return pl.pallas_call(
-        prepare_kernel,
-        out_shape=[jax.ShapeDtypeStruct((HEADS, WTOK, WTOK), F32), jax.ShapeDtypeStruct((1, width), F32)]
-        + [jax.ShapeDtypeStruct(shape, BF16) for shape in shapes]
-        + [jax.ShapeDtypeStruct((width, LANES), F32)],
+    bias = pl.pallas_call(
+        bias_kernel,
+        out_shape=jax.ShapeDtypeStruct((HEADS, WTOK, WTOK), F32),
         scratch_shapes=[pltpu.VMEM((HEADS, -(-table.shape[1] // LANES) * LANES), F32)],
         cost_estimate=cost(1),
         compiler_params=pltpu.CompilerParams(vmem_limit_bytes=32 << 20),
-        name="bias_and_weights",
-    )(rel_index, table, w_qkv, w_proj, w_up, w_down, gain_attn, gain_mlp)
+        name="gather_bias",
+    )(rel_index, table)
+    shapes = [(2 * width, width), (width, width), (width, width), (hidden, width), (width, hidden)]
+    others = pl.pallas_call(
+        weights_kernel,
+        in_specs=[pl.BlockSpec(memory_space=pl.ANY)] + [pl.BlockSpec(memory_space=pltpu.VMEM)] * 6,
+        out_shape=[jax.ShapeDtypeStruct((1, width), F32)]
+        + [jax.ShapeDtypeStruct(shape, BF16) for shape in shapes]
+        + [jax.ShapeDtypeStruct((width, LANES), F32)],
+        cost_estimate=cost(0.3),
+        compiler_params=pltpu.CompilerParams(vmem_limit_bytes=32 << 20),
+        name="turn_weights",
+    )(bias, w_qkv, w_proj, w_up, w_down, gain_attn, gain_mlp)
+    return bias, *others
 
 
 def cost(micros):
@@ -213,7 +225,10 @@
         low_ref[x_from : x_from + SX] = rows_of(low, SX)
 
 
-def shifted_kernel(tokens_ref, low_ref, region_ref, send_ref, own_ref, send_y_ref, own_y_ref):
+def shifted_kernel(
+    tokens_ref, low_ref, region_ref, given_ref, send_ref, own_ref, send_y_ref, own_y_ref, table_ref
+):
+    table_ref[...] = given_ref[...]
     windows = own_ref.shape[0]
     size_y = low_ref.shape[1] // SZ
 
@@ -280,21 +295,24 @@
             q_t = dot_nt(w_qv_t[:width], normed[span]).astype(BF16)
             v_t = dot_nt(w_qv_t[width:], normed).astype(BF16)
         k = dot_nn(normed, w_k[...]).astype(BF16)
-        fade = jnp.where(column[:, span] == row[:, span], 0.0, -1e9 * LOG2E)
+        lane = lax.broadcasted_iota(jnp.int32, column.shape, 1).astype(F32)
+        k = jnp.concatenate([k, jnp.where(column == lane, 1.0, 0.0).astype(BF16)], axis=1)
+        line = lax.broadcasted_iota(jnp.int32, (LANES, q_t.shape[1]), 0).astype(F32)
+        fade = jnp.where(row[:, span] == line, 0.0, -1e10).astype(BF16)
         states.append((x_t, q_t, v_t, k, fade, span))
     tasks = [(at, head) for at in range(len(states)) for head in range(HEADS)]
 
     def scores(task):
         at, head = task
-        _, q_t, _, k, _, _ = states[at]
+        _, q_t, _, k, fade, _ = states[at]
         pieces = [jnp.zeros((size, q_t.shape[1]), BF16)] * HEADS
         pieces[head] = q_t[head * size : (head + 1) * size]
-        return dot_nn(k, jnp.concatenate(pieces, axis=0))
+        return dot_nn(k, jnp.concatenate(pieces + [fade], axis=0))
 
     def attend(task, raw):
         at, head = task
-        _, _, v_t, _, fade, span = states[at]
-        score = raw * scale + bias_ref[head, :, span] + fade
+        _, _, v_t, _, _, span = states[at]
+        score = raw * scale + bias_ref[head, :, span]
         weight = jnp.exp2(score - jnp.max(score, axis=0, keepdims=True))
         total = jnp.sum(weight, axis=0, keepdims=True)
         part = dot_nn(v_t[head * size : (head + 1) * size], weight.astype(BF16))
@@ -345,7 +363,7 @@
     y = lax.broadcasted_iota(jnp.int32, lines.shape, 1)
     wanted = number // 2 * WY + at // HALF * SY + at // WZ % SY
     lone = jnp.where(y == wanted, lines, 0.0).astype(BF16)
-    ones = jnp.ones((WTOK, lines.shape[1]), BF16)
+    ones = jnp.ones((LANES, lines.shape[1]), BF16)
     return dot_nt(lone, ones), dot_nt(ones[:8], lone)[:1]
 
 
@@ -388,7 +406,7 @@
             x16s.append(jnp.concatenate([near[0], own[0], near[1], own[1]], axis=0))
             labels.append(window_labels(region, windows + layer))
             spans.append(slice(place * HALF, (place + 1) * HALF))
-    afters = windows_after(x16s, labels, spans, bias_ref, weights)
+    afters = windows_after(x16s, labels, spans, bias_ref, weights, ahead=8)
     for place, after in enumerate(afters):
         for layer in range(2):
             back_ref[layer, place] = quarters(after, 2 * layer)
@@ -415,24 +433,50 @@
             out_ref[x_from : x_from + SX, start * SZ : (start + SY) * SZ] = rows_of(far, SX)
 
 
-def last_kernel(low_ref, kept_ref, back_ref, kept_across_ref, back_across_ref, out_ref):
+def last_kernel(
+    low_ref, kept_ref, back_ref, kept_across_ref, back_across_ref, out_ref, block_ref, sent
+):
     size_y = low_ref.shape[1] // SZ
     size_z = 8
+    moves = []
     for x_from, inside_ref, across_ref in (
         (0, kept_ref, kept_across_ref),
         (SX, back_ref, back_across_ref),
     ):
+        planes = slice(x_from, x_from + SX)
         for start, (core, edge) in strips(size_y, inside_ref, across_ref):
             low = tall_of(low_ref, x_from, start, start + SY, SZ)
             near = unpair_edge(as_groups(edge))[0]
             tall = join_tall(low, as_groups(core), near)
-            out_ref[x_from : x_from + SX, start * size_z : (start + SY) * size_z] = rows_of(tall, SX)
+            block_ref[planes, start * size_z : (start + SY) * size_z] = rows_of(tall, SX)
+        move = pltpu.make_async_copy(
+            block_ref.at[planes], out_ref.at[planes], sent.at[len(moves)]
+        )
+        move.start()
+        moves.append(move)
+    for move in moves:
+        move.wait()
+
+
+def last_call(low, after, shape):
+    return pl.pallas_call(
+        last_kernel,
+        in_specs=[pl.BlockSpec(memory_space=pltpu.VMEM)] * 5,
+        out_specs=pl.BlockSpec(memory_space=pl.ANY),
+        out_shape=jax.ShapeDtypeStruct(shape, BF16),
+        scratch_shapes=[pltpu.VMEM(shape, BF16), pltpu.SemaphoreType.DMA((2,))],
+        cost_estimate=cost(1),
+        compiler_params=pltpu.CompilerParams(vmem_limit_bytes=48 << 20),
+        name="last_pieces",
+    )(low, *after)
 
 
 def kernel_call(kernel, name, micros, outs, *operands):
     return pl.pallas_call(
         kernel,
-        out_shape=[jax.ShapeDtypeStruct(shape, BF16) for shape in outs],
+        out_shape=[
+            shape if hasattr(shape, "dtype") else jax.ShapeDtypeStruct(shape, BF16) for shape in outs
+        ],
         cost_estimate=cost(micros),
         compiler_params=pltpu.CompilerParams(vmem_limit_bytes=48 << 20),
         name=name,
@@ -448,7 +492,7 @@
     flat = tokens.reshape(size_x, size_y * size_z, width)
     low = kernel_call(low_kernel, "low_pieces", 0.2, [(size_x, size_y * SZ, width)], flat)[0]
     low = moved(low, "gz", -1)
-    sent, own, strip, own_strip = kernel_call(
+    sent, own, strip, own_strip, table = kernel_call(
         shifted_kernel,
         "shifted_pieces",
         0.3,
@@ -457,10 +501,12 @@
             (windows, HALF, width),
             (8 * QUARTER + lines, width),
             (8 * QUARTER, width),
+            jax.ShapeDtypeStruct(bias_table.shape[::-1], F32),
         ],
         flat,
         low,
         region.transpose(0, 2, 1),
+        bias_table.T,
     )
     near = moved(sent, "gx", 1)
     if lax.axis_size("gy") == 2:
@@ -470,7 +516,7 @@
             [moved(strip[: 4 * QUARTER], "gy", -1), moved(strip[4 * QUARTER :], "gy", 1)]
         )
     fixed = prepare(
-        rel_index, bias_table.T, w_qkv, w_proj, w_up, w_down, gain_attn[None], gain_mlp[None]
+        rel_index, table, w_qkv, w_proj, w_up, w_down, gain_attn[None], gain_mlp[None]
     )
     sent_across = kernel_call(
         across_pieces_kernel, "across_pieces", 0.2, [(8 * QUARTER + lines, width)], own_strip, got
@@ -489,8 +535,7 @@
     after = (kept, back, kept_across, back_across)
     far = kernel_call(far_kernel, "far_pieces", 0.1, [(size_x, size_y * SZ, width)], *after)[0]
     far = moved(far, "gz", 1)
-    out = kernel_call(last_kernel, "last_pieces", 1, [flat.shape], far, *after)[0]
-    return out.reshape(tokens.shape)
+    return last_call(far, after, flat.shape).reshape(tokens.shape)
 
 
 def solution(mesh):

time: 30.9 us -> 30.3 us (0.981)
  Pallas kernels: 13.3 us -> 12.7 us
    pallas_call x8 -> x9, Pallas kernels: 13.3 us -> 12.7 us  [the longest x6 7.71 us: kernel_call(): pl.pallas_call(kernel, out_shape=[shape if hasattr(shape, 'dtype') else j...]
  transfers between devices with their start and end apart: 7 -> 7, of which waited for: 3 -> 3; matrix products, arithmetic and copies ran while one was open for 0% -> 0% of each run, Pallas kernels for 38% -> 37%
where the time goes in v4:
time: 30.3 us; the launch traced here: 30.2 us
  Pallas kernels  12.7 us (42%)
  starting transfers between devices  9.5 us (31%)
  waiting for transfers between devices  6.14 us (20%)
  local copies, waits for them, and re-layouts  1.69 us (6%)
    ppermute x7, starting transfers between devices, moved(): return lax.ppermute(value, names, pairs)  9.5 us
    pallas_call x6, Pallas kernels, kernel_call(): pl.pallas_call(kernel, out_shape=[shape if hasattr(shape, 'dtype') else j...  7.71 us
    ppermute x7, waiting for transfers between devices, moved(): return lax.ppermute(value, names, pairs)  6.14 us
    pallas_call x1, Pallas kernels, prepare(): pl.pallas_call(bias_kernel, out_shape=jax.ShapeDtypeStruct((HEADS, WTOK,...  3.86 us
    unnamed x20, local copies, waits for them, and re-layouts  1.69 us
    pallas_call x1, Pallas kernels, last_call(): pl.pallas_call(last_kernel, in_specs=[pl.BlockSpec(memory_space=pltpu.VME...  0.98 us
  transfers between devices with their start and end apart: 7, of which 3 were waited for; matrix products, arithmetic and copies ran while one was open for 0% of the time, Pallas kernels for 37%

profile of v4, /device:TPU:0, one launch (start us, length us, event | category | flops | bytes accessed | tf_op | source)
XLA Modules:
  0.0 30.2 jit_solution(13214456598088804341)
XLA Ops:
  0.0 0.0 copy-start.6
  0.0 1.0 %copy-done.6 = bf16[8,32,8,128]{3,2,1,0:T(8,128)(2,1)S(1)} copy-done((bf16[8,32,8,128]{3,2,1,0:T(8,128)(2,1)S(1)}, bf16[8,32,8,128]{3,2,1,0:T(8,128)(2,1)}, u32[]{:S(2)}) %copy-start.6) | copy-done | bytes 524312
  1.0 0.0 copy-start.8
  1.0 0.0 copy-start.9
  1.0 0.1 low_pieces.1
  1.1 0.5 %collective-permute-start = (bf16[8,64,128]{2,1,0:T(8,128)(2,1)S(1)}, bf16[8,64,128]{2,1,0:T(8,128)(2,1)S(1)}, u32[]{:S(2)}, u32[]{:S(2)}) collective-permute-start(bf16[8,64,128]{2,1,0:T(8,128)(2,1)S(1)} %low_pieces.1), channel_id=1, source_target_pairs={{0,1},{1,0},{2,3},{3,2},{4,5},{5,4},{6,7},{7,6},{8,9},{9,8},{10,11... | collective-permute-start | bytes 393224 | tf_op jit(solution)/shard_map/ppermute | solution.py:133
  1.7 1.0 %collective-permute-done.low_ref = bf16[8,64,128]{2,1,0:T(8,128)(2,1)S(1)} collective-permute-done((bf16[8,64,128]{2,1,0:T(8,128)(2,1)S(1)}, bf16[8,64,128]{2,1,0:T(8,128)(2,1)S(1)}, u32[]{:S(2)}, u32[]{:S(2)}) %collective-permute-start) | collective-permute-done | bytes 131104 | tf_op jit(solution)/shard_map/ppermute | solution.py:133
  2.6 0.0 copy-done.8
  2.7 0.0 copy-done.9
  2.7 0.0 copy-start.7
  2.7 0.2 shifted_pieces.1
  2.9 3.0 %collective-permute-start.1 = (bf16[832,128]{1,0:T(8,128)(2,1)S(1)}, bf16[832,128]{1,0:T(8,128)(2,1)S(1)}, u32[]{:S(2)}, u32[]{:S(2)}) collective-permute-start(bf16[832,128]{1,0:T(8,128)(2,1)S(1)} %get-tuple-element.21), channel_id=1, source_target_pairs={{0,4},{4,8},{8,12},{12,0},{1,5},{5,9},{9,13},{13,1},{2,6},{6,10},{... | collective-permute-start | bytes 638984 | tf_op jit(solution)/shard_map/ppermute | solution.py:133
  5.9 1.5 %collective-permute-start.3 = (bf16[576,128]{1,0:T(8,128)(2,1)S(1)}, bf16[576,128]{1,0:T(8,128)(2,1)S(1)}, u32[]{:S(2)}, u32[]{:S(2)}) collective-permute-start(bf16[576,128]{1,0:T(8,128)(2,1)S(1)} %get-tuple-element.34), channel_id=1, source_target_pairs={{0,2},{2,0},{1,3},{3,1},{4,6},{6,4},{5,7},{7,5},{8,10},{10,8},{9,1... | collective-permute-start | bytes 442376 | tf_op jit(solution)/shard_map/ppermute | solution.py:133
  7.4 0.0 copy-done.7
  7.4 0.0 copy-start
  7.4 0.0 copy-start.1
  7.4 0.0 copy-start.2
  7.4 0.0 copy-start.3
  7.4 3.9 %gather_bias.1._.bias_ref = f32[4,256,256]{2,1,0:T(8,128)S(1)} custom-call(s32[256,256]{1,0:T(8,128)S(1)} %copy-done.7, f32[4,1575]{1,0:T(4,128)S(1)} %get-tuple-element.23.given_ref), custom_call_target="tpu_custom_call" | custom-call | flops 1100000000 | bytes 3300000 | tf_op jit(solution)/shard_map/gather_bias/pallas_call | solution.py:71
  11.3 0.0 copy-start.4
  11.3 0.0 copy-start.5
  11.3 0.0 copy-done
  11.3 0.0 copy-done.1
  11.3 0.0 copy-done.2
  11.3 0.0 copy-done.3
  11.3 0.6 %copy-done.4 = f32[128]{0:T(128)S(1)} copy-done((f32[128]{0:T(128)S(1)}, f32[128]{0:T(128)}, u32[]{:S(2)}) %copy-start.4) | copy-done | bytes 536
  11.9 0.0 copy-done.5
  11.9 0.2 turn_weights.1
  12.1 0.0 collective-permute-done.3.got_ref
  12.1 1.6 %collective-permute-start.4 = (bf16[576,128]{1,0:T(8,128)(2,1)S(1)}, bf16[576,128]{1,0:T(8,128)(2,1)S(1)}, u32[]{:S(2)}, u32[]{:S(2)}) collective-permute-start(bf16[576,128]{1,0:T(8,128)(2,1)S(1)} %across_pieces.1), channel_id=1, source_target_pairs={{0,4},{4,8},{8,12},{12,0},{1,5},{5,9},{9,13},{13,1},{2,6},{6,10},{... | collective-permute-start | bytes 442376 | tf_op jit(solution)/shard_map/ppermute | solution.py:133
  13.8 0.0 collective-permute-done.1.near_ref.inside_ref
  13.8 4.5 %inside_windows.1 = (bf16[2,3,2,64,128]{4,3,2,1,0:T(8,128)(2,1)S(1)}, bf16[2,3,2,64,128]{4,3,2,1,0:T(8,128)(2,1)S(1)}) custom-call(bf16[832,128]{1,0:T(8,128)(2,1)S(1)} %collective-permute-done.1.near_ref.inside_ref, bf16[6,128,128]{2,1,0:T(8,128)(2,1)S(1)} %get-tuple-element.22.own_ref, f32[4,256,256]{2,1,0:T(8,128)S(1)} %gather_bias.1._.bias_ref, ...), custom_call_target="tpu_custom_call" | custom-call | flops 16499999744 | bytes 49500000 | tf_op jit(solution)/shard_map/inside_windows/pallas_call | solution.py:475
  18.2 2.3 %collective-permute-start.2 = (bf16[2,3,2,64,128]{4,3,2,1,0:T(8,128)(2,1)S(1)}, bf16[2,3,2,64,128]{4,3,2,1,0:T(8,128)(2,1)S(1)}, u32[]{:S(2)}, u32[]{:S(2)}) collective-permute-start(bf16[2,3,2,64,128]{4,3,2,1,0:T(8,128)(2,1)S(1)} %get-tuple-element.32), channel_id=1, source_target_pairs={{0,12},{4,0},{8,4},{12,8},{1,13},{5,1},{9,5},{13,9},{2,14},{6,2},{... | collective-permute-start | bytes 589832 | tf_op jit(solution)/shard_map/ppermute | solution.py:133
  20.5 0.0 collective-permute-done.4.near_ref
  20.5 2.8 %across_windows.1 = (bf16[2,2,64,128]{3,2,1,0:T(8,128)(2,1)S(1)}, bf16[2,2,64,128]{3,2,1,0:T(8,128)(2,1)S(1)}) custom-call(bf16[832,128]{1,0:T(8,128)(2,1)S(1)} %collective-permute-done.1.near_ref.inside_ref, bf16[576,128]{1,0:T(8,128)(2,1)S(1)} %collective-permute-done.4.near_ref, bf16[512,128]{1,0:T(8,128)(2,1)S(1)} %get-tuple-element.33.own_ref, ...), custom_call_target="tpu_custom_call" | custom-call | flops 2529999872 | bytes 7589999 | tf_op jit(solution)/shard_map/across_windows/pallas_call | solution.py:475
  23.4 0.5 %collective-permute-start.5 = (bf16[2,2,64,128]{3,2,1,0:T(8,128)(2,1)S(1)}, bf16[2,2,64,128]{3,2,1,0:T(8,128)(2,1)S(1)}, u32[]{:S(2)}, u32[]{:S(2)}) collective-permute-start(bf16[2,2,64,128]{3,2,1,0:T(8,128)(2,1)S(1)} %get-tuple-element.36), channel_id=1, source_target_pairs={{0,12},{4,0},{8,4},{12,8},{1,13},{5,1},{9,5},{13,9},{2,14},{6,2},{... | collective-permute-start | bytes 196616 | tf_op jit(solution)/shard_map/ppermute | solution.py:133
  23.9 3.8 %collective-permute-done.5.back_across_ref = bf16[2,2,64,128]{3,2,1,0:T(8,128)(2,1)S(1)} collective-permute-done((bf16[2,2,64,128]{3,2,1,0:T(8,128)(2,1)S(1)}, bf16[2,2,64,128]{3,2,1,0:T(8,128)(2,1)S(1)}, u32[]{:S(2)}, u32[]{:S(2)}) %collective-permute-start.5) | collective-permute-done | bytes 65568 | tf_op jit(solution)/shard_map/ppermute | solution.py:133
  27.7 0.0 collective-permute-done.2.back_ref
  27.7 0.1 far_pieces.1
  27.8 0.1 collective-permute-start.6
  27.9 1.3 %collective-permute-done.6.low_ref = bf16[8,64,128]{2,1,0:T(8,128)(2,1)S(1)} collective-permute-done((bf16[8,64,128]{2,1,0:T(8,128)(2,1)S(1)}, bf16[8,64,128]{2,1,0:T(8,128)(2,1)S(1)}, u32[]{:S(2)}, u32[]{:S(2)}) %collective-permute-start.6) | collective-permute-done | bytes 131104 | tf_op jit(solution)/shard_map/ppermute | solution.py:133
  29.2 1.0 %last_pieces.1 = bf16[8,256,128]{2,1,0:T(8,128)(2,1)} custom-call(bf16[8,64,128]{2,1,0:T(8,128)(2,1)S(1)} %collective-permute-done.6.low_ref, bf16[2,3,2,64,128]{4,3,2,1,0:T(8,128)(2,1)S(1)} %get-tuple-element.31.kept_ref, bf16[2,3,2,64,128]{4,3,2,1,0:T(8,128)(2,1)S(1)} %collective-permute-done.2.back_ref, ...), custom_call_target="tpu_custom_call" | custom-call | flops 1100000000 | bytes 3300000 | tf_op jit(solution)/shard_map/last_pieces/pallas_call | solution.py:462
  (1 shorter events, 0.0 us)
Async XLA Ops:
  0.0 1.0 %copy-start.6 = (bf16[8,32,8,128]{3,2,1,0:T(8,128)(2,1)S(1)}, bf16[8,32,8,128]{3,2,1,0:T(8,128)(2,1)}, u32[]{:S(2)}) copy-start(bf16[8,32,8,128]{3,2,1,0:T(8,128)(2,1)} %param.10) | copy-start | bytes 1572868
  1.0 1.6 %copy-start.8 = (s32[8,32,8]{1,2,0:T(8,128)S(1)}, s32[8,32,8]{1,2,0:T(8,128)}, u32[]{:S(2)}) copy-start(s32[8,32,8]{1,2,0:T(8,128)} %param.11) | copy-start | bytes 24580
  1.0 1.6 %copy-start.9 = (f32[1575,4]{0,1:T(4,128)S(1)}, f32[1575,4]{0,1:T(4,128)}, u32[]{:S(2)}) copy-start(f32[1575,4]{0,1:T(4,128)} %param.13) | copy-start | bytes 75604
  1.1 1.5 %collective-permute-start = (bf16[8,64,128]{2,1,0:T(8,128)(2,1)S(1)}, bf16[8,64,128]{2,1,0:T(8,128)(2,1)S(1)}, u32[]{:S(2)}, u32[]{:S(2)}) collective-permute-start(bf16[8,64,128]{2,1,0:T(8,128)(2,1)S(1)} %low_pieces.1), channel_id=1, source_target_pairs={{0,1},{1,0},{2,3},{3,2},{4,5},{5,4},{6,7},{7,6},{8,9},{9,8},{10,11... | collective-permute-start | bytes 393224 | tf_op jit(solution)/shard_map/ppermute | solution.py:133
  2.7 4.7 %copy-start.7 = (s32[256,256]{1,0:T(8,128)S(1)}, s32[256,256]{1,0:T(8,128)}, u32[]{:S(2)}) copy-start(s32[256,256]{1,0:T(8,128)} %index_ref.1) | copy-start | bytes 786436
  2.9 10.9 %collective-permute-start.1 = (bf16[832,128]{1,0:T(8,128)(2,1)S(1)}, bf16[832,128]{1,0:T(8,128)(2,1)S(1)}, u32[]{:S(2)}, u32[]{:S(2)}) collective-permute-start(bf16[832,128]{1,0:T(8,128)(2,1)S(1)} %get-tuple-element.21), channel_id=1, source_target_pairs={{0,4},{4,8},{8,12},{12,0},{1,5},{5,9},{9,13},{13,1},{2,6},{6,10},{... | collective-permute-start | bytes 638984 | tf_op jit(solution)/shard_map/ppermute | solution.py:133
  5.9 6.2 %collective-permute-start.3 = (bf16[576,128]{1,0:T(8,128)(2,1)S(1)}, bf16[576,128]{1,0:T(8,128)(2,1)S(1)}, u32[]{:S(2)}, u32[]{:S(2)}) collective-permute-start(bf16[576,128]{1,0:T(8,128)(2,1)S(1)} %get-tuple-element.34), channel_id=1, source_target_pairs={{0,2},{2,0},{1,3},{3,1},{4,6},{6,4},{5,7},{7,5},{8,10},{10,8},{9,1... | collective-permute-start | bytes 442376 | tf_op jit(solution)/shard_map/ppermute | solution.py:133
  7.4 3.9 %copy-start = (bf16[128,512]{1,0:T(8,128)(2,1)S(1)}, bf16[128,512]{1,0:T(8,128)(2,1)}, u32[]{:S(2)}) copy-start(bf16[128,512]{1,0:T(8,128)(2,1)} %w_up_ref.1) | copy-start | bytes 393220
  7.4 3.9 %copy-start.1 = (bf16[512,128]{1,0:T(8,128)(2,1)S(1)}, bf16[512,128]{1,0:T(8,128)(2,1)}, u32[]{:S(2)}) copy-start(bf16[512,128]{1,0:T(8,128)(2,1)} %w_down_ref.1) | copy-start | bytes 393220
  7.4 3.9 %copy-start.2 = (bf16[128,384]{1,0:T(8,128)(2,1)S(1)}, bf16[128,384]{1,0:T(8,128)(2,1)}, u32[]{:S(2)}) copy-start(bf16[128,384]{1,0:T(8,128)(2,1)} %w_qkv_ref.1) | copy-start | bytes 294916
  7.4 3.9 %copy-start.3 = (bf16[128,128]{1,0:T(8,128)(2,1)S(1)}, bf16[128,128]{1,0:T(8,128)(2,1)}, u32[]{:S(2)}) copy-start(bf16[128,128]{1,0:T(8,128)(2,1)} %w_proj_ref.1) | copy-start | bytes 98308
  11.3 0.7 %copy-start.4 = (f32[128]{0:T(128)S(1)}, f32[128]{0:T(128)}, u32[]{:S(2)}) copy-start(f32[128]{0:T(128)} %param.14) | copy-start | bytes 1540
  11.3 0.7 %copy-start.5 = (f32[128]{0:T(128)S(1)}, f32[128]{0:T(128)}, u32[]{:S(2)}) copy-start(f32[128]{0:T(128)} %param.17) | copy-start | bytes 1540
  12.1 8.4 %collective-permute-start.4 = (bf16[576,128]{1,0:T(8,128)(2,1)S(1)}, bf16[576,128]{1,0:T(8,128)(2,1)S(1)}, u32[]{:S(2)}, u32[]{:S(2)}) collective-permute-start(bf16[576,128]{1,0:T(8,128)(2,1)S(1)} %across_pieces.1), channel_id=1, source_target_pairs={{0,4},{4,8},{8,12},{12,0},{1,5},{5,9},{9,13},{13,1},{2,6},{6,10},{... | collective-permute-start | bytes 442376 | tf_op jit(solution)/shard_map/ppermute | solution.py:133
  18.2 9.4 %collective-permute-start.2 = (bf16[2,3,2,64,128]{4,3,2,1,0:T(8,128)(2,1)S(1)}, bf16[2,3,2,64,128]{4,3,2,1,0:T(8,128)(2,1)S(1)}, u32[]{:S(2)}, u32[]{:S(2)}) collective-permute-start(bf16[2,3,2,64,128]{4,3,2,1,0:T(8,128)(2,1)S(1)} %get-tuple-element.32), channel_id=1, source_target_pairs={{0,12},{4,0},{8,4},{12,8},{1,13},{5,1},{9,5},{13,9},{2,14},{6,2},{... | collective-permute-start | bytes 589832 | tf_op jit(solution)/shard_map/ppermute | solution.py:133
  23.4 4.3 %collective-permute-start.5 = (bf16[2,2,64,128]{3,2,1,0:T(8,128)(2,1)S(1)}, bf16[2,2,64,128]{3,2,1,0:T(8,128)(2,1)S(1)}, u32[]{:S(2)}, u32[]{:S(2)}) collective-permute-start(bf16[2,2,64,128]{3,2,1,0:T(8,128)(2,1)S(1)} %get-tuple-element.36), channel_id=1, source_target_pairs={{0,12},{4,0},{8,4},{12,8},{1,13},{5,1},{9,5},{13,9},{2,14},{6,2},{... | collective-permute-start | bytes 196616 | tf_op jit(solution)/shard_map/ppermute | solution.py:133
  27.8 1.4 %collective-permute-start.6 = (bf16[8,64,128]{2,1,0:T(8,128)(2,1)S(1)}, bf16[8,64,128]{2,1,0:T(8,128)(2,1)S(1)}, u32[]{:S(2)}, u32[]{:S(2)}) collective-permute-start(bf16[8,64,128]{2,1,0:T(8,128)(2,1)S(1)} %far_pieces.1), channel_id=1, source_target_pairs={{0,1},{1,0},{2,3},{3,2},{4,5},{5,4},{6,7},{7,6},{8,9},{9,8},{10,11... | collective-permute-start | bytes 393224 | tf_op jit(solution)/shard_map/ppermute | solution.py:133

commit v5 on v4

--- a/solution.py
+++ b/solution.py
@@ -44,14 +44,11 @@
     gain_t_ref[...] = jnp.broadcast_to(gain_ref[...], (LANES, width)).T
 
 
-def bias_kernel(index_ref, given_ref, bias_ref, table_ref):
-    rows = given_ref.shape[1]
-    table_ref[:, :rows] = given_ref[...]
+def gather_rows(index_ref, table_ref, bias_ref, start):
     chunks = table_ref.shape[1] // LANES
-    index = reordered(reordered(index_ref[...].astype(F32)).T).astype(jnp.int32)
     for column in range(0, WTOK, LANES):
-        for row in range(0, WTOK, 8):
-            part = index[row : row + 8, column : column + LANES]
+        for row in range(0, bias_ref.shape[1], 8):
+            part = index_ref[start + row : start + row + 8, column : column + LANES]
             low = part & (LANES - 1)
             high = part >> 7
             found = [jnp.zeros((8, LANES), F32) for _ in range(HEADS)]
@@ -66,18 +63,56 @@
                 bias_ref[head, row : row + 8, column : column + LANES] = found[head] * LOG2E
 
 
-def prepare(rel_index, table, w_qkv, w_proj, w_up, w_down, gain_attn, gain_mlp):
-    width, hidden = w_up.shape
-    bias = pl.pallas_call(
-        bias_kernel,
-        out_shape=jax.ShapeDtypeStruct((HEADS, WTOK, WTOK), F32),
-        scratch_shapes=[pltpu.VMEM((HEADS, -(-table.shape[1] // LANES) * LANES), F32)],
+def first_bias_kernel(
+    given_index_ref, given_ref, region_ref, gain_ref, other_gain_ref,
+    bias_ref, index_ref, table_ref, region_out_ref, gain_out_ref, other_gain_out_ref,
+):
+    region_out_ref[...] = region_ref[...]
+    gain_out_ref[...] = gain_ref[...]
+    other_gain_out_ref[...] = other_gain_ref[...]
+    rows = given_ref.shape[1]
+    table_ref[...] = jnp.zeros_like(table_ref)
+    table_ref[:, :rows] = given_ref[...]
+    index = reordered(reordered(given_index_ref[...].astype(F32)).T)
+    index_ref[...] = index.astype(jnp.int32)
+    gather_rows(index_ref, table_ref, bias_ref, 0)
+
+
+def second_bias_kernel(index_ref, table_ref, bias_ref):
+    gather_rows(index_ref, table_ref, bias_ref, WTOK - bias_ref.shape[1])
+
+
+def first_bias(rel_index, table, region, gain_attn, gain_mlp):
+    passed = (region, gain_attn, gain_mlp)
+    padded = -(-table.shape[1] // LANES) * LANES
+    return pl.pallas_call(
+        first_bias_kernel,
+        out_shape=[
+            jax.ShapeDtypeStruct((HEADS, EARLY, WTOK), F32),
+            jax.ShapeDtypeStruct((WTOK, WTOK), jnp.int32),
+            jax.ShapeDtypeStruct((HEADS, padded), F32),
+        ]
+        + [jax.ShapeDtypeStruct(a.shape, a.dtype) for a in passed],
+        cost_estimate=cost(0.7),
+        compiler_params=pltpu.CompilerParams(vmem_limit_bytes=32 << 20),
+        name="first_bias",
+    )(rel_index, table, *passed)
+
+
+def second_bias(index, table):
+    return pl.pallas_call(
+        second_bias_kernel,
+        out_shape=jax.ShapeDtypeStruct((HEADS, WTOK - EARLY, WTOK), F32),
         cost_estimate=cost(1),
         compiler_params=pltpu.CompilerParams(vmem_limit_bytes=32 << 20),
-        name="gather_bias",
-    )(rel_index, table)
+        name="second_bias",
+    )(index, table)
+
+
+def turn_weights(after, w_qkv, w_proj, w_up, w_down, gain_attn, gain_mlp):
+    width, hidden = w_up.shape
     shapes = [(2 * width, width), (width, width), (width, width), (hidden, width), (width, hidden)]
-    others = pl.pallas_call(
+    return pl.pallas_call(
         weights_kernel,
         in_specs=[pl.BlockSpec(memory_space=pl.ANY)] + [pl.BlockSpec(memory_space=pltpu.VMEM)] * 6,
         out_shape=[jax.ShapeDtypeStruct((1, width), F32)]
@@ -86,8 +121,7 @@
         cost_estimate=cost(0.3),
         compiler_params=pltpu.CompilerParams(vmem_limit_bytes=32 << 20),
         name="turn_weights",
-    )(bias, w_qkv, w_proj, w_up, w_down, gain_attn, gain_mlp)
-    return bias, *others
+    )(after, w_qkv, w_proj, w_up, w_down, gain_attn, gain_mlp)
 
 
 def cost(micros):
@@ -116,6 +150,7 @@
 
 HALF = SX * WY * WZ
 QUARTER = HALF // 2
+EARLY = 32
 
 
 def moved(value, axis, steps):
@@ -226,9 +261,8 @@
 
 
 def shifted_kernel(
-    tokens_ref, low_ref, region_ref, given_ref, send_ref, own_ref, send_y_ref, own_y_ref, table_ref
+    tokens_ref, low_ref, region_ref, send_ref, own_ref, send_y_ref, own_y_ref
 ):
-    table_ref[...] = given_ref[...]
     windows = own_ref.shape[0]
     size_y = low_ref.shape[1] // SZ
 
@@ -273,7 +307,7 @@
     send_ref[4 * strip :] = got_ref[4 * strip :]
 
 
-def windows_after(x16s, labels, spans, bias_ref, weights, ahead=4):
+def windows_after(x16s, labels, spans, bias_refs, weights, ahead=4):
     gain_attn, w_qv_t, w_k, w_proj_t, w_up_t, w_down_t, gain_mlp = weights
     width = x16s[0].shape[1]
     size = width // HEADS
@@ -312,7 +346,8 @@
     def attend(task, raw):
         at, head = task
         _, _, v_t, _, _, span = states[at]
-        score = raw * scale + bias_ref[head, :, span]
+        bias = jnp.concatenate([ref[head, :, span] for ref in bias_refs], axis=0)
+        score = raw * scale + bias
         weight = jnp.exp2(score - jnp.max(score, axis=0, keepdims=True))
         total = jnp.sum(weight, axis=0, keepdims=True)
         part = dot_nn(v_t[head * size : (head + 1) * size], weight.astype(BF16))
@@ -372,7 +407,7 @@
     return rows[at : at + QUARTER]
 
 
-def inside_kernel(near_ref, own_ref, bias_ref, *rest):
+def inside_kernel(near_ref, own_ref, early_ref, late_ref, *rest):
     weights, (back_ref, kept_ref) = rest[:7], rest[7:]
     windows = own_ref.shape[0]
     region = near_ref[windows * HALF :]
@@ -383,14 +418,14 @@
             jnp.concatenate([near[:QUARTER], own[:QUARTER], near[QUARTER:], own[QUARTER:]], axis=0)
         )
     labels = [window_labels(region, at) for at in range(windows)]
-    afters = windows_after(x16s, labels, [slice(0, WTOK)] * windows, bias_ref, weights)
+    afters = windows_after(x16s, labels, [slice(0, WTOK)] * windows, (early_ref, late_ref), weights)
     for at, after in enumerate(afters):
         for side in range(2):
             back_ref[at % 2, at // 2, side] = quarters(after, 2 * side)
             kept_ref[at % 2, at // 2, side] = quarters(after, 2 * side + 1)
 
 
-def across_kernel(inside_ref, near_ref, own_ref, got_ref, bias_ref, *rest):
+def across_kernel(inside_ref, near_ref, own_ref, got_ref, early_ref, late_ref, *rest):
     weights, (back_ref, kept_ref) = rest[:7], rest[7:]
     size = near_ref.shape[0] - 8 * QUARTER
     windows = (inside_ref.shape[0] - size) // HALF
@@ -406,7 +441,7 @@
             x16s.append(jnp.concatenate([near[0], own[0], near[1], own[1]], axis=0))
             labels.append(window_labels(region, windows + layer))
             spans.append(slice(place * HALF, (place + 1) * HALF))
-    afters = windows_after(x16s, labels, spans, bias_ref, weights, ahead=8)
+    afters = windows_after(x16s, labels, spans, (early_ref, late_ref), weights, ahead=8)
     for place, after in enumerate(afters):
         for layer in range(2):
             back_ref[layer, place] = quarters(after, 2 * layer)
@@ -492,7 +527,10 @@
     flat = tokens.reshape(size_x, size_y * size_z, width)
     low = kernel_call(low_kernel, "low_pieces", 0.2, [(size_x, size_y * SZ, width)], flat)[0]
     low = moved(low, "gz", -1)
-    sent, own, strip, own_strip, table = kernel_call(
+    early, index, table, region, gain_attn, gain_mlp = first_bias(
+        rel_index, bias_table.T, region.transpose(0, 2, 1), gain_attn[None], gain_mlp[None]
+    )
+    sent, own, strip, own_strip = kernel_call(
         shifted_kernel,
         "shifted_pieces",
         0.3,
@@ -501,12 +539,10 @@
             (windows, HALF, width),
             (8 * QUARTER + lines, width),
             (8 * QUARTER, width),
-            jax.ShapeDtypeStruct(bias_table.shape[::-1], F32),
         ],
         flat,
         low,
-        region.transpose(0, 2, 1),
-        bias_table.T,
+        region,
     )
     near = moved(sent, "gx", 1)
     if lax.axis_size("gy") == 2:
@@ -515,8 +551,9 @@
         got = jnp.concatenate(
             [moved(strip[: 4 * QUARTER], "gy", -1), moved(strip[4 * QUARTER :], "gy", 1)]
         )
-    fixed = prepare(
-        rel_index, table, w_qkv, w_proj, w_up, w_down, gain_attn[None], gain_mlp[None]
+    late = second_bias(index, table)
+    fixed = (
+        early, late, *turn_weights(late, w_qkv, w_proj, w_up, w_down, gain_attn, gain_mlp)
     )
     sent_across = kernel_call(
         across_pieces_kernel, "across_pieces", 0.2, [(8 * QUARTER + lines, width)], own_strip, got

time: 30.3 us -> 30.1 us (level)
  starting transfers between devices: 9.5 us -> 9.08 us
    ppermute x7, starting transfers between devices: 9.5 us -> 9.08 us  [moved(): return lax.ppermute(value, names, pairs)]
    pallas_call x2 -> x3, Pallas kernels: 4.03 us -> 4.1 us  [the longest x1 3.32 us: second_bias(): pl.pallas_call(second_bias_kernel, out_shape=jax.ShapeDtypeStruct((HEADS,...]
  transfers between devices with their start and end apart: 7 -> 7, of which waited for: 3 -> 4; matrix products, arithmetic and copies ran while one was open for 0% -> 0% of each run, Pallas kernels for 37% -> 38%
where the time goes in v5:
time: 30.1 us; the launch traced here: 29.9 us
  Pallas kernels  12.8 us (43%)
  starting transfers between devices  9.08 us (30%)
  waiting for transfers between devices  6.18 us (21%)
  local copies, waits for them, and re-layouts  1.75 us (6%)
    ppermute x7, starting transfers between devices, moved(): return lax.ppermute(value, names, pairs)  9.08 us
    pallas_call x6, Pallas kernels, kernel_call(): pl.pallas_call(kernel, out_shape=[shape if hasattr(shape, 'dtype') else j...  7.7 us
    ppermute x7, waiting for transfers between devices, moved(): return lax.ppermute(value, names, pairs)  6.18 us
    pallas_call x1, Pallas kernels, second_bias(): pl.pallas_call(second_bias_kernel, out_shape=jax.ShapeDtypeStruct((HEADS,...  3.32 us
    unnamed x20, local copies, waits for them, and re-layouts  1.75 us
    pallas_call x1, Pallas kernels, last_call(): pl.pallas_call(last_kernel, in_specs=[pl.BlockSpec(memory_space=pltpu.VME...  0.98 us
    pallas_call x1, Pallas kernels, first_bias(): pl.pallas_call(first_bias_kernel, out_shape=[jax.ShapeDtypeStruct((HEADS,...  0.61 us
  transfers between devices with their start and end apart: 7, of which 4 were waited for; matrix products, arithmetic and copies ran while one was open for 0% of the time, Pallas kernels for 38%

profile of v5, /device:TPU:0, one launch (start us, length us, event | category | flops | bytes accessed | tf_op | source)
XLA Modules:
  0.0 29.9 jit_solution(7069568233074431575)
XLA Ops:
  0.0 0.0 copy-start.4
  0.0 1.0 %copy-done.4 = bf16[8,32,8,128]{3,2,1,0:T(8,128)(2,1)S(1)} copy-done((bf16[8,32,8,128]{3,2,1,0:T(8,128)(2,1)S(1)}, bf16[8,32,8,128]{3,2,1,0:T(8,128)(2,1)}, u32[]{:S(2)}) %copy-start.4) | copy-done | bytes 524312
  1.0 0.0 copy-start.5
  1.0 0.0 copy-start.6
  1.0 0.0 copy-start.7
  1.0 0.1 low_pieces.1
  1.1 0.5 %collective-permute-start = (bf16[8,64,128]{2,1,0:T(8,128)(2,1)S(1)}, bf16[8,64,128]{2,1,0:T(8,128)(2,1)S(1)}, u32[]{:S(2)}, u32[]{:S(2)}) collective-permute-start(bf16[8,64,128]{2,1,0:T(8,128)(2,1)S(1)} %low_pieces.1), channel_id=1, source_target_pairs={{0,1},{1,0},{2,3},{3,2},{4,5},{5,4},{6,7},{7,6},{8,9},{9,8},{10,11... | collective-permute-start | bytes 393224 | tf_op jit(solution)/shard_map/ppermute | solution.py:168
  1.7 0.0 copy-start.8
  1.7 0.0 copy-start.9
  1.7 0.3 %copy-done.5 = s32[256,256]{1,0:T(8,128)S(1)} copy-done((s32[256,256]{1,0:T(8,128)S(1)}, s32[256,256]{1,0:T(8,128)}, u32[]{:S(2)}) %copy-start.5) | copy-done | bytes 262168
  2.0 0.0 copy-done.6
  2.0 0.0 copy-done.7
  2.0 0.3 %copy-done.8 = f32[128]{0:T(128)S(1)} copy-done((f32[128]{0:T(128)S(1)}, f32[128]{0:T(128)}, u32[]{:S(2)}) %copy-start.8) | copy-done | bytes 536
  2.3 0.0 copy-done.9
  2.4 0.6 %first_bias.1 = (f32[4,32,256]{2,1,0:T(8,128)S(1)}, s32[256,256]{1,0:T(8,128)S(1)}, f32[4,1664]{1,0:T(4,128)S(1)}, s32[8,8,32]{2,1,0:T(8,128)S(1)}, f32[1,128]{1,0:T(1,128)S(1)}, /*index=5*/f32[1,128]{1,0:T(1,128)S(1)}) custom-call(s32[256,256]{1,0:T(8,128)S(1)} %copy-done.5, f32[4,1575]{1,0:T(4,128)S(1)} %bitcast.9, s32[8,8,32]{2,1,0:T(8,128)S(1)} %bitcast.8, ...), custom_call_target="tpu_custom_call" | custom-call | flops 770000000 | bytes 2310000 | tf_op jit(solution)/shard_map/first_bias/pallas_call | solution.py:88
  3.0 0.0 collective-permute-done.low_ref
  3.0 0.2 shifted_pieces.1
  3.2 2.7 %collective-permute-start.1 = (bf16[832,128]{1,0:T(8,128)(2,1)S(1)}, bf16[832,128]{1,0:T(8,128)(2,1)S(1)}, u32[]{:S(2)}, u32[]{:S(2)}) collective-permute-start(bf16[832,128]{1,0:T(8,128)(2,1)S(1)} %get-tuple-element.27), channel_id=1, source_target_pairs={{0,4},{4,8},{8,12},{12,0},{1,5},{5,9},{9,13},{13,1},{2,6},{6,10},{... | collective-permute-start | bytes 638984 | tf_op jit(solution)/shard_map/ppermute | solution.py:168
  6.0 1.5 %collective-permute-start.3 = (bf16[576,128]{1,0:T(8,128)(2,1)S(1)}, bf16[576,128]{1,0:T(8,128)(2,1)S(1)}, u32[]{:S(2)}, u32[]{:S(2)}) collective-permute-start(bf16[576,128]{1,0:T(8,128)(2,1)S(1)} %get-tuple-element.44), channel_id=1, source_target_pairs={{0,2},{2,0},{1,3},{3,1},{4,6},{6,4},{5,7},{7,5},{8,10},{10,8},{9,1... | collective-permute-start | bytes 442376 | tf_op jit(solution)/shard_map/ppermute | solution.py:168
  7.5 0.0 copy-start
  7.5 0.0 copy-start.1
  7.5 0.0 copy-start.2
  7.5 0.0 copy-start.3
  7.5 3.3 %second_bias.1._.late_ref = f32[4,224,256]{2,1,0:T(8,128)S(1)} custom-call(s32[256,256]{1,0:T(8,128)S(1)} %get-tuple-element.30.index_ref, f32[4,1664]{1,0:T(4,128)S(1)} %get-tuple-element.31.table_ref), custom_call_target="tpu_custom_call" | custom-call | flops 1100000000 | bytes 3300000 | tf_op jit(solution)/shard_map/second_bias/pallas_call | solution.py:103
  10.8 0.0 copy-done
  10.8 0.0 copy-done.1
  10.8 0.0 copy-done.2
  10.8 0.0 copy-done.3
  10.8 0.2 turn_weights.1
  11.0 0.9 %collective-permute-done.3.got_ref = bf16[576,128]{1,0:T(8,128)(2,1)S(1)} collective-permute-done((bf16[576,128]{1,0:T(8,128)(2,1)S(1)}, bf16[576,128]{1,0:T(8,128)(2,1)S(1)}, u32[]{:S(2)}, u32[]{:S(2)}) %collective-permute-start.3) | collective-permute-done | bytes 147488 | tf_op jit(solution)/shard_map/ppermute | solution.py:168
  11.9 1.6 %collective-permute-start.4 = (bf16[576,128]{1,0:T(8,128)(2,1)S(1)}, bf16[576,128]{1,0:T(8,128)(2,1)S(1)}, u32[]{:S(2)}, u32[]{:S(2)}) collective-permute-start(bf16[576,128]{1,0:T(8,128)(2,1)S(1)} %across_pieces.1), channel_id=1, source_target_pairs={{0,4},{4,8},{8,12},{12,0},{1,5},{5,9},{9,13},{13,1},{2,6},{6,10},{... | collective-permute-start | bytes 442376 | tf_op jit(solution)/shard_map/ppermute | solution.py:168
  13.5 0.3 collective-permute-done.1.near_ref.inside_ref
  13.8 4.5 %inside_windows.1 = (bf16[2,3,2,64,128]{4,3,2,1,0:T(8,128)(2,1)S(1)}, bf16[2,3,2,64,128]{4,3,2,1,0:T(8,128)(2,1)S(1)}) custom-call(bf16[832,128]{1,0:T(8,128)(2,1)S(1)} %collective-permute-done.1.near_ref.inside_ref, bf16[6,128,128]{2,1,0:T(8,128)(2,1)S(1)} %get-tuple-element.28.own_ref, f32[4,32,256]{2,1,0:T(8,128)S(1)} %get-tuple-element.29.early_ref, ...), custom_call_target="tpu_custom_call" | custom-call | flops 16499999744 | bytes 49500000 | tf_op jit(solution)/shard_map/inside_windows/pallas_call | solution.py:510
  18.3 2.0 %collective-permute-start.2 = (bf16[2,3,2,64,128]{4,3,2,1,0:T(8,128)(2,1)S(1)}, bf16[2,3,2,64,128]{4,3,2,1,0:T(8,128)(2,1)S(1)}, u32[]{:S(2)}, u32[]{:S(2)}) collective-permute-start(bf16[2,3,2,64,128]{4,3,2,1,0:T(8,128)(2,1)S(1)} %get-tuple-element.42), channel_id=1, source_target_pairs={{0,12},{4,0},{8,4},{12,8},{1,13},{5,1},{9,5},{13,9},{2,14},{6,2},{... | collective-permute-start | bytes 589832 | tf_op jit(solution)/shard_map/ppermute | solution.py:168
  20.3 0.0 collective-permute-done.4.near_ref
  20.3 2.8 %across_windows.1 = (bf16[2,2,64,128]{3,2,1,0:T(8,128)(2,1)S(1)}, bf16[2,2,64,128]{3,2,1,0:T(8,128)(2,1)S(1)}) custom-call(bf16[832,128]{1,0:T(8,128)(2,1)S(1)} %collective-permute-done.1.near_ref.inside_ref, bf16[576,128]{1,0:T(8,128)(2,1)S(1)} %collective-permute-done.4.near_ref, bf16[512,128]{1,0:T(8,128)(2,1)S(1)} %get-tuple-element.43.own_ref, ...), custom_call_target="tpu_custom_call" | custom-call | flops 2529999872 | bytes 7589999 | tf_op jit(solution)/shard_map/across_windows/pallas_call | solution.py:510
  23.1 0.6 %collective-permute-start.5 = (bf16[2,2,64,128]{3,2,1,0:T(8,128)(2,1)S(1)}, bf16[2,2,64,128]{3,2,1,0:T(8,128)(2,1)S(1)}, u32[]{:S(2)}, u32[]{:S(2)}) collective-permute-start(bf16[2,2,64,128]{3,2,1,0:T(8,128)(2,1)S(1)} %get-tuple-element.46), channel_id=1, source_target_pairs={{0,12},{4,0},{8,4},{12,8},{1,13},{5,1},{9,5},{13,9},{2,14},{6,2},{... | collective-permute-start | bytes 196616 | tf_op jit(solution)/shard_map/ppermute | solution.py:168
  23.7 3.7 %collective-permute-done.5.back_across_ref = bf16[2,2,64,128]{3,2,1,0:T(8,128)(2,1)S(1)} collective-permute-done((bf16[2,2,64,128]{3,2,1,0:T(8,128)(2,1)S(1)}, bf16[2,2,64,128]{3,2,1,0:T(8,128)(2,1)S(1)}, u32[]{:S(2)}, u32[]{:S(2)}) %collective-permute-start.5) | collective-permute-done | bytes 65568 | tf_op jit(solution)/shard_map/ppermute | solution.py:168
  27.4 0.0 collective-permute-done.2.back_ref
  27.4 0.1 far_pieces.1
  27.5 0.1 collective-permute-start.6
  27.6 1.3 %collective-permute-done.6.low_ref = bf16[8,64,128]{2,1,0:T(8,128)(2,1)S(1)} collective-permute-done((bf16[8,64,128]{2,1,0:T(8,128)(2,1)S(1)}, bf16[8,64,128]{2,1,0:T(8,128)(2,1)S(1)}, u32[]{:S(2)}, u32[]{:S(2)}) %collective-permute-start.6) | collective-permute-done | bytes 131104 | tf_op jit(solution)/shard_map/ppermute | solution.py:168
  28.9 1.0 %last_pieces.1 = bf16[8,256,128]{2,1,0:T(8,128)(2,1)} custom-call(bf16[8,64,128]{2,1,0:T(8,128)(2,1)S(1)} %collective-permute-done.6.low_ref, bf16[2,3,2,64,128]{4,3,2,1,0:T(8,128)(2,1)S(1)} %get-tuple-element.41.kept_ref, bf16[2,3,2,64,128]{4,3,2,1,0:T(8,128)(2,1)S(1)} %collective-permute-done.2.back_ref, ...), custom_call_target="tpu_custom_call" | custom-call | flops 1100000000 | bytes 3300000 | tf_op jit(solution)/shard_map/last_pieces/pallas_call | solution.py:497
  (1 shorter events, 0.0 us)
Async XLA Ops:
  0.0 1.0 %copy-start.4 = (bf16[8,32,8,128]{3,2,1,0:T(8,128)(2,1)S(1)}, bf16[8,32,8,128]{3,2,1,0:T(8,128)(2,1)}, u32[]{:S(2)}) copy-start(bf16[8,32,8,128]{3,2,1,0:T(8,128)(2,1)} %param.10) | copy-start | bytes 1572868
  1.0 0.9 %copy-start.5 = (s32[256,256]{1,0:T(8,128)S(1)}, s32[256,256]{1,0:T(8,128)}, u32[]{:S(2)}) copy-start(s32[256,256]{1,0:T(8,128)} %given_index_ref.1) | copy-start | bytes 786436
  1.0 1.0 %copy-start.6 = (s32[8,32,8]{1,2,0:T(8,128)S(1)}, s32[8,32,8]{1,2,0:T(8,128)}, u32[]{:S(2)}) copy-start(s32[8,32,8]{1,2,0:T(8,128)} %param.11) | copy-start | bytes 24580
  1.0 1.0 %copy-start.7 = (f32[1575,4]{0,1:T(4,128)S(1)}, f32[1575,4]{0,1:T(4,128)}, u32[]{:S(2)}) copy-start(f32[1575,4]{0,1:T(4,128)} %param.13) | copy-start | bytes 75604
  1.1 1.8 %collective-permute-start = (bf16[8,64,128]{2,1,0:T(8,128)(2,1)S(1)}, bf16[8,64,128]{2,1,0:T(8,128)(2,1)S(1)}, u32[]{:S(2)}, u32[]{:S(2)}) collective-permute-start(bf16[8,64,128]{2,1,0:T(8,128)(2,1)S(1)} %low_pieces.1), channel_id=1, source_target_pairs={{0,1},{1,0},{2,3},{3,2},{4,5},{5,4},{6,7},{7,6},{8,9},{9,8},{10,11... | collective-permute-start | bytes 393224 | tf_op jit(solution)/shard_map/ppermute | solution.py:168
  1.7 0.7 %copy-start.8 = (f32[128]{0:T(128)S(1)}, f32[128]{0:T(128)}, u32[]{:S(2)}) copy-start(f32[128]{0:T(128)} %param.14) | copy-start | bytes 1540
  1.7 0.7 %copy-start.9 = (f32[128]{0:T(128)S(1)}, f32[128]{0:T(128)}, u32[]{:S(2)}) copy-start(f32[128]{0:T(128)} %param.17) | copy-start | bytes 1540
  3.2 10.6 %collective-permute-start.1 = (bf16[832,128]{1,0:T(8,128)(2,1)S(1)}, bf16[832,128]{1,0:T(8,128)(2,1)S(1)}, u32[]{:S(2)}, u32[]{:S(2)}) collective-permute-start(bf16[832,128]{1,0:T(8,128)(2,1)S(1)} %get-tuple-element.27), channel_id=1, source_target_pairs={{0,4},{4,8},{8,12},{12,0},{1,5},{5,9},{9,13},{13,1},{2,6},{6,10},{... | collective-permute-start | bytes 638984 | tf_op jit(solution)/shard_map/ppermute | solution.py:168
  6.0 5.9 %collective-permute-start.3 = (bf16[576,128]{1,0:T(8,128)(2,1)S(1)}, bf16[576,128]{1,0:T(8,128)(2,1)S(1)}, u32[]{:S(2)}, u32[]{:S(2)}) collective-permute-start(bf16[576,128]{1,0:T(8,128)(2,1)S(1)} %get-tuple-element.44), channel_id=1, source_target_pairs={{0,2},{2,0},{1,3},{3,1},{4,6},{6,4},{5,7},{7,5},{8,10},{10,8},{9,1... | collective-permute-start | bytes 442376 | tf_op jit(solution)/shard_map/ppermute | solution.py:168
  7.5 3.3 %copy-start = (bf16[128,512]{1,0:T(8,128)(2,1)S(1)}, bf16[128,512]{1,0:T(8,128)(2,1)}, u32[]{:S(2)}) copy-start(bf16[128,512]{1,0:T(8,128)(2,1)} %w_up_ref.1) | copy-start | bytes 393220
  7.5 3.3 %copy-start.1 = (bf16[512,128]{1,0:T(8,128)(2,1)S(1)}, bf16[512,128]{1,0:T(8,128)(2,1)}, u32[]{:S(2)}) copy-start(bf16[512,128]{1,0:T(8,128)(2,1)} %w_down_ref.1) | copy-start | bytes 393220
  7.5 3.3 %copy-start.2 = (bf16[128,384]{1,0:T(8,128)(2,1)S(1)}, bf16[128,384]{1,0:T(8,128)(2,1)}, u32[]{:S(2)}) copy-start(bf16[128,384]{1,0:T(8,128)(2,1)} %w_qkv_ref.1) | copy-start | bytes 294916
  7.5 3.4 %copy-start.3 = (bf16[128,128]{1,0:T(8,128)(2,1)S(1)}, bf16[128,128]{1,0:T(8,128)(2,1)}, u32[]{:S(2)}) copy-start(bf16[128,128]{1,0:T(8,128)(2,1)} %w_proj_ref.1) | copy-start | bytes 98308
  11.9 8.4 %collective-permute-start.4 = (bf16[576,128]{1,0:T(8,128)(2,1)S(1)}, bf16[576,128]{1,0:T(8,128)(2,1)S(1)}, u32[]{:S(2)}, u32[]{:S(2)}) collective-permute-start(bf16[576,128]{1,0:T(8,128)(2,1)S(1)} %across_pieces.1), channel_id=1, source_target_pairs={{0,4},{4,8},{8,12},{12,0},{1,5},{5,9},{9,13},{13,1},{2,6},{6,10},{... | collective-permute-start | bytes 442376 | tf_op jit(solution)/shard_map/ppermute | solution.py:168
  18.3 9.2 %collective-permute-start.2 = (bf16[2,3,2,64,128]{4,3,2,1,0:T(8,128)(2,1)S(1)}, bf16[2,3,2,64,128]{4,3,2,1,0:T(8,128)(2,1)S(1)}, u32[]{:S(2)}, u32[]{:S(2)}) collective-permute-start(bf16[2,3,2,64,128]{4,3,2,1,0:T(8,128)(2,1)S(1)} %get-tuple-element.42), channel_id=1, source_target_pairs={{0,12},{4,0},{8,4},{12,8},{1,13},{5,1},{9,5},{13,9},{2,14},{6,2},{... | collective-permute-start | bytes 589832 | tf_op jit(solution)/shard_map/ppermute | solution.py:168
  23.1 4.3 %collective-permute-start.5 = (bf16[2,2,64,128]{3,2,1,0:T(8,128)(2,1)S(1)}, bf16[2,2,64,128]{3,2,1,0:T(8,128)(2,1)S(1)}, u32[]{:S(2)}, u32[]{:S(2)}) collective-permute-start(bf16[2,2,64,128]{3,2,1,0:T(8,128)(2,1)S(1)} %get-tuple-element.46), channel_id=1, source_target_pairs={{0,12},{4,0},{8,4},{12,8},{1,13},{5,1},{9,5},{13,9},{2,14},{6,2},{... | collective-permute-start | bytes 196616 | tf_op jit(solution)/shard_map/ppermute | solution.py:168
  27.5 1.4 %collective-permute-start.6 = (bf16[8,64,128]{2,1,0:T(8,128)(2,1)S(1)}, bf16[8,64,128]{2,1,0:T(8,128)(2,1)S(1)}, u32[]{:S(2)}, u32[]{:S(2)}) collective-permute-start(bf16[8,64,128]{2,1,0:T(8,128)(2,1)S(1)} %far_pieces.1), channel_id=1, source_target_pairs={{0,1},{1,0},{2,3},{3,2},{4,5},{5,4},{6,7},{7,6},{8,9},{9,8},{10,11... | collective-permute-start | bytes 393224 | tf_op jit(solution)/shard_map/ppermute | solution.py:168

commit v6 on v5

--- a/solution.py
+++ b/solution.py
@@ -1,3 +1,4 @@
+import functools
 import math
 
 import jax
@@ -457,53 +458,41 @@
     yield 0, [across_ref[layer, 1] for layer in range(2)]
 
 
-def far_kernel(kept_ref, back_ref, kept_across_ref, back_across_ref, out_ref):
+def far_kernel(inside_ref, across_ref, out_ref):
     size_y = out_ref.shape[1] // SZ
-    for x_from, inside_ref, across_ref in (
-        (0, kept_ref, kept_across_ref),
-        (SX, back_ref, back_across_ref),
-    ):
-        for start, (_, edge) in strips(size_y, inside_ref, across_ref):
-            far = unpair_edge(as_groups(edge))[1]
-            out_ref[x_from : x_from + SX, start * SZ : (start + SY) * SZ] = rows_of(far, SX)
-
-
-def last_kernel(
-    low_ref, kept_ref, back_ref, kept_across_ref, back_across_ref, out_ref, block_ref, sent
-):
+    for start, (_, edge) in strips(size_y, inside_ref, across_ref):
+        far = unpair_edge(as_groups(edge))[1]
+        out_ref[:, start * SZ : (start + SY) * SZ] = rows_of(far, SX)
+
+
+def join_kernel(x_from, low_ref, inside_ref, across_ref, *rest):
+    out_ref, block_ref, sent = rest[-3:]
     size_y = low_ref.shape[1] // SZ
     size_z = 8
-    moves = []
-    for x_from, inside_ref, across_ref in (
-        (0, kept_ref, kept_across_ref),
-        (SX, back_ref, back_across_ref),
-    ):
-        planes = slice(x_from, x_from + SX)
-        for start, (core, edge) in strips(size_y, inside_ref, across_ref):
-            low = tall_of(low_ref, x_from, start, start + SY, SZ)
-            near = unpair_edge(as_groups(edge))[0]
-            tall = join_tall(low, as_groups(core), near)
-            block_ref[planes, start * size_z : (start + SY) * size_z] = rows_of(tall, SX)
-        move = pltpu.make_async_copy(
-            block_ref.at[planes], out_ref.at[planes], sent.at[len(moves)]
-        )
-        move.start()
-        moves.append(move)
-    for move in moves:
-        move.wait()
-
-
-def last_call(low, after, shape):
+    for start, (core, edge) in strips(size_y, inside_ref, across_ref):
+        low = low_ref[:, start * SZ : (start + SY) * SZ, :].astype(F32).reshape(-1, 8, LANES)
+        near = unpair_edge(as_groups(edge))[0]
+        tall = join_tall(low, as_groups(core), near)
+        block_ref[:, start * size_z : (start + SY) * size_z] = rows_of(tall, SX)
+    move = pltpu.make_async_copy(block_ref, out_ref.at[x_from : x_from + SX], sent)
+    move.start()
+    move.wait()
+
+
+def join_call(name, x_from, shape, *operands):
+    given = len(operands) - 3
     return pl.pallas_call(
-        last_kernel,
-        in_specs=[pl.BlockSpec(memory_space=pltpu.VMEM)] * 5,
+        functools.partial(join_kernel, x_from),
+        in_specs=[pl.BlockSpec(memory_space=pltpu.VMEM)] * 3
+        + [pl.BlockSpec(memory_space=pl.ANY)] * given,
         out_specs=pl.BlockSpec(memory_space=pl.ANY),
         out_shape=jax.ShapeDtypeStruct(shape, BF16),
-        scratch_shapes=[pltpu.VMEM(shape, BF16), pltpu.SemaphoreType.DMA((2,))],
-        cost_estimate=cost(1),
+        scratch_shapes=[pltpu.VMEM((SX,) + shape[1:], BF16), pltpu.SemaphoreType.DMA],
+        input_output_aliases={3: 0} if given else {},
+        cost_estimate=cost(0.7),
         compiler_params=pltpu.CompilerParams(vmem_limit_bytes=48 << 20),
-        name="last_pieces",
-    )(low, *after)
+        name=name,
+    )(*operands)
 
 
 def kernel_call(kernel, name, micros, outs, *operands):
@@ -569,10 +558,16 @@
         across_kernel, "across_windows", 2.3, [halves, halves], near, near_across, own_strip, got, *fixed
     )
     back_across = moved(back_across, "gx", -1)
-    after = (kept, back, kept_across, back_across)
-    far = kernel_call(far_kernel, "far_pieces", 0.1, [(size_x, size_y * SZ, width)], *after)[0]
-    far = moved(far, "gz", 1)
-    return last_call(far, after, flat.shape).reshape(tokens.shape)
+    low_shape = [(SX, size_y * SZ, width)]
+    low_own = kernel_call(far_kernel, "far_own", 0.1, low_shape, kept, kept_across)[0]
+    out = join_call(
+        "own_pieces", 0, flat.shape, moved(low_own, "gz", 1), kept, kept_across
+    )
+    low_back = kernel_call(far_kernel, "far_back", 0.1, low_shape, back, back_across)[0]
+    out = join_call(
+        "last_pieces", SX, flat.shape, moved(low_back, "gz", 1), back, back_across, out
+    )
+    return out.reshape(tokens.shape)
 
 
 def solution(mesh):

time: 30.1 us -> 29.8 us (0.990)
  waiting for transfers between devices: 6.18 us -> 5.11 us
  Pallas kernels: 12.8 us -> 13.5 us
    ppermute x7 -> x8, waiting for transfers between devices: 6.18 us -> 5.11 us  [moved(): return lax.ppermute(value, names, pairs)]
    pallas_call x1 -> x2, Pallas kernels: 0.98 us -> 1.69 us  [join_call(): pl.pallas_call(functools.partial(join_kernel, x_from), in_specs=[pl.Block...]
    ppermute x7 -> x8, starting transfers between devices: 9.08 us -> 9.15 us  [moved(): return lax.ppermute(value, names, pairs)]
    pallas_call x6 -> x7, Pallas kernels: 7.7 us -> 7.72 us  [kernel_call(): pl.pallas_call(kernel, out_shape=[shape if hasattr(shape, 'dtype') else j...]
  transfers between devices with their start and end apart: 7 -> 8, of which waited for: 4 -> 4; matrix products, arithmetic and copies ran while one was open for 0% -> 0% of each run, Pallas kernels for 38% -> 42%
where the time goes in v6:
time: 29.8 us; the launch traced here: 29.6 us
  Pallas kernels  13.5 us (45%)
  starting transfers between devices  9.15 us (31%)
  waiting for transfers between devices  5.11 us (17%)
  local copies, waits for them, and re-layouts  1.75 us (6%)
    ppermute x8, starting transfers between devices, moved(): return lax.ppermute(value, names, pairs)  9.15 us
    pallas_call x7, Pallas kernels, kernel_call(): pl.pallas_call(kernel, out_shape=[shape if hasattr(shape, 'dtype') else j...  7.72 us
    ppermute x8, waiting for transfers between devices, moved(): return lax.ppermute(value, names, pairs)  5.11 us
    pallas_call x1, Pallas kernels, second_bias(): pl.pallas_call(second_bias_kernel, out_shape=jax.ShapeDtypeStruct((HEADS,...  3.31 us
    unnamed x20, local copies, waits for them, and re-layouts  1.75 us
    pallas_call x2, Pallas kernels, join_call(): pl.pallas_call(functools.partial(join_kernel, x_from), in_specs=[pl.Block...  1.69 us
    pallas_call x1, Pallas kernels, first_bias(): pl.pallas_call(first_bias_kernel, out_shape=[jax.ShapeDtypeStruct((HEADS,...  0.61 us
  transfers between devices with their start and end apart: 8, of which 4 were waited for; matrix products, arithmetic and copies ran while one was open for 0% of the time, Pallas kernels for 42%

profile of v6, /device:TPU:0, one launch (start us, length us, event | category | flops | bytes accessed | tf_op | source)
XLA Modules:
  0.0 29.6 jit_solution(18141371663446628703)
XLA Ops:
  0.0 0.0 copy-start.4
  0.0 1.0 %copy-done.4 = bf16[8,32,8,128]{3,2,1,0:T(8,128)(2,1)S(1)} copy-done((bf16[8,32,8,128]{3,2,1,0:T(8,128)(2,1)S(1)}, bf16[8,32,8,128]{3,2,1,0:T(8,128)(2,1)}, u32[]{:S(2)}) %copy-start.4) | copy-done | bytes 524312
  1.0 0.0 copy-start.5
  1.0 0.0 copy-start.6
  1.0 0.0 copy-start.7
  1.0 0.1 low_pieces.1
  1.1 0.5 %collective-permute-start = (bf16[8,64,128]{2,1,0:T(8,128)(2,1)S(1)}, bf16[8,64,128]{2,1,0:T(8,128)(2,1)S(1)}, u32[]{:S(2)}, u32[]{:S(2)}) collective-permute-start(bf16[8,64,128]{2,1,0:T(8,128)(2,1)S(1)} %low_pieces.1), channel_id=1, source_target_pairs={{0,1},{1,0},{2,3},{3,2},{4,5},{5,4},{6,7},{7,6},{8,9},{9,8},{10,11... | collective-permute-start | bytes 393224 | tf_op jit(solution)/shard_map/ppermute | solution.py:169
  1.7 0.0 copy-start.8
  1.7 0.0 copy-start.9
  1.7 0.3 %copy-done.5 = s32[256,256]{1,0:T(8,128)S(1)} copy-done((s32[256,256]{1,0:T(8,128)S(1)}, s32[256,256]{1,0:T(8,128)}, u32[]{:S(2)}) %copy-start.5) | copy-done | bytes 262168
  2.0 0.0 copy-done.6
  2.0 0.0 copy-done.7
  2.0 0.3 %copy-done.8 = f32[128]{0:T(128)S(1)} copy-done((f32[128]{0:T(128)S(1)}, f32[128]{0:T(128)}, u32[]{:S(2)}) %copy-start.8) | copy-done | bytes 536
  2.3 0.0 copy-done.9
  2.4 0.6 %first_bias.1 = (f32[4,32,256]{2,1,0:T(8,128)S(1)}, s32[256,256]{1,0:T(8,128)S(1)}, f32[4,1664]{1,0:T(4,128)S(1)}, s32[8,8,32]{2,1,0:T(8,128)S(1)}, f32[1,128]{1,0:T(1,128)S(1)}, /*index=5*/f32[1,128]{1,0:T(1,128)S(1)}) custom-call(s32[256,256]{1,0:T(8,128)S(1)} %copy-done.5, f32[4,1575]{1,0:T(4,128)S(1)} %bitcast.9, s32[8,8,32]{2,1,0:T(8,128)S(1)} %bitcast.8, ...), custom_call_target="tpu_custom_call" | custom-call | flops 770000000 | bytes 2310000 | tf_op jit(solution)/shard_map/first_bias/pallas_call | solution.py:89
  3.0 0.0 collective-permute-done.low_ref
  3.0 0.2 shifted_pieces.1
  3.2 2.7 %collective-permute-start.1 = (bf16[832,128]{1,0:T(8,128)(2,1)S(1)}, bf16[832,128]{1,0:T(8,128)(2,1)S(1)}, u32[]{:S(2)}, u32[]{:S(2)}) collective-permute-start(bf16[832,128]{1,0:T(8,128)(2,1)S(1)} %get-tuple-element.27), channel_id=1, source_target_pairs={{0,4},{4,8},{8,12},{12,0},{1,5},{5,9},{9,13},{13,1},{2,6},{6,10},{... | collective-permute-start | bytes 638984 | tf_op jit(solution)/shard_map/ppermute | solution.py:169
  6.0 1.5 %collective-permute-start.3 = (bf16[576,128]{1,0:T(8,128)(2,1)S(1)}, bf16[576,128]{1,0:T(8,128)(2,1)S(1)}, u32[]{:S(2)}, u32[]{:S(2)}) collective-permute-start(bf16[576,128]{1,0:T(8,128)(2,1)S(1)} %get-tuple-element.43), channel_id=1, source_target_pairs={{0,2},{2,0},{1,3},{3,1},{4,6},{6,4},{5,7},{7,5},{8,10},{10,8},{9,1... | collective-permute-start | bytes 442376 | tf_op jit(solution)/shard_map/ppermute | solution.py:169
  7.5 0.0 copy-start
  7.5 0.0 copy-start.1
  7.5 0.0 copy-start.2
  7.5 0.0 copy-start.3
  7.5 3.3 %second_bias.1._.late_ref = f32[4,224,256]{2,1,0:T(8,128)S(1)} custom-call(s32[256,256]{1,0:T(8,128)S(1)} %get-tuple-element.30.index_ref, f32[4,1664]{1,0:T(4,128)S(1)} %get-tuple-element.31.table_ref), custom_call_target="tpu_custom_call" | custom-call | flops 1100000000 | bytes 3300000 | tf_op jit(solution)/shard_map/second_bias/pallas_call | solution.py:104
  10.8 0.0 copy-done
  10.8 0.0 copy-done.1
  10.8 0.0 copy-done.2
  10.8 0.0 copy-done.3
  10.8 0.2 turn_weights.1
  11.0 0.9 %collective-permute-done.3.got_ref = bf16[576,128]{1,0:T(8,128)(2,1)S(1)} collective-permute-done((bf16[576,128]{1,0:T(8,128)(2,1)S(1)}, bf16[576,128]{1,0:T(8,128)(2,1)S(1)}, u32[]{:S(2)}, u32[]{:S(2)}) %collective-permute-start.3) | collective-permute-done | bytes 147488 | tf_op jit(solution)/shard_map/ppermute | solution.py:169
  11.9 1.6 %collective-permute-start.4 = (bf16[576,128]{1,0:T(8,128)(2,1)S(1)}, bf16[576,128]{1,0:T(8,128)(2,1)S(1)}, u32[]{:S(2)}, u32[]{:S(2)}) collective-permute-start(bf16[576,128]{1,0:T(8,128)(2,1)S(1)} %across_pieces.1), channel_id=1, source_target_pairs={{0,4},{4,8},{8,12},{12,0},{1,5},{5,9},{9,13},{13,1},{2,6},{6,10},{... | collective-permute-start | bytes 442376 | tf_op jit(solution)/shard_map/ppermute | solution.py:169
  13.5 0.3 %collective-permute-done.1.near_ref.inside_ref = bf16[832,128]{1,0:T(8,128)(2,1)S(1)} collective-permute-done((bf16[832,128]{1,0:T(8,128)(2,1)S(1)}, bf16[832,128]{1,0:T(8,128)(2,1)S(1)}, u32[]{:S(2)}, u32[]{:S(2)}) %collective-permute-start.1) | collective-permute-done | bytes 213024 | tf_op jit(solution)/shard_map/ppermute | solution.py:169
  13.8 4.5 %inside_windows.1 = (bf16[2,3,2,64,128]{4,3,2,1,0:T(8,128)(2,1)S(1)}, bf16[2,3,2,64,128]{4,3,2,1,0:T(8,128)(2,1)S(1)}) custom-call(bf16[832,128]{1,0:T(8,128)(2,1)S(1)} %collective-permute-done.1.near_ref.inside_ref, bf16[6,128,128]{2,1,0:T(8,128)(2,1)S(1)} %get-tuple-element.28.own_ref, f32[4,32,256]{2,1,0:T(8,128)S(1)} %get-tuple-element.29.early_ref, ...), custom_call_target="tpu_custom_call" | custom-call | flops 16499999744 | bytes 49500000 | tf_op jit(solution)/shard_map/inside_windows/pallas_call | solution.py:499
  18.3 2.0 %collective-permute-start.2 = (bf16[2,3,2,64,128]{4,3,2,1,0:T(8,128)(2,1)S(1)}, bf16[2,3,2,64,128]{4,3,2,1,0:T(8,128)(2,1)S(1)}, u32[]{:S(2)}, u32[]{:S(2)}) collective-permute-start(bf16[2,3,2,64,128]{4,3,2,1,0:T(8,128)(2,1)S(1)} %get-tuple-element.41), channel_id=1, source_target_pairs={{0,12},{4,0},{8,4},{12,8},{1,13},{5,1},{9,5},{13,9},{2,14},{6,2},{... | collective-permute-start | bytes 589832 | tf_op jit(solution)/shard_map/ppermute | solution.py:169
  20.3 0.0 collective-permute-done.4.near_ref
  20.3 2.8 %across_windows.1 = (bf16[2,2,64,128]{3,2,1,0:T(8,128)(2,1)S(1)}, bf16[2,2,64,128]{3,2,1,0:T(8,128)(2,1)S(1)}) custom-call(bf16[832,128]{1,0:T(8,128)(2,1)S(1)} %collective-permute-done.1.near_ref.inside_ref, bf16[576,128]{1,0:T(8,128)(2,1)S(1)} %collective-permute-done.4.near_ref, bf16[512,128]{1,0:T(8,128)(2,1)S(1)} %get-tuple-element.42.own_ref, ...), custom_call_target="tpu_custom_call" | custom-call | flops 2529999872 | bytes 7589999 | tf_op jit(solution)/shard_map/across_windows/pallas_call | solution.py:499
  23.1 0.6 %collective-permute-start.5 = (bf16[2,2,64,128]{3,2,1,0:T(8,128)(2,1)S(1)}, bf16[2,2,64,128]{3,2,1,0:T(8,128)(2,1)S(1)}, u32[]{:S(2)}, u32[]{:S(2)}) collective-permute-start(bf16[2,2,64,128]{3,2,1,0:T(8,128)(2,1)S(1)} %get-tuple-element.44), channel_id=1, source_target_pairs={{0,12},{4,0},{8,4},{12,8},{1,13},{5,1},{9,5},{13,9},{2,14},{6,2},{... | collective-permute-start | bytes 196616 | tf_op jit(solution)/shard_map/ppermute | solution.py:169
  23.8 0.1 collective-permute-start.7
  23.9 3.6 %collective-permute-done.5.across_ref = bf16[2,2,64,128]{3,2,1,0:T(8,128)(2,1)S(1)} collective-permute-done((bf16[2,2,64,128]{3,2,1,0:T(8,128)(2,1)S(1)}, bf16[2,2,64,128]{3,2,1,0:T(8,128)(2,1)S(1)}, u32[]{:S(2)}, u32[]{:S(2)}) %collective-permute-start.5) | collective-permute-done | bytes 65568 | tf_op jit(solution)/shard_map/ppermute | solution.py:169
  27.4 0.0 collective-permute-done.2.inside_ref
  27.5 0.1 collective-permute-start.6
  27.6 0.0 collective-permute-done.7.low_ref
  27.6 0.8 %own_pieces.1.rest_0_ = bf16[8,256,128]{2,1,0:T(8,128)(2,1)} custom-call(bf16[4,64,128]{2,1,0:T(8,128)(2,1)S(1)} %collective-permute-done.7.low_ref, bf16[2,3,2,64,128]{4,3,2,1,0:T(8,128)(2,1)S(1)} %get-tuple-element.45.inside_ref, bf16[2,2,64,128]{3,2,1,0:T(8,128)(2,1)S(1)} %get-tuple-element.46.across_ref), custom_call_target="tpu_custom_call" | custom-call | flops 770000000 | bytes 2310000 | tf_op jit(solution)/shard_map/own_pieces/pallas_call | solution.py:484
  28.4 0.4 %collective-permute-done.6.low_ref = bf16[4,64,128]{2,1,0:T(8,128)(2,1)S(1)} collective-permute-done((bf16[4,64,128]{2,1,0:T(8,128)(2,1)S(1)}, bf16[4,64,128]{2,1,0:T(8,128)(2,1)S(1)}, u32[]{:S(2)}, u32[]{:S(2)}) %collective-permute-start.6) | collective-permute-done | bytes 65568 | tf_op jit(solution)/shard_map/ppermute | solution.py:169
  28.8 0.8 %last_pieces.1 = bf16[8,256,128]{2,1,0:T(8,128)(2,1)} custom-call(bf16[4,64,128]{2,1,0:T(8,128)(2,1)S(1)} %collective-permute-done.6.low_ref, bf16[2,3,2,64,128]{4,3,2,1,0:T(8,128)(2,1)S(1)} %collective-permute-done.2.inside_ref, bf16[2,2,64,128]{3,2,1,0:T(8,128)(2,1)S(1)} %collective-permute-done.5.across_ref, ...), custom_call_target="tpu_custom_call", output_to_operand_aliasing={{}: (3, {})} | custom-call | flops 770000000 | bytes 2310000 | tf_op jit(solution)/shard_map/last_pieces/pallas_call | solution.py:484
  (3 shorter events, 0.1 us)
Async XLA Ops:
  0.0 1.0 %copy-start.4 = (bf16[8,32,8,128]{3,2,1,0:T(8,128)(2,1)S(1)}, bf16[8,32,8,128]{3,2,1,0:T(8,128)(2,1)}, u32[]{:S(2)}) copy-start(bf16[8,32,8,128]{3,2,1,0:T(8,128)(2,1)} %param.10) | copy-start | bytes 1572868
  1.0 0.9 %copy-start.5 = (s32[256,256]{1,0:T(8,128)S(1)}, s32[256,256]{1,0:T(8,128)}, u32[]{:S(2)}) copy-start(s32[256,256]{1,0:T(8,128)} %given_index_ref.1) | copy-start | bytes 786436
  1.0 1.0 %copy-start.6 = (s32[8,32,8]{1,2,0:T(8,128)S(1)}, s32[8,32,8]{1,2,0:T(8,128)}, u32[]{:S(2)}) copy-start(s32[8,32,8]{1,2,0:T(8,128)} %param.11) | copy-start | bytes 24580
  1.0 1.0 %copy-start.7 = (f32[1575,4]{0,1:T(4,128)S(1)}, f32[1575,4]{0,1:T(4,128)}, u32[]{:S(2)}) copy-start(f32[1575,4]{0,1:T(4,128)} %param.13) | copy-start | bytes 75604
  1.1 1.8 %collective-permute-start = (bf16[8,64,128]{2,1,0:T(8,128)(2,1)S(1)}, bf16[8,64,128]{2,1,0:T(8,128)(2,1)S(1)}, u32[]{:S(2)}, u32[]{:S(2)}) collective-permute-start(bf16[8,64,128]{2,1,0:T(8,128)(2,1)S(1)} %low_pieces.1), channel_id=1, source_target_pairs={{0,1},{1,0},{2,3},{3,2},{4,5},{5,4},{6,7},{7,6},{8,9},{9,8},{10,11... | collective-permute-start | bytes 393224 | tf_op jit(solution)/shard_map/ppermute | solution.py:169
  1.7 0.7 %copy-start.8 = (f32[128]{0:T(128)S(1)}, f32[128]{0:T(128)}, u32[]{:S(2)}) copy-start(f32[128]{0:T(128)} %param.14) | copy-start | bytes 1540
  1.7 0.7 %copy-start.9 = (f32[128]{0:T(128)S(1)}, f32[128]{0:T(128)}, u32[]{:S(2)}) copy-start(f32[128]{0:T(128)} %param.17) | copy-start | bytes 1540
  3.2 10.6 %collective-permute-start.1 = (bf16[832,128]{1,0:T(8,128)(2,1)S(1)}, bf16[832,128]{1,0:T(8,128)(2,1)S(1)}, u32[]{:S(2)}, u32[]{:S(2)}) collective-permute-start(bf16[832,128]{1,0:T(8,128)(2,1)S(1)} %get-tuple-element.27), channel_id=1, source_target_pairs={{0,4},{4,8},{8,12},{12,0},{1,5},{5,9},{9,13},{13,1},{2,6},{6,10},{... | collective-permute-start | bytes 638984 | tf_op jit(solution)/shard_map/ppermute | solution.py:169
  6.0 5.9 %collective-permute-start.3 = (bf16[576,128]{1,0:T(8,128)(2,1)S(1)}, bf16[576,128]{1,0:T(8,128)(2,1)S(1)}, u32[]{:S(2)}, u32[]{:S(2)}) collective-permute-start(bf16[576,128]{1,0:T(8,128)(2,1)S(1)} %get-tuple-element.43), channel_id=1, source_target_pairs={{0,2},{2,0},{1,3},{3,1},{4,6},{6,4},{5,7},{7,5},{8,10},{10,8},{9,1... | collective-permute-start | bytes 442376 | tf_op jit(solution)/shard_map/ppermute | solution.py:169
  7.5 3.3 %copy-start = (bf16[128,512]{1,0:T(8,128)(2,1)S(1)}, bf16[128,512]{1,0:T(8,128)(2,1)}, u32[]{:S(2)}) copy-start(bf16[128,512]{1,0:T(8,128)(2,1)} %w_up_ref.1) | copy-start | bytes 393220
  7.5 3.3 %copy-start.1 = (bf16[512,128]{1,0:T(8,128)(2,1)S(1)}, bf16[512,128]{1,0:T(8,128)(2,1)}, u32[]{:S(2)}) copy-start(bf16[512,128]{1,0:T(8,128)(2,1)} %w_down_ref.1) | copy-start | bytes 393220
  7.5 3.3 %copy-start.2 = (bf16[128,384]{1,0:T(8,128)(2,1)S(1)}, bf16[128,384]{1,0:T(8,128)(2,1)}, u32[]{:S(2)}) copy-start(bf16[128,384]{1,0:T(8,128)(2,1)} %w_qkv_ref.1) | copy-start | bytes 294916
  7.5 3.3 %copy-start.3 = (bf16[128,128]{1,0:T(8,128)(2,1)S(1)}, bf16[128,128]{1,0:T(8,128)(2,1)}, u32[]{:S(2)}) copy-start(bf16[128,128]{1,0:T(8,128)(2,1)} %w_proj_ref.1) | copy-start | bytes 98308
  11.9 8.4 %collective-permute-start.4 = (bf16[576,128]{1,0:T(8,128)(2,1)S(1)}, bf16[576,128]{1,0:T(8,128)(2,1)S(1)}, u32[]{:S(2)}, u32[]{:S(2)}) collective-permute-start(bf16[576,128]{1,0:T(8,128)(2,1)S(1)} %across_pieces.1), channel_id=1, source_target_pairs={{0,4},{4,8},{8,12},{12,0},{1,5},{5,9},{9,13},{13,1},{2,6},{6,10},{... | collective-permute-start | bytes 442376 | tf_op jit(solution)/shard_map/ppermute | solution.py:169
  18.3 9.2 %collective-permute-start.2 = (bf16[2,3,2,64,128]{4,3,2,1,0:T(8,128)(2,1)S(1)}, bf16[2,3,2,64,128]{4,3,2,1,0:T(8,128)(2,1)S(1)}, u32[]{:S(2)}, u32[]{:S(2)}) collective-permute-start(bf16[2,3,2,64,128]{4,3,2,1,0:T(8,128)(2,1)S(1)} %get-tuple-element.41), channel_id=1, source_target_pairs={{0,12},{4,0},{8,4},{12,8},{1,13},{5,1},{9,5},{13,9},{2,14},{6,2},{... | collective-permute-start | bytes 589832 | tf_op jit(solution)/shard_map/ppermute | solution.py:169
  23.1 4.3 %collective-permute-start.5 = (bf16[2,2,64,128]{3,2,1,0:T(8,128)(2,1)S(1)}, bf16[2,2,64,128]{3,2,1,0:T(8,128)(2,1)S(1)}, u32[]{:S(2)}, u32[]{:S(2)}) collective-permute-start(bf16[2,2,64,128]{3,2,1,0:T(8,128)(2,1)S(1)} %get-tuple-element.44), channel_id=1, source_target_pairs={{0,12},{4,0},{8,4},{12,8},{1,13},{5,1},{9,5},{13,9},{2,14},{6,2},{... | collective-permute-start | bytes 196616 | tf_op jit(solution)/shard_map/ppermute | solution.py:169
  23.8 3.8 %collective-permute-start.7 = (bf16[4,64,128]{2,1,0:T(8,128)(2,1)S(1)}, bf16[4,64,128]{2,1,0:T(8,128)(2,1)S(1)}, u32[]{:S(2)}, u32[]{:S(2)}) collective-permute-start(bf16[4,64,128]{2,1,0:T(8,128)(2,1)S(1)} %far_own.1), channel_id=1, source_target_pairs={{0,1},{1,0},{2,3},{3,2},{4,5},{5,4},{6,7},{7,6},{8,9},{9,8},{10,11... | collective-permute-start | bytes 196616 | tf_op jit(solution)/shard_map/ppermute | solution.py:169
  27.5 1.3 %collective-permute-start.6 = (bf16[4,64,128]{2,1,0:T(8,128)(2,1)S(1)}, bf16[4,64,128]{2,1,0:T(8,128)(2,1)S(1)}, u32[]{:S(2)}, u32[]{:S(2)}) collective-permute-start(bf16[4,64,128]{2,1,0:T(8,128)(2,1)S(1)} %far_back.1), channel_id=1, source_target_pairs={{0,1},{1,0},{2,3},{3,2},{4,5},{5,4},{6,7},{7,6},{8,9},{9,8},{10,11... | collective-permute-start | bytes 196616 | tf_op jit(solution)/shard_map/ppermute | solution.py:169

commit v7 on v6

--- a/solution.py
+++ b/solution.py
@@ -151,7 +151,7 @@
 
 HALF = SX * WY * WZ
 QUARTER = HALF // 2
-EARLY = 32
+EARLY = 16
 
 
 def moved(value, axis, steps):

time: 29.8 us -> 29.6 us (level)
  waiting for transfers between devices: 5.11 us -> 4.72 us
    ppermute x8, waiting for transfers between devices: 5.11 us -> 4.72 us  [moved(): return lax.ppermute(value, names, pairs)]
where the time goes in v7:
time: 29.6 us; the launch traced here: 29.4 us
  Pallas kernels  13.5 us (46%)
  starting transfers between devices  9.27 us (31%)
  waiting for transfers between devices  4.72 us (16%)
  local copies, waits for them, and re-layouts  1.75 us (6%)
    ppermute x8, starting transfers between devices, moved(): return lax.ppermute(value, names, pairs)  9.27 us
    pallas_call x7, Pallas kernels, kernel_call(): pl.pallas_call(kernel, out_shape=[shape if hasattr(shape, 'dtype') else j...  7.72 us
    ppermute x8, waiting for transfers between devices, moved(): return lax.ppermute(value, names, pairs)  4.72 us
    pallas_call x1, Pallas kernels, second_bias(): pl.pallas_call(second_bias_kernel, out_shape=jax.ShapeDtypeStruct((HEADS,...  3.54 us
    unnamed x20, local copies, waits for them, and re-layouts  1.75 us
    pallas_call x2, Pallas kernels, join_call(): pl.pallas_call(functools.partial(join_kernel, x_from), in_specs=[pl.Block...  1.69 us
  transfers between devices with their start and end apart: 8, of which 4 were waited for; matrix products, arithmetic and copies ran while one was open for 0% of the time, Pallas kernels for 42%

profile of v7, /device:TPU:0, one launch (start us, length us, event | category | flops | bytes accessed | tf_op | source)
XLA Modules:
  0.0 29.4 jit_solution(16860982009389256306)
XLA Ops:
  0.0 0.0 copy-start.4
  0.0 1.0 %copy-done.4 = bf16[8,32,8,128]{3,2,1,0:T(8,128)(2,1)S(1)} copy-done((bf16[8,32,8,128]{3,2,1,0:T(8,128)(2,1)S(1)}, bf16[8,32,8,128]{3,2,1,0:T(8,128)(2,1)}, u32[]{:S(2)}) %copy-start.4) | copy-done | bytes 524312
  1.0 0.0 copy-start.5
  1.0 0.0 copy-start.6
  1.0 0.0 copy-start.7
  1.0 0.1 low_pieces.1
  1.1 0.5 %collective-permute-start = (bf16[8,64,128]{2,1,0:T(8,128)(2,1)S(1)}, bf16[8,64,128]{2,1,0:T(8,128)(2,1)S(1)}, u32[]{:S(2)}, u32[]{:S(2)}) collective-permute-start(bf16[8,64,128]{2,1,0:T(8,128)(2,1)S(1)} %low_pieces.1), channel_id=1, source_target_pairs={{0,1},{1,0},{2,3},{3,2},{4,5},{5,4},{6,7},{7,6},{8,9},{9,8},{10,11... | collective-permute-start | bytes 393224 | tf_op jit(solution)/shard_map/ppermute | solution.py:169
  1.7 0.0 copy-start.8
  1.7 0.0 copy-start.9
  1.7 0.3 %copy-done.5 = s32[256,256]{1,0:T(8,128)S(1)} copy-done((s32[256,256]{1,0:T(8,128)S(1)}, s32[256,256]{1,0:T(8,128)}, u32[]{:S(2)}) %copy-start.5) | copy-done | bytes 262168
  2.0 0.0 copy-done.6
  2.0 0.0 copy-done.7
  2.0 0.3 %copy-done.8 = f32[128]{0:T(128)S(1)} copy-done((f32[128]{0:T(128)S(1)}, f32[128]{0:T(128)}, u32[]{:S(2)}) %copy-start.8) | copy-done | bytes 536
  2.3 0.0 copy-done.9
  2.4 0.4 %first_bias.1 = (f32[4,16,256]{2,1,0:T(8,128)S(1)}, s32[256,256]{1,0:T(8,128)S(1)}, f32[4,1664]{1,0:T(4,128)S(1)}, s32[8,8,32]{2,1,0:T(8,128)S(1)}, f32[1,128]{1,0:T(1,128)S(1)}, /*index=5*/f32[1,128]{1,0:T(1,128)S(1)}) custom-call(s32[256,256]{1,0:T(8,128)S(1)} %copy-done.5, f32[4,1575]{1,0:T(4,128)S(1)} %bitcast.9, s32[8,8,32]{2,1,0:T(8,128)S(1)} %bitcast.8, ...), custom_call_target="tpu_custom_call" | custom-call | flops 770000000 | bytes 2310000 | tf_op jit(solution)/shard_map/first_bias/pallas_call | solution.py:89
  2.7 0.0 collective-permute-done.low_ref
  2.8 0.2 shifted_pieces.1
  3.0 2.9 %collective-permute-start.1 = (bf16[832,128]{1,0:T(8,128)(2,1)S(1)}, bf16[832,128]{1,0:T(8,128)(2,1)S(1)}, u32[]{:S(2)}, u32[]{:S(2)}) collective-permute-start(bf16[832,128]{1,0:T(8,128)(2,1)S(1)} %get-tuple-element.27), channel_id=1, source_target_pairs={{0,4},{4,8},{8,12},{12,0},{1,5},{5,9},{9,13},{13,1},{2,6},{6,10},{... | collective-permute-start | bytes 638984 | tf_op jit(solution)/shard_map/ppermute | solution.py:169
  5.9 1.5 %collective-permute-start.3 = (bf16[576,128]{1,0:T(8,128)(2,1)S(1)}, bf16[576,128]{1,0:T(8,128)(2,1)S(1)}, u32[]{:S(2)}, u32[]{:S(2)}) collective-permute-start(bf16[576,128]{1,0:T(8,128)(2,1)S(1)} %get-tuple-element.43), channel_id=1, source_target_pairs={{0,2},{2,0},{1,3},{3,1},{4,6},{6,4},{5,7},{7,5},{8,10},{10,8},{9,1... | collective-permute-start | bytes 442376 | tf_op jit(solution)/shard_map/ppermute | solution.py:169
  7.4 0.0 copy-start
  7.4 0.0 copy-start.1
  7.4 0.0 copy-start.2
  7.4 0.0 copy-start.3
  7.4 3.5 %second_bias.1._.late_ref = f32[4,240,256]{2,1,0:T(8,128)S(1)} custom-call(s32[256,256]{1,0:T(8,128)S(1)} %get-tuple-element.30.index_ref, f32[4,1664]{1,0:T(4,128)S(1)} %get-tuple-element.31.table_ref), custom_call_target="tpu_custom_call" | custom-call | flops 1100000000 | bytes 3300000 | tf_op jit(solution)/shard_map/second_bias/pallas_call | solution.py:104
  10.9 0.0 copy-done
  10.9 0.0 copy-done.1
  11.0 0.0 copy-done.2
  11.0 0.0 copy-done.3
  11.0 0.2 turn_weights.1
  11.2 0.5 %collective-permute-done.3.got_ref = bf16[576,128]{1,0:T(8,128)(2,1)S(1)} collective-permute-done((bf16[576,128]{1,0:T(8,128)(2,1)S(1)}, bf16[576,128]{1,0:T(8,128)(2,1)S(1)}, u32[]{:S(2)}, u32[]{:S(2)}) %collective-permute-start.3) | collective-permute-done | bytes 147488 | tf_op jit(solution)/shard_map/ppermute | solution.py:169
  11.6 1.6 %collective-permute-start.4 = (bf16[576,128]{1,0:T(8,128)(2,1)S(1)}, bf16[576,128]{1,0:T(8,128)(2,1)S(1)}, u32[]{:S(2)}, u32[]{:S(2)}) collective-permute-start(bf16[576,128]{1,0:T(8,128)(2,1)S(1)} %across_pieces.1), channel_id=1, source_target_pairs={{0,4},{4,8},{8,12},{12,0},{1,5},{5,9},{9,13},{13,1},{2,6},{6,10},{... | collective-permute-start | bytes 442376 | tf_op jit(solution)/shard_map/ppermute | solution.py:169
  13.3 0.3 %collective-permute-done.1.near_ref.inside_ref = bf16[832,128]{1,0:T(8,128)(2,1)S(1)} collective-permute-done((bf16[832,128]{1,0:T(8,128)(2,1)S(1)}, bf16[832,128]{1,0:T(8,128)(2,1)S(1)}, u32[]{:S(2)}, u32[]{:S(2)}) %collective-permute-start.1) | collective-permute-done | bytes 213024 | tf_op jit(solution)/shard_map/ppermute | solution.py:169
  13.6 4.5 %inside_windows.1 = (bf16[2,3,2,64,128]{4,3,2,1,0:T(8,128)(2,1)S(1)}, bf16[2,3,2,64,128]{4,3,2,1,0:T(8,128)(2,1)S(1)}) custom-call(bf16[832,128]{1,0:T(8,128)(2,1)S(1)} %collective-permute-done.1.near_ref.inside_ref, bf16[6,128,128]{2,1,0:T(8,128)(2,1)S(1)} %get-tuple-element.28.own_ref, f32[4,16,256]{2,1,0:T(8,128)S(1)} %get-tuple-element.29.early_ref, ...), custom_call_target="tpu_custom_call" | custom-call | flops 16499999744 | bytes 49500000 | tf_op jit(solution)/shard_map/inside_windows/pallas_call | solution.py:499
  18.1 2.0 %collective-permute-start.2 = (bf16[2,3,2,64,128]{4,3,2,1,0:T(8,128)(2,1)S(1)}, bf16[2,3,2,64,128]{4,3,2,1,0:T(8,128)(2,1)S(1)}, u32[]{:S(2)}, u32[]{:S(2)}) collective-permute-start(bf16[2,3,2,64,128]{4,3,2,1,0:T(8,128)(2,1)S(1)} %get-tuple-element.41), channel_id=1, source_target_pairs={{0,12},{4,0},{8,4},{12,8},{1,13},{5,1},{9,5},{13,9},{2,14},{6,2},{... | collective-permute-start | bytes 589832 | tf_op jit(solution)/shard_map/ppermute | solution.py:169
  20.0 0.0 collective-permute-done.4.near_ref
  20.0 2.8 %across_windows.1 = (bf16[2,2,64,128]{3,2,1,0:T(8,128)(2,1)S(1)}, bf16[2,2,64,128]{3,2,1,0:T(8,128)(2,1)S(1)}) custom-call(bf16[832,128]{1,0:T(8,128)(2,1)S(1)} %collective-permute-done.1.near_ref.inside_ref, bf16[576,128]{1,0:T(8,128)(2,1)S(1)} %collective-permute-done.4.near_ref, bf16[512,128]{1,0:T(8,128)(2,1)S(1)} %get-tuple-element.42.own_ref, ...), custom_call_target="tpu_custom_call" | custom-call | flops 2529999872 | bytes 7589999 | tf_op jit(solution)/shard_map/across_windows/pallas_call | solution.py:499
  22.9 0.6 %collective-permute-start.5 = (bf16[2,2,64,128]{3,2,1,0:T(8,128)(2,1)S(1)}, bf16[2,2,64,128]{3,2,1,0:T(8,128)(2,1)S(1)}, u32[]{:S(2)}, u32[]{:S(2)}) collective-permute-start(bf16[2,2,64,128]{3,2,1,0:T(8,128)(2,1)S(1)} %get-tuple-element.44), channel_id=1, source_target_pairs={{0,12},{4,0},{8,4},{12,8},{1,13},{5,1},{9,5},{13,9},{2,14},{6,2},{... | collective-permute-start | bytes 196616 | tf_op jit(solution)/shard_map/ppermute | solution.py:169
  23.5 0.1 collective-permute-start.7
  23.6 3.6 %collective-permute-done.5.across_ref = bf16[2,2,64,128]{3,2,1,0:T(8,128)(2,1)S(1)} collective-permute-done((bf16[2,2,64,128]{3,2,1,0:T(8,128)(2,1)S(1)}, bf16[2,2,64,128]{3,2,1,0:T(8,128)(2,1)S(1)}, u32[]{:S(2)}, u32[]{:S(2)}) %collective-permute-start.5) | collective-permute-done | bytes 65568 | tf_op jit(solution)/shard_map/ppermute | solution.py:169
  27.2 0.0 collective-permute-done.2.inside_ref
  27.2 0.1 collective-permute-start.6
  27.3 0.0 collective-permute-done.7.low_ref
  27.3 0.8 %own_pieces.1.rest_0_ = bf16[8,256,128]{2,1,0:T(8,128)(2,1)} custom-call(bf16[4,64,128]{2,1,0:T(8,128)(2,1)S(1)} %collective-permute-done.7.low_ref, bf16[2,3,2,64,128]{4,3,2,1,0:T(8,128)(2,1)S(1)} %get-tuple-element.45.inside_ref, bf16[2,2,64,128]{3,2,1,0:T(8,128)(2,1)S(1)} %get-tuple-element.46.across_ref), custom_call_target="tpu_custom_call" | custom-call | flops 770000000 | bytes 2310000 | tf_op jit(solution)/shard_map/own_pieces/pallas_call | solution.py:484
  28.2 0.4 %collective-permute-done.6.low_ref = bf16[4,64,128]{2,1,0:T(8,128)(2,1)S(1)} collective-permute-done((bf16[4,64,128]{2,1,0:T(8,128)(2,1)S(1)}, bf16[4,64,128]{2,1,0:T(8,128)(2,1)S(1)}, u32[]{:S(2)}, u32[]{:S(2)}) %collective-permute-start.6) | collective-permute-done | bytes 65568 | tf_op jit(solution)/shard_map/ppermute | solution.py:169
  28.5 0.8 %last_pieces.1 = bf16[8,256,128]{2,1,0:T(8,128)(2,1)} custom-call(bf16[4,64,128]{2,1,0:T(8,128)(2,1)S(1)} %collective-permute-done.6.low_ref, bf16[2,3,2,64,128]{4,3,2,1,0:T(8,128)(2,1)S(1)} %collective-permute-done.2.inside_ref, bf16[2,2,64,128]{3,2,1,0:T(8,128)(2,1)S(1)} %collective-permute-done.5.across_ref, ...), custom_call_target="tpu_custom_call", output_to_operand_aliasing={{}: (3, {})} | custom-call | flops 770000000 | bytes 2310000 | tf_op jit(solution)/shard_map/last_pieces/pallas_call | solution.py:484
  (3 shorter events, 0.1 us)
Async XLA Ops:
  0.0 1.0 %copy-start.4 = (bf16[8,32,8,128]{3,2,1,0:T(8,128)(2,1)S(1)}, bf16[8,32,8,128]{3,2,1,0:T(8,128)(2,1)}, u32[]{:S(2)}) copy-start(bf16[8,32,8,128]{3,2,1,0:T(8,128)(2,1)} %param.10) | copy-start | bytes 1572868
  1.0 0.9 %copy-start.5 = (s32[256,256]{1,0:T(8,128)S(1)}, s32[256,256]{1,0:T(8,128)}, u32[]{:S(2)}) copy-start(s32[256,256]{1,0:T(8,128)} %given_index_ref.1) | copy-start | bytes 786436
  1.0 1.0 %copy-start.6 = (s32[8,32,8]{1,2,0:T(8,128)S(1)}, s32[8,32,8]{1,2,0:T(8,128)}, u32[]{:S(2)}) copy-start(s32[8,32,8]{1,2,0:T(8,128)} %param.11) | copy-start | bytes 24580
  1.0 1.0 %copy-start.7 = (f32[1575,4]{0,1:T(4,128)S(1)}, f32[1575,4]{0,1:T(4,128)}, u32[]{:S(2)}) copy-start(f32[1575,4]{0,1:T(4,128)} %param.13) | copy-start | bytes 75604
  1.1 1.6 %collective-permute-start = (bf16[8,64,128]{2,1,0:T(8,128)(2,1)S(1)}, bf16[8,64,128]{2,1,0:T(8,128)(2,1)S(1)}, u32[]{:S(2)}, u32[]{:S(2)}) collective-permute-start(bf16[8,64,128]{2,1,0:T(8,128)(2,1)S(1)} %low_pieces.1), channel_id=1, source_target_pairs={{0,1},{1,0},{2,3},{3,2},{4,5},{5,4},{6,7},{7,6},{8,9},{9,8},{10,11... | collective-permute-start | bytes 393224 | tf_op jit(solution)/shard_map/ppermute | solution.py:169
  1.7 0.7 %copy-start.8 = (f32[128]{0:T(128)S(1)}, f32[128]{0:T(128)}, u32[]{:S(2)}) copy-start(f32[128]{0:T(128)} %param.14) | copy-start | bytes 1540
  1.7 0.7 %copy-start.9 = (f32[128]{0:T(128)S(1)}, f32[128]{0:T(128)}, u32[]{:S(2)}) copy-start(f32[128]{0:T(128)} %param.17) | copy-start | bytes 1540
  3.0 10.6 %collective-permute-start.1 = (bf16[832,128]{1,0:T(8,128)(2,1)S(1)}, bf16[832,128]{1,0:T(8,128)(2,1)S(1)}, u32[]{:S(2)}, u32[]{:S(2)}) collective-permute-start(bf16[832,128]{1,0:T(8,128)(2,1)S(1)} %get-tuple-element.27), channel_id=1, source_target_pairs={{0,4},{4,8},{8,12},{12,0},{1,5},{5,9},{9,13},{13,1},{2,6},{6,10},{... | collective-permute-start | bytes 638984 | tf_op jit(solution)/shard_map/ppermute | solution.py:169
  5.9 5.7 %collective-permute-start.3 = (bf16[576,128]{1,0:T(8,128)(2,1)S(1)}, bf16[576,128]{1,0:T(8,128)(2,1)S(1)}, u32[]{:S(2)}, u32[]{:S(2)}) collective-permute-start(bf16[576,128]{1,0:T(8,128)(2,1)S(1)} %get-tuple-element.43), channel_id=1, source_target_pairs={{0,2},{2,0},{1,3},{3,1},{4,6},{6,4},{5,7},{7,5},{8,10},{10,8},{9,1... | collective-permute-start | bytes 442376 | tf_op jit(solution)/shard_map/ppermute | solution.py:169
  7.4 3.6 %copy-start = (bf16[128,512]{1,0:T(8,128)(2,1)S(1)}, bf16[128,512]{1,0:T(8,128)(2,1)}, u32[]{:S(2)}) copy-start(bf16[128,512]{1,0:T(8,128)(2,1)} %w_up_ref.1) | copy-start | bytes 393220
  7.4 3.6 %copy-start.1 = (bf16[512,128]{1,0:T(8,128)(2,1)S(1)}, bf16[512,128]{1,0:T(8,128)(2,1)}, u32[]{:S(2)}) copy-start(bf16[512,128]{1,0:T(8,128)(2,1)} %w_down_ref.1) | copy-start | bytes 393220
  7.4 3.6 %copy-start.2 = (bf16[128,384]{1,0:T(8,128)(2,1)S(1)}, bf16[128,384]{1,0:T(8,128)(2,1)}, u32[]{:S(2)}) copy-start(bf16[128,384]{1,0:T(8,128)(2,1)} %w_qkv_ref.1) | copy-start | bytes 294916
  7.4 3.6 %copy-start.3 = (bf16[128,128]{1,0:T(8,128)(2,1)S(1)}, bf16[128,128]{1,0:T(8,128)(2,1)}, u32[]{:S(2)}) copy-start(bf16[128,128]{1,0:T(8,128)(2,1)} %w_proj_ref.1) | copy-start | bytes 98308
  11.6 8.4 %collective-permute-start.4 = (bf16[576,128]{1,0:T(8,128)(2,1)S(1)}, bf16[576,128]{1,0:T(8,128)(2,1)S(1)}, u32[]{:S(2)}, u32[]{:S(2)}) collective-permute-start(bf16[576,128]{1,0:T(8,128)(2,1)S(1)} %across_pieces.1), channel_id=1, source_target_pairs={{0,4},{4,8},{8,12},{12,0},{1,5},{5,9},{9,13},{13,1},{2,6},{6,10},{... | collective-permute-start | bytes 442376 | tf_op jit(solution)/shard_map/ppermute | solution.py:169
  18.1 9.1 %collective-permute-start.2 = (bf16[2,3,2,64,128]{4,3,2,1,0:T(8,128)(2,1)S(1)}, bf16[2,3,2,64,128]{4,3,2,1,0:T(8,128)(2,1)S(1)}, u32[]{:S(2)}, u32[]{:S(2)}) collective-permute-start(bf16[2,3,2,64,128]{4,3,2,1,0:T(8,128)(2,1)S(1)} %get-tuple-element.41), channel_id=1, source_target_pairs={{0,12},{4,0},{8,4},{12,8},{1,13},{5,1},{9,5},{13,9},{2,14},{6,2},{... | collective-permute-start | bytes 589832 | tf_op jit(solution)/shard_map/ppermute | solution.py:169
  22.9 4.3 %collective-permute-start.5 = (bf16[2,2,64,128]{3,2,1,0:T(8,128)(2,1)S(1)}, bf16[2,2,64,128]{3,2,1,0:T(8,128)(2,1)S(1)}, u32[]{:S(2)}, u32[]{:S(2)}) collective-permute-start(bf16[2,2,64,128]{3,2,1,0:T(8,128)(2,1)S(1)} %get-tuple-element.44), channel_id=1, source_target_pairs={{0,12},{4,0},{8,4},{12,8},{1,13},{5,1},{9,5},{13,9},{2,14},{6,2},{... | collective-permute-start | bytes 196616 | tf_op jit(solution)/shard_map/ppermute | solution.py:169
  23.5 3.8 %collective-permute-start.7 = (bf16[4,64,128]{2,1,0:T(8,128)(2,1)S(1)}, bf16[4,64,128]{2,1,0:T(8,128)(2,1)S(1)}, u32[]{:S(2)}, u32[]{:S(2)}) collective-permute-start(bf16[4,64,128]{2,1,0:T(8,128)(2,1)S(1)} %far_own.1), channel_id=1, source_target_pairs={{0,1},{1,0},{2,3},{3,2},{4,5},{5,4},{6,7},{7,6},{8,9},{9,8},{10,11... | collective-permute-start | bytes 196616 | tf_op jit(solution)/shard_map/ppermute | solution.py:169
  27.2 1.3 %collective-permute-start.6 = (bf16[4,64,128]{2,1,0:T(8,128)(2,1)S(1)}, bf16[4,64,128]{2,1,0:T(8,128)(2,1)S(1)}, u32[]{:S(2)}, u32[]{:S(2)}) collective-permute-start(bf16[4,64,128]{2,1,0:T(8,128)(2,1)S(1)} %far_back.1), channel_id=1, source_target_pairs={{0,1},{1,0},{2,3},{3,2},{4,5},{5,4},{6,7},{7,6},{8,9},{9,8},{10,11... | collective-permute-start | bytes 196616 | tf_op jit(solution)/shard_map/ppermute | solution.py:169
